TPU v7x, 32 devices: a whole 2x2x4 slice. The times are simulated.
32 devices in a mesh: dp: 4 (over x, core), expert: 8 (over z, y).
Axes of the slice: x: 2, y: 2, z: 4, core: 2. Of those that a mesh axis runs over, the one named last changes fastest.
Arguments:
- events: bfloat16 [64, 1024], P(('dp', 'expert')), may hold values from -6 to 6
- labels: int32 [64, 4], P(('dp', 'expert')), may hold values 0 or 1
- w_in: bfloat16 [8, 1024, 4096], P('expert', None, 'dp'), may hold values from -0.1875 to 0.1875
- w_out: bfloat16 [8, 4096, 1024], P('expert', 'dp'), may hold values from -0.09375 to 0.09375
- gate_weight: bfloat16 [4, 1024, 8], replicated, may hold values from -4 to 4
- tower_in: bfloat16 [4, 1024, 256], replicated, may hold values from -0.1875 to 0.1875
- tower_bias: float32 [4, 256], replicated, may hold values from -3 to 3
- tower_out: float32 [4, 256], replicated, may hold values from -0.75 to 0.75
- tower_out_bias: float32 [4], replicated, may hold values from -3 to 3
Outputs:
- grad_in: bfloat16 [8, 1024, 4096], P('expert', None, 'dp')
- grad_out: bfloat16 [8, 4096, 1024], P('expert', 'dp')
- grad_gate: float32 [4, 1024, 8], P(None, None, 'expert')
All inputs are finite; a program needn't handle non-finite values. No bound on the sum of `labels` on one device may be relied on, other than what follows from the above.
Results may differ from a plain program's by a relative error of at most 0.035.
Values may be sent and summed in bfloat16 or wider, within the bound.
No kernel may reach another device: no remote copies, remote signals or barrier semaphores. Data moves between devices by JAX's collectives and lax.ppermute only.
A program may use at most 64 MiB of HBM per device.

v0:
```python
import jax
import jax.numpy as jnp
from jax import lax
from jax.sharding import PartitionSpec as P


def gelu_tanh(value):
    return jax.nn.gelu(value, approximate=True)


def tower_apply(mixed, tower_in, tower_bias, tower_out, tower_out_bias):
    tower_pre = (
        jnp.einsum(
            "trd,tdk->trk", mixed, tower_in.astype(jnp.float32), precision=lax.Precision.HIGHEST
        )
        + tower_bias[:, None, :]
    )
    return jnp.sum(gelu_tanh(tower_pre) * tower_out[:, None, :], -1) + tower_out_bias[:, None]


def per_device(
    events, labels, w_in, w_out, gate_weight, tower_in, tower_bias, tower_out, tower_out_bias
):
    experts_here = lax.axis_size("expert")
    own_rows = events.shape[0]
    every = lax.all_gather(events, ("dp", "expert"), axis=0, tiled=True)
    span = own_rows * experts_here
    dp_index = lax.axis_index("dp")
    expert_index = lax.axis_index("expert")
    pre = jnp.dot(every, w_in[0], preferred_element_type=jnp.float32)
    hidden = gelu_tanh(pre).astype(jnp.bfloat16)
    expert_out = lax.psum_scatter(
        jnp.dot(hidden, w_out[0], preferred_element_type=jnp.float32).astype(jnp.bfloat16),
        "dp",
        scatter_dimension=0,
        tiled=True,
    )
    targets = labels.T.astype(jnp.float32)

    def tower_of(value):
        return tower_apply(value, tower_in, tower_bias, tower_out, tower_out_bias)

    block_rows = lax.dynamic_slice_in_dim(every, dp_index * span, span, 0)
    gate_logits = jnp.einsum(
        "rd,tde->tre", block_rows, gate_weight, preferred_element_type=jnp.float32
    )
    probs = jax.nn.softmax(gate_logits, axis=-1)
    own_prob = lax.dynamic_slice_in_dim(probs, expert_index, 1, 2)[:, :, 0]
    outs_wide = expert_out.astype(jnp.float32)
    terms = own_prob[:, :, None] * outs_wide[None]
    mixed = lax.psum_scatter(terms.astype(jnp.bfloat16), "expert", scatter_dimension=1, tiled=True)
    logit, tower_back = jax.vjp(tower_of, mixed.astype(jnp.float32))
    dmixed = tower_back(jax.nn.sigmoid(logit) - targets)[0].astype(jnp.bfloat16)
    block_grads = lax.all_gather(dmixed, "expert", axis=1, tiled=True)
    dprob = jnp.einsum("trd,rd->tr", block_grads, expert_out, preferred_element_type=jnp.float32)
    weighted = lax.psum(own_prob * dprob, "expert")
    dgate = own_prob * (dprob - weighted)
    grads_wide = block_grads.astype(jnp.float32)
    dexpert = jnp.einsum(
        "tr,trd->rd", own_prob, grads_wide, precision=lax.Precision.HIGHEST
    ).astype(jnp.bfloat16)
    gate_part = jnp.einsum(
        "rd,tr->td", block_rows.astype(jnp.float32), dgate, precision=lax.Precision.HIGHEST
    )
    grad_gate = lax.psum(gate_part, "dp")[:, :, None]
    all_grads = lax.all_gather(dexpert, "dp", axis=0, tiled=True)
    dhidden = lax.dot_general(
        all_grads, w_out[0], (((1,), (1,)), ((), ())), preferred_element_type=jnp.float32
    )
    gelu_back = jax.vjp(gelu_tanh, pre)[1]
    dpre = gelu_back(dhidden)[0].astype(jnp.bfloat16)
    grad_second = lax.dot_general(
        hidden, all_grads, (((0,), (0,)), ((), ())), preferred_element_type=jnp.float32
    ).astype(jnp.bfloat16)
    grad_first = lax.dot_general(
        every, dpre, (((0,), (0,)), ((), ())), preferred_element_type=jnp.float32
    ).astype(jnp.bfloat16)
    return (grad_first[None], grad_second[None], grad_gate)


def solution(mesh):
    placed = (
        P(("dp", "expert"), None),
        P(("dp", "expert"), None),
        P("expert", None, "dp"),
        P("expert", "dp", None),
        P(),
        P(),
        P(),
        P(),
        P(),
    )
    return jax.shard_map(
        per_device,
        mesh=mesh,
        in_specs=placed,
        out_specs=(P("expert", None, "dp"), P("expert", "dp", None), P(None, None, "expert")),
        check_vma=False,
    )
```

profile of v0, /device:TPU:0, one launch (start us, length us, event | category | flops | bytes accessed | tf_op | source)
XLA Modules:
  0.0 259.1 jit_solution(11331316045219559111)
XLA Ops:
  7.2 0.0 reduce-scatter.2.cloned.1.call-start
  7.2 70.8 %all-gather = bf16[32,2,1024]{2,1,0:T(2,128)(2,1)S(1)} all-gather(bf16[1,2,1024]{2,1,0:T(2,128)(2,1)} %bitcast.66), channel_id=1, replica_groups=mesh['dp'=4,'expert'=8] {'dp','expert'}, dimensions={0}, use_global_device_ids=true | all-gather | bytes 135168 | tf_op jit(solution)/shard_map/all_gather | solution.py:26
  78.0 0.1 reshape.13
  78.1 2.1 fusion.4
  80.2 1.1 fusion.6
  81.4 0.0 reduce-scatter.2.cloned.1.call-update
  81.4 0.0 all-reduce.3.cloned.1.call-start
  81.5 0.2 fusion.79
  81.7 0.1 copy.15
  81.8 15.7 %reduce-scatter.2.cloned.1.call-done = bf16[16,1024]{1,0:T(8,128)(2,1)} async-done(((bf16[64,1024]{1,0:T(8,128)(2,1)}), bf16[16,1024]{1,0:T(8,128)(2,1)}) %reduce-scatter.2.cloned.1.call-update) | async-done | bytes 32784 | tf_op jit(solution)/shard_map/reduce_scatter | solution.py:32
  97.5 0.8 convert_element_type.42
  98.2 0.8 multiply_convert_fusion
  99.0 0.1 copy.17
  99.1 0.1 copy.21
  99.2 0.6 dynamic-slice
  100.4 71.0 %all-reduce.3.cloned.1.call-done = bf16[4,16,1024]{2,0,1:T(4,128)(2,1)} async-done(((bf16[4,16,1024]{2,0,1:T(4,128)(2,1)}), bf16[4,16,1024]{2,0,1:T(4,128)(2,1)}) %all-reduce.3.cloned.1.call-update) | async-done | bytes 131088
  171.4 0.9 constant_dynamic-slice_fusion
  172.3 2.1 multiply_reduce_fusion
  174.4 0.1 divide_subtract_fusion
  174.4 1.8 convolution_convert_fusion
  176.2 30.6 %all_gather.10 = bf16[4,16,1024]{2,0,1:T(4,128)(2,1)S(1)} all-gather(bf16[4,2,1024]{2,0,1:T(4,128)(2,1)S(1)} %copy.18), channel_id=1, replica_groups=mesh['dp'=4,'expert'=8] {'expert'}, dimensions={1}, use_global_device_ids=true | all-gather | bytes 147456 | tf_op jit(solution)/shard_map/all_gather | solution.py:54
  206.8 0.4 fusion.80
  207.2 5.4 %all_gather.11 = bf16[64,1024]{1,0:T(8,128)(2,1)S(1)} all-gather(bf16[16,1024]{1,0:T(8,128)(2,1)S(1)} %bitcast.60), channel_id=1, replica_groups=mesh['dp'=4,'expert'=8] {'dp'}, dimensions={0}, use_global_device_ids=true | all-gather | bytes 163840 | tf_op jit(solution)/shard_map/all_gather | solution.py:66
  212.6 2.8 %convert_bitcast_fusion.1 = bf16[1,1024,1024]{1,2,0:T(8,128)(2,1)} fusion(bf16[64,1024]{1,0:T(8,128)(2,1)S(1)} %reshape.13, f32[64,1024]{1,0:T(8,128)S(1)} %fusion.4, bf16[64,1024]{1,0:T(8,128)(2,1)S(1)} %all_gather.11, bf16[1,1024,1024]{2,1,0:T(8,128)(2,1)S(1)} %copy-done), kind=kOutput, calls=%fused_computation.7 | convolution fusion | flops 270794752 | bytes 4718592 | tf_op jit(solution)/shard_map/dot_general | solution.py:75
  215.4 2.1 convert_bitcast_fusion
  217.4 0.2 fusion.30
  217.7 0.1 copy.24
  217.8 19.7 %psum.14 = f32[4,16]{1,0:T(4,128)S(1)} all-reduce(f32[4,16]{1,0:T(4,128)S(1)} %bitcast_multiply_fusion), channel_id=1, replica_groups=mesh['dp'=4,'expert'=8] {'expert'}, use_global_device_ids=true, to_apply=%region_5.0 | all-reduce | flops 64 | bytes 512 | tf_op jit(solution)/shard_map/psum | solution.py:56
  237.4 0.1 convolution_bitcast_fusion
  237.6 10.1 %psum.15 = f32[4,1024,1]{1,0,2:T(4,128)S(1)} all-reduce(f32[4,1024,1]{1,0,2:T(4,128)S(1)} %convolution_bitcast_fusion), channel_id=1, replica_groups=mesh['dp'=4,'expert'=8] {'dp'}, use_global_device_ids=true, to_apply=%region_6.0 | all-reduce | flops 4096 | bytes 32768 | tf_op jit(solution)/shard_map/psum | solution.py:65
  247.7 0.6 copy.20
  248.3 3.9 %copy.19 = bf16[1,1024,1024]{2,1,0:T(8,128)(2,1)} copy(bf16[1,1024,1024]{1,2,0:T(8,128)(2,1)} %convert_bitcast_fusion.1) | data formatting | bytes 4194304
  (24 shorter events, 0.2 us)
Async XLA Ops:
  7.2 73.0 %copy-start = (bf16[1,1024,1024]{2,1,0:T(8,128)(2,1)S(1)}, bf16[1,1024,1024]{2,1,0:T(8,128)(2,1)}, u32[]{:S(2)}) copy-start(bf16[1,1024,1024]{2,1,0:T(8,128)(2,1)} %param.12) | copy-start | bytes 6291460
  7.2 90.3 %reduce-scatter.2.cloned.1.call-start = ((), (), s32[]{:S(2)}) async-start(), calls=%async_computation.1 | async-start | bytes 163840 | tf_op jit(solution)/shard_map/reduce_scatter | solution.py:32
  78.1 3.4 %copy-start.2 = (bf16[4,1024,8]{1,2,0:T(8,128)(2,1)S(1)}, bf16[4,1024,8]{1,2,0:T(8,128)(2,1)}, u32[]{:S(2)}) copy-start(bf16[4,1024,8]{1,2,0:T(8,128)(2,1)} %param.13) | copy-start | bytes 196612
  80.2 18.8 %copy-start.6 = (s32[2,4]{1,0:T(2,128)S(1)}, s32[2,4]{1,0:T(2,128)}, u32[]{:S(2)}) copy-start(s32[2,4]{1,0:T(2,128)} %param.10) | copy-start | bytes 100
  80.2 19.0 %copy-start.8 = (u32[32]{0:T(128)S(1)}, u32[32]{0:T(128)}, u32[]{:S(2)}) copy-start(u32[32]{0:T(128)} %constant.46) | copy-start | bytes 388
  80.2 92.1 %copy-start.4 = (f32[4,256]{1,0:T(4,128)S(1)}, f32[4,256]{1,0:T(4,128)}, u32[]{:S(2)}) copy-start(f32[4,256]{1,0:T(4,128)} %param.16) | copy-start | bytes 12292
  80.2 92.0 %copy-start.5 = (f32[4,256]{1,0:T(4,128)S(1)}, f32[4,256]{1,0:T(4,128)}, u32[]{:S(2)}) copy-start(f32[4,256]{1,0:T(4,128)} %param.15) | copy-start | bytes 12292
  81.4 93.0 %copy-start.7 = (f32[4]{0:T(128)S(1)}, f32[4]{0:T(128)}, u32[]{:S(2)}) copy-start(f32[4]{0:T(128)} %param.17) | copy-start | bytes 52
  81.4 90.0 %all-reduce.3.cloned.1.call-start = ((), (), s32[]{:S(2)}) async-start(), calls=%async_computation.2 | async-start | bytes 262144
  171.4 3.0 %copy-start.1 = (bf16[4,1024,256]{2,1,0:T(8,128)(2,1)S(1)}, bf16[4,1024,256]{2,1,0:T(8,128)(2,1)}, u32[]{:S(2)}) copy-start(bf16[4,1024,256]{2,1,0:T(8,128)(2,1)} %param.14) | copy-start | bytes 6291460
  215.4 2.1 copy-start.3
Sparse Core Ops, SparseCore 0:
  81.5 15.8 reduce-scatter.1
  101.7 69.6 all-reduce.2
where the time goes:
time: 259 us
  blocking collectives  137 us (53%)
  waiting for transfers between devices  86.7 us (33%)
  between operations  14.8 us (6%)
  matrix products  12.8 us (5%)
  local copies, waits for them, and re-layouts  6.49 us (3%)
    unnamed x3, waiting for transfers between devices  71 us
    all_gather x1, blocking collectives, per_device(): every = lax.all_gather(events, ('dp', 'expert'), axis=0, tiled=True)  70.8 us
    all_gather x1, blocking collectives, per_device(): block_grads = lax.all_gather(dmixed, 'expert', axis=1, tiled=True)  30.6 us
    psum x1, blocking collectives, per_device(): weighted = lax.psum(own_prob * dprob, 'expert')  19.7 us
    reduce_scatter x1, waiting for transfers between devices, per_device(): lax.psum_scatter(jnp.dot(hidden, w_out[0], preferred_element_type=jnp.flo...  15.7 us
    psum x1, blocking collectives, per_device(): grad_gate = lax.psum(gate_part, 'dp')[:, :, None]  10.1 us
    unnamed x24, local copies, waits for them, and re-layouts  6.21 us
    all_gather x1, blocking collectives, per_device(): all_grads = lax.all_gather(dexpert, 'dp', axis=0, tiled=True)  5.43 us
  transfers between devices with their start and end apart: 2, of which 2 were waited for; matrix products, arithmetic and copies ran while one was open for 0% of the time, Pallas kernels for 0%

commit v1 on v0

v1 whole, which is shorter than its diff:
```python
import jax
import jax.numpy as jnp
from jax import lax
from jax.sharding import PartitionSpec as P

BOTH = ("dp", "expert")


def gelu_tanh(value):
    return jax.nn.gelu(value, approximate=True)


def pieces_of(value):
    high = value.astype(jnp.bfloat16)
    rest = value - high.astype(jnp.float32)
    middle = rest.astype(jnp.bfloat16)
    low = (rest - middle.astype(jnp.float32)).astype(jnp.bfloat16)
    return high, middle, low


def per_device(
    events, labels, w_in, w_out, gate_weight, tower_in, tower_bias, tower_out, tower_out_bias
):
    dp = lax.axis_size("dp")
    experts = lax.axis_size("expert")
    devices = dp * experts
    own, width = events.shape
    tasks = tower_in.shape[0]
    rows = devices * own

    gate_logits = jnp.einsum(
        "rd,tde->tre", events, gate_weight, preferred_element_type=jnp.float32
    )
    probs = jax.nn.softmax(gate_logits, axis=-1)

    every = lax.all_to_all(
        jnp.broadcast_to(events[None], (devices, own, width)), BOTH, 0, 0, tiled=True
    ).reshape(rows, width)
    pre = jnp.dot(every, w_in[0], preferred_element_type=jnp.float32)
    hidden = gelu_tanh(pre).astype(jnp.bfloat16)
    part = jnp.dot(hidden, w_out[0], preferred_element_type=jnp.float32).astype(jnp.bfloat16)

    parts = lax.all_to_all(part.reshape(devices, own, width), BOTH, 0, 0, tiled=True)
    parts = parts.reshape(dp, experts, own, width).astype(jnp.float32)
    outs = jnp.sum(parts, 0).astype(jnp.bfloat16)
    outs_wide = outs.astype(jnp.float32)
    mixed = jnp.sum(
        jnp.transpose(probs, (0, 2, 1))[..., None] * outs_wide[None], 1
    ).astype(jnp.bfloat16)
    tower_pre = (
        jnp.einsum("trd,tdk->trk", mixed, tower_in, preferred_element_type=jnp.float32)
        + tower_bias[:, None, :]
    )
    active, gelu_back = jax.vjp(gelu_tanh, tower_pre)
    logit = jnp.sum(active * tower_out[:, None, :], -1) + tower_out_bias[:, None]
    dlogit = jax.nn.sigmoid(logit) - labels.T.astype(jnp.float32)
    dtower = gelu_back(dlogit[..., None] * tower_out[:, None, :])[0]
    stacked = jnp.concatenate(pieces_of(dtower), 1)
    dmixed = jnp.einsum("trk,tdk->trd", stacked, tower_in, preferred_element_type=jnp.float32)
    dmixed = jnp.sum(dmixed.reshape(tasks, 3, own, width), 1).astype(jnp.bfloat16)
    dmixed_wide = dmixed.astype(jnp.float32)
    dprob = jnp.sum(dmixed_wide[:, None] * outs_wide[None], -1)
    probs_ter = jnp.transpose(probs, (0, 2, 1))
    dgate = probs_ter * (dprob - jnp.sum(probs_ter * dprob, 1, keepdims=True))
    dexpert = jnp.sum(probs_ter[..., None] * dmixed_wide[:, None], 0).astype(jnp.bfloat16)

    packed = jnp.transpose(jnp.concatenate(pieces_of(dgate), 0), (1, 2, 0))
    packed = jnp.pad(packed, ((0, 0), (0, 0), (0, 128 - 3 * tasks)))
    message = jnp.concatenate([dexpert, packed], -1)
    message = jnp.broadcast_to(message[None], (dp, experts, own, width + 128))
    message = message.reshape(devices, own, width + 128)
    arrived = lax.all_to_all(message, BOTH, 0, 0, tiled=True).reshape(rows, width + 128)
    all_grads = arrived[:, :width]
    gate_rows = arrived[:, width : width + 3 * tasks]

    dhidden = lax.dot_general(
        all_grads, w_out[0], (((1,), (1,)), ((), ())), preferred_element_type=jnp.float32
    )
    dpre = jax.vjp(gelu_tanh, pre)[1](dhidden)[0].astype(jnp.bfloat16)
    grad_second = lax.dot_general(
        hidden, all_grads, (((0,), (0,)), ((), ())), preferred_element_type=jnp.float32
    ).astype(jnp.bfloat16)
    grad_first = lax.dot_general(
        every, dpre, (((0,), (0,)), ((), ())), preferred_element_type=jnp.float32
    ).astype(jnp.bfloat16)
    grad_gate = lax.dot_general(
        gate_rows, every, (((0,), (0,)), ((), ())), preferred_element_type=jnp.float32
    )
    grad_gate = jnp.sum(grad_gate.reshape(3, tasks, width), 0)
    return (grad_first[None], grad_second[None], grad_gate[:, :, None])


def solution(mesh):
    placed = (
        P(BOTH, None),
        P(BOTH, None),
        P("expert", None, "dp"),
        P("expert", "dp", None),
        P(),
        P(),
        P(),
        P(),
        P(),
    )
    return jax.shard_map(
        per_device,
        mesh=mesh,
        in_specs=placed,
        out_specs=(P("expert", None, "dp"), P("expert", "dp", None), P(None, None, "expert")),
        check_vma=False,
    )
```

time: 259 us -> 57.9 us (0.22)
  blocking collectives: 137 us -> 0 us
  waiting for transfers between devices: 86.7 us -> 21.7 us
  between operations: 14.8 us -> 0.85 us
  starting transfers between devices: 0.08 us -> 12.4 us
    all_gather x3 -> x0, blocking collectives: 107 us -> none  [the longest x1 70.8 us: per_device(): every = lax.all_gather(events, ('dp', 'expert'), axis=0, tiled=True)]
    unnamed x3 -> x0, waiting for transfers between devices: 71 us -> none
    psum x2 -> x0, blocking collectives: 29.8 us -> none  [the longest x1 19.7 us: per_device(): weighted = lax.psum(own_prob * dprob, 'expert')]
    all_to_all x0 -> x3, waiting for transfers between devices: none -> 21.7 us  [the longest x1 7.77 us: per_device(): lax.all_to_all(message, BOTH, 0, 0, tiled=True).reshape(rows, width + 128)]
    reduce_scatter x1 -> x0, waiting for transfers between devices: 15.7 us -> none  [per_device(): lax.psum_scatter(jnp.dot(hidden, w_out[0], preferred_element_type=jnp.flo...]
    all_to_all x0 -> x3, starting transfers between devices: none -> 12.4 us  [the longest x1 7.3 us: per_device(): lax.all_to_all(jnp.broadcast_to(events[None], (devices, own, width)), BOT...]
    broadcast_in_dim x0 -> x3, local copies, waits for them, and re-layouts: none -> 2.92 us  [the longest x1 1.56 us: per_device(): jnp.broadcast_to(events[None], (devices, own, width))]
    unnamed x24 -> x14, local copies, waits for them, and re-layouts: 6.21 us -> 4.26 us
  transfers between devices with their start and end apart: 2 -> 3, of which waited for: 2 -> 3; matrix products, arithmetic and copies ran while one was open for 0% -> 3% of each run, Pallas kernels for 0% -> 0%
where the time goes in v1:
time: 57.9 us; the launch traced here: 57.4 us
  waiting for transfers between devices  21.7 us (37%)
  matrix products  12.9 us (22%)
  starting transfers between devices  12.4 us (21%)
  local copies, waits for them, and re-layouts  8.36 us (14%)
  other arithmetic  1.11 us (2%)
  between operations  0.85 us (1%)
    all_to_all x1, waiting for transfers between devices, per_device(): lax.all_to_all(message, BOTH, 0, 0, tiled=True).reshape(rows, width + 128)  7.77 us
    all_to_all x1, waiting for transfers between devices, per_device(): lax.all_to_all(part.reshape(devices, own, width), BOTH, 0, 0, tiled=True)  7.39 us
    all_to_all x1, starting transfers between devices, per_device(): lax.all_to_all(jnp.broadcast_to(events[None], (devices, own, width)), BOT...  7.3 us
    all_to_all x1, waiting for transfers between devices, per_device(): lax.all_to_all(jnp.broadcast_to(events[None], (devices, own, width)), BOT...  6.57 us
    unnamed x14, local copies, waits for them, and re-layouts  4.26 us
    dot_general x1, matrix products, per_device(): lax.dot_general(every, dpre, (((0,), (0,)), ((), ())), preferred_element_...  2.77 us
    all_to_all x1, starting transfers between devices, per_device(): lax.all_to_all(message, BOTH, 0, 0, tiled=True).reshape(rows, width + 128)  2.58 us
    all_to_all x1, starting transfers between devices, per_device(): lax.all_to_all(part.reshape(devices, own, width), BOTH, 0, 0, tiled=True)  2.58 us
  transfers between devices with their start and end apart: 3, of which 3 were waited for; matrix products, arithmetic and copies ran while one was open for 3% of the time, Pallas kernels for 0%

profile of v1, /device:TPU:0, one launch (start us, length us, event | category | flops | bytes accessed | tf_op | source)
XLA Modules:
  0.0 57.4 jit_solution(15731458878378903834)
XLA Ops:
  0.6 1.6 %broadcast_in_dim.10 = bf16[32,2,1024]{2,1,0:T(2,128)(2,1)} broadcast(bf16[2,1024]{1,0:T(2,128)(2,1)} %param.9), dimensions={1,2} | broadcast | bytes 135168 | tf_op jit(solution)/shard_map/broadcast_in_dim | solution.py:37
  2.2 7.3 %all-to-all-start = ((bf16[32,2,1024]{2,1,0:T(2,128)(2,1)}), bf16[32,2,1024]{2,1,0:T(2,128)(2,1)S(1)}, u32[]{:S(2)}, u32[]{:S(2)}) async-start(bf16[32,2,1024]{2,1,0:T(2,128)(2,1)} %broadcast_in_dim.10), calls=%async_computation | async-start | bytes 262144 | tf_op jit(solution)/shard_map/all_to_all | solution.py:36
  9.5 1.2 %bitcast_reduce_fusion = (f32[4,2]{1,0:T(4,128)S(1)}, f32[4,8,2]{1,2,0:T(2,128)S(1)}) fusion(bf16[4,1024,8]{1,2,0:T(8,128)(2,1)} %param.13, bf16[2,1024]{1,0:T(2,128)(2,1)} %param.9), kind=kOutput, calls=%fused_computation.67 | convolution fusion | flops 131128 | bytes 69920 | tf_op jit(solution)/shard_map/rd,tde->tre/dot_general | solution.py:31
  10.7 6.6 %all-to-all-done = bf16[32,2,1024]{2,1,0:T(2,128)(2,1)S(1)} async-done(((bf16[32,2,1024]{2,1,0:T(2,128)(2,1)}), bf16[32,2,1024]{2,1,0:T(2,128)(2,1)S(1)}, u32[]{:S(2)}, u32[]{:S(2)}) %all-to-all-start) | async-done | bytes 131104 | tf_op jit(solution)/shard_map/all_to_all | solution.py:36
  17.3 2.1 %fusion.5 = f32[64,1024]{1,0:T(8,128)S(1)} fusion(bf16[64,1024]{1,0:T(8,128)(2,1)S(1)} %reshape.43, bf16[1,1024,1024]{2,1,0:T(8,128)(2,1)} %param.11), kind=kOutput, calls=%fused_computation.5 | convolution fusion | flops 134217728 | bytes 2490368 | tf_op jit(solution)/shard_map/dot_general | solution.py:39
  19.4 0.5 fusion.7
  19.9 0.7 %reshape.44 = bf16[32,2,1024]{2,1,0:T(2,128)(2,1)} reshape(bf16[64,1024]{1,0:T(8,128)(2,1)S(1)} %fusion.7) | data formatting | bytes 262144 | tf_op jit(solution)/shard_map/reshape | solution.py:43
  20.6 2.6 %all-to-all-start.1 = ((bf16[32,2,1024]{2,1,0:T(2,128)(2,1)}), bf16[32,2,1024]{2,1,0:T(2,128)(2,1)S(1)}, u32[]{:S(2)}, u32[]{:S(2)}) async-start(bf16[32,2,1024]{2,1,0:T(2,128)(2,1)} %reshape.44), calls=%async_computation.1 | async-start | bytes 262144 | tf_op jit(solution)/shard_map/all_to_all | solution.py:43
  23.2 0.2 fusion.52
  23.4 0.1 copy.47
  23.5 0.1 exponential_divide_fusion
  23.6 7.4 %all-to-all-done.1 = bf16[32,2,1024]{2,1,0:T(2,128)(2,1)S(1)} async-done(((bf16[32,2,1024]{2,1,0:T(2,128)(2,1)}), bf16[32,2,1024]{2,1,0:T(2,128)(2,1)S(1)}, u32[]{:S(2)}, u32[]{:S(2)}) %all-to-all-start.1) | async-done | bytes 131104 | tf_op jit(solution)/shard_map/all_to_all | solution.py:43
  31.0 0.1 reduce_sum.85
  31.1 0.2 multiply_reduce_fusion.2
  31.3 2.0 %fusion.66 = f32[4,2,256]{2,1,0:T(2,128)S(1)} fusion(bf16[4,2,1024]{2,1,0:T(2,128)(2,1)S(1)} %multiply_reduce_fusion.2, bf16[4,1024,256]{2,1,0:T(8,128)(2,1)} %param.14), kind=kOutput, calls=%fused_computation.87 | convolution fusion | flops 4194304 | bytes 2121728 | tf_op jit(solution)/shard_map/trd,tdk->trk/dot_general | solution.py:51
  33.2 0.1 multiply_reduce_fusion.3
  33.4 0.1 copy.56
  33.5 0.1 copy.48
  33.6 0.1 fusion.63
  33.8 2.2 %fusion.37 = f32[4,6,1024]{2,1,0:T(8,128)S(1)} fusion(bf16[4,1024,256]{2,1,0:T(8,128)(2,1)} %param.14, bf16[4,6,256]{2,0,1:T(4,128)(2,1)S(1)} %pad_maximum_fusion), kind=kOutput, calls=%fused_computation.41 | convolution fusion | flops 12582912 | bytes 2207744 | tf_op jit(solution)/shard_map/trk,tdk->trd/dot_general | solution.py:59
  36.0 0.1 copy.50
  36.1 0.1 multiply_reduce_fusion.1
  36.3 0.1 fusion.65
  36.4 0.1 copy.57
  36.5 0.7 %broadcast_in_dim.11 = bf16[4,8,2,1152]{3,2,1,0:T(2,128)(2,1)} broadcast(bf16[8,2,1152]{2,1,0:T(2,128)(2,1)S(1)} %copy.53), dimensions={1,2,3} | broadcast | bytes 184320 | tf_op jit(solution)/shard_map/broadcast_in_dim | solution.py:70
  37.3 2.6 %all-to-all-start.2 = ((bf16[32,2,1152]{2,1,0:T(2,128)(2,1)}), bf16[32,2,1152]{2,1,0:T(2,128)(2,1)S(1)}, u32[]{:S(2)}, u32[]{:S(2)}) async-start(bf16[32,2,1152]{2,1,0:T(2,128)(2,1)} %bitcast.8), calls=%async_computation.2 | async-start | bytes 294912 | tf_op jit(solution)/shard_map/all_to_all | solution.py:72
  39.9 7.8 %all-to-all-done.2 = bf16[32,2,1152]{2,1,0:T(2,128)(2,1)S(1)} async-done(((bf16[32,2,1152]{2,1,0:T(2,128)(2,1)}), bf16[32,2,1152]{2,1,0:T(2,128)(2,1)S(1)}, u32[]{:S(2)}, u32[]{:S(2)}) %all-to-all-start.2) | async-done | bytes 147488 | tf_op jit(solution)/shard_map/all_to_all | solution.py:72
  47.7 2.8 %convert_bitcast_fusion.1 = bf16[1,1024,1024]{1,2,0:T(8,128)(2,1)} fusion(bf16[64,1024]{1,0:T(8,128)(2,1)S(1)} %reshape.43, f32[64,1024]{1,0:T(8,128)S(1)} %fusion.5, bf16[1,1024,1024]{2,1,0:T(8,128)(2,1)S(1)} %copy-done, bf16[64,1152]{1,0:T(8,128)(2,1)S(1)} %reshape.48), kind=kOutput, calls=%fused_computation.8 | convolution fusion | flops 270794752 | bytes 4718592 | tf_op jit(solution)/shard_map/dot_general | solution.py:83
  50.5 2.1 %convert_bitcast_fusion = bf16[1,1024,1024]{2,1,0:T(8,128)(2,1)} fusion(bf16[64,1152]{1,0:T(8,128)(2,1)S(1)} %reshape.48, f32[64,1024]{1,0:T(8,128)S(1)} %fusion.5), kind=kOutput, calls=%fused_computation.7 | convolution fusion | flops 135856128 | bytes 2490368 | tf_op jit(solution)/shard_map/dot_general | solution.py:80
  52.7 0.2 convolution_reduce_fusion
  52.8 0.6 %broadcast_in_dim.14 = f32[4,1024,1]{1,2,0:T(1,128)} reshape(f32[4,1024]{1,0:T(4,128)S(1)} %convolution_reduce_fusion) | data formatting | bytes 32768 | tf_op jit(solution)/shard_map/broadcast_in_dim | solution.py:90
  53.5 3.9 %copy.55 = bf16[1,1024,1024]{2,1,0:T(8,128)(2,1)} copy(bf16[1,1024,1024]{1,2,0:T(8,128)(2,1)} %convert_bitcast_fusion.1) | data formatting | bytes 4194304
  (25 shorter events, 0.5 us)
Async XLA Ops:
  0.6 18.8 %copy-start = (bf16[1,1024,1024]{2,1,0:T(8,128)(2,1)S(1)}, bf16[1,1024,1024]{2,1,0:T(8,128)(2,1)}, u32[]{:S(2)}) copy-start(bf16[1,1024,1024]{2,1,0:T(8,128)(2,1)} %param.12) | copy-start | bytes 6291460
  2.2 15.0 %all-to-all-start = ((bf16[32,2,1024]{2,1,0:T(2,128)(2,1)}), bf16[32,2,1024]{2,1,0:T(2,128)(2,1)S(1)}, u32[]{:S(2)}, u32[]{:S(2)}) async-start(bf16[32,2,1024]{2,1,0:T(2,128)(2,1)} %broadcast_in_dim.10), calls=%async_computation | async-start | bytes 262144 | tf_op jit(solution)/shard_map/all_to_all | solution.py:36
  19.4 4.0 %copy-start.3 = (s32[2,4]{1,0:T(2,128)S(1)}, s32[2,4]{1,0:T(2,128)}, u32[]{:S(2)}) copy-start(s32[2,4]{1,0:T(2,128)} %param.10) | copy-start | bytes 100
  19.9 13.4 %copy-start.1 = (f32[4,256]{1,0:T(4,128)S(1)}, f32[4,256]{1,0:T(4,128)}, u32[]{:S(2)}) copy-start(f32[4,256]{1,0:T(4,128)} %param.15) | copy-start | bytes 12292
  19.9 13.3 %copy-start.2 = (f32[4,256]{1,0:T(4,128)S(1)}, f32[4,256]{1,0:T(4,128)}, u32[]{:S(2)}) copy-start(f32[4,256]{1,0:T(4,128)} %param.16) | copy-start | bytes 12292
  19.9 13.5 %copy-start.4 = (f32[4]{0:T(128)S(1)}, f32[4]{0:T(128)}, u32[]{:S(2)}) copy-start(f32[4]{0:T(128)} %param.17) | copy-start | bytes 52
  20.6 10.3 %all-to-all-start.1 = ((bf16[32,2,1024]{2,1,0:T(2,128)(2,1)}), bf16[32,2,1024]{2,1,0:T(2,128)(2,1)S(1)}, u32[]{:S(2)}, u32[]{:S(2)}) async-start(bf16[32,2,1024]{2,1,0:T(2,128)(2,1)} %reshape.44), calls=%async_computation.1 | async-start | bytes 262144 | tf_op jit(solution)/shard_map/all_to_all | solution.py:43
  37.3 10.4 %all-to-all-start.2 = ((bf16[32,2,1152]{2,1,0:T(2,128)(2,1)}), bf16[32,2,1152]{2,1,0:T(2,128)(2,1)S(1)}, u32[]{:S(2)}, u32[]{:S(2)}) async-start(bf16[32,2,1152]{2,1,0:T(2,128)(2,1)} %bitcast.8), calls=%async_computation.2 | async-start | bytes 294912 | tf_op jit(solution)/shard_map/all_to_all | solution.py:72

commit v2 on v1

--- a/solution.py
+++ b/solution.py
@@ -33,16 +33,20 @@
     )
     probs = jax.nn.softmax(gate_logits, axis=-1)
 
+    block = experts * own
     every = lax.all_to_all(
-        jnp.broadcast_to(events[None], (devices, own, width)), BOTH, 0, 0, tiled=True
+        jnp.broadcast_to(events[None], (experts, own, width)), "expert", 0, 0, tiled=True
+    ).reshape(block, width)
+    every = lax.all_to_all(
+        jnp.broadcast_to(every[None], (dp, block, width)), "dp", 0, 0, tiled=True
     ).reshape(rows, width)
     pre = jnp.dot(every, w_in[0], preferred_element_type=jnp.float32)
     hidden = gelu_tanh(pre).astype(jnp.bfloat16)
     part = jnp.dot(hidden, w_out[0], preferred_element_type=jnp.float32).astype(jnp.bfloat16)
 
-    parts = lax.all_to_all(part.reshape(devices, own, width), BOTH, 0, 0, tiled=True)
-    parts = parts.reshape(dp, experts, own, width).astype(jnp.float32)
-    outs = jnp.sum(parts, 0).astype(jnp.bfloat16)
+    parts = lax.all_to_all(part.reshape(dp, block, width), "dp", 0, 0, tiled=True)
+    outs = jnp.sum(parts.astype(jnp.float32), 0).astype(jnp.bfloat16)
+    outs = lax.all_to_all(outs.reshape(experts, own, width), "expert", 0, 0, tiled=True)
     outs_wide = outs.astype(jnp.float32)
     mixed = jnp.sum(
         jnp.transpose(probs, (0, 2, 1))[..., None] * outs_wide[None], 1
@@ -67,9 +71,11 @@
     packed = jnp.transpose(jnp.concatenate(pieces_of(dgate), 0), (1, 2, 0))
     packed = jnp.pad(packed, ((0, 0), (0, 0), (0, 128 - 3 * tasks)))
     message = jnp.concatenate([dexpert, packed], -1)
-    message = jnp.broadcast_to(message[None], (dp, experts, own, width + 128))
-    message = message.reshape(devices, own, width + 128)
-    arrived = lax.all_to_all(message, BOTH, 0, 0, tiled=True).reshape(rows, width + 128)
+    arrived = lax.all_to_all(message, "expert", 0, 0, tiled=True)
+    arrived = arrived.reshape(block, width + 128)
+    arrived = lax.all_to_all(
+        jnp.broadcast_to(arrived[None], (dp, block, width + 128)), "dp", 0, 0, tiled=True
+    ).reshape(rows, width + 128)
     all_grads = arrived[:, :width]
     gate_rows = arrived[:, width : width + 3 * tasks]
 

time: 57.9 us -> 77.8 us (1.34)
  blocking collectives: 0 us -> 30 us
  waiting for transfers between devices: 21.7 us -> 14.3 us
  starting transfers between devices: 12.4 us -> 9.99 us
  local copies, waits for them, and re-layouts: 8.36 us -> 7.4 us
    all_to_all x0 -> x3, blocking collectives: none -> 30 us  [the longest x1 13.8 us: per_device(): lax.all_to_all(jnp.broadcast_to(events[None], (experts, own, width)), 'ex...]
    all_to_all x3, waiting for transfers between devices: 21.7 us -> 14.3 us  [the longest x1 6.43 us: per_device(): lax.all_to_all(outs.reshape(experts, own, width), 'expert', 0, 0, tiled=T...]
    all_to_all x3, starting transfers between devices: 12.4 us -> 9.99 us  [the longest x1 3.34 us: per_device(): lax.all_to_all(outs.reshape(experts, own, width), 'expert', 0, 0, tiled=T...]
    broadcast_in_dim x2 -> x5, local copies, waits for them, and re-layouts: 2.3 us -> 1.57 us  [the longest x1 0.86 us: per_device(): jnp.broadcast_to(events[None], (experts, own, width))]
  transfers between devices with their start and end apart: 3 -> 3, of which waited for: 3 -> 3; matrix products, arithmetic and copies ran while one was open for 3% -> 2% of each run, Pallas kernels for 0% -> 0%
where the time goes in v2:
time: 77.8 us; the launch traced here: 77.1 us
  blocking collectives  30 us (39%)
  waiting for transfers between devices  14.3 us (18%)
  matrix products  13.6 us (17%)
  starting transfers between devices  9.99 us (13%)
  local copies, waits for them, and re-layouts  7.4 us (10%)
  other arithmetic  1 us (1%)
  between operations  0.83 us (1%)
    all_to_all x1, blocking collectives, per_device(): lax.all_to_all(jnp.broadcast_to(events[None], (experts, own, width)), 'ex...  13.8 us
    all_to_all x1, blocking collectives, per_device(): arrived = lax.all_to_all(message, 'expert', 0, 0, tiled=True)  9.09 us
    all_to_all x1, blocking collectives, per_device(): lax.all_to_all(jnp.broadcast_to(arrived[None], (dp, block, width + 128)),...  7.16 us
    all_to_all x1, waiting for transfers between devices, per_device(): lax.all_to_all(outs.reshape(experts, own, width), 'expert', 0, 0, tiled=T...  6.43 us
    all_to_all x1, waiting for transfers between devices, per_device(): lax.all_to_all(part.reshape(dp, block, width), 'dp', 0, 0, tiled=True)  4.44 us
    unnamed x14, local copies, waits for them, and re-layouts  4.26 us
    all_to_all x1, waiting for transfers between devices, per_device(): lax.all_to_all(jnp.broadcast_to(every[None], (dp, block, width)), 'dp', 0...  3.43 us
    all_to_all x1, starting transfers between devices, per_device(): lax.all_to_all(outs.reshape(experts, own, width), 'expert', 0, 0, tiled=T...  3.34 us
  transfers between devices with their start and end apart: 3, of which 3 were waited for; matrix products, arithmetic and copies ran while one was open for 2% of the time, Pallas kernels for 0%

profile of v2, /device:TPU:0, one launch (start us, length us, event | category | flops | bytes accessed | tf_op | source)
XLA Modules:
  0.0 77.1 jit_solution(5241642533615835398)
XLA Ops:
  0.6 0.9 %broadcast_in_dim.16 = bf16[8,2,1024]{2,1,0:T(2,128)(2,1)S(1)} broadcast(bf16[2,1024]{1,0:T(2,128)(2,1)} %param.9), dimensions={1,2} | broadcast | bytes 36864 | tf_op jit(solution)/shard_map/broadcast_in_dim | solution.py:38
  1.5 13.8 %all_to_all.30 = bf16[8,2,1024]{2,1,0:T(2,128)(2,1)S(1)} all-to-all(bf16[8,2,1024]{2,1,0:T(2,128)(2,1)S(1)} %broadcast_in_dim.16), channel_id=1, replica_groups=mesh['dp'=4,'expert'=8] {'expert'}, dimensions={0} | all-to-all | bytes 65536 | tf_op jit(solution)/shard_map/all_to_all | solution.py:37
  15.3 0.7 broadcast_in_dim.18
  16.0 3.3 %all-to-all-start.1 = ((bf16[4,16,1024]{2,1,0:T(8,128)(2,1)}), bf16[4,16,1024]{2,1,0:T(8,128)(2,1)S(1)}, u32[]{:S(2)}, u32[]{:S(2)}) async-start(bf16[4,16,1024]{2,1,0:T(8,128)(2,1)} %broadcast_in_dim.18), calls=%async_computation.1 | async-start | bytes 262144 | tf_op jit(solution)/shard_map/all_to_all | solution.py:40
  19.3 1.2 %bitcast_reduce_fusion = (f32[4,2]{1,0:T(4,128)S(1)}, f32[4,8,2]{1,2,0:T(2,128)S(1)}) fusion(bf16[4,1024,8]{1,2,0:T(8,128)(2,1)} %param.13, bf16[2,1024]{1,0:T(2,128)(2,1)} %param.9), kind=kOutput, calls=%fused_computation.67 | convolution fusion | flops 131128 | bytes 69920 | tf_op jit(solution)/shard_map/rd,tde->tre/dot_general | solution.py:31
  20.5 3.4 %all-to-all-done.1 = bf16[4,16,1024]{2,1,0:T(8,128)(2,1)S(1)} async-done(((bf16[4,16,1024]{2,1,0:T(8,128)(2,1)}), bf16[4,16,1024]{2,1,0:T(8,128)(2,1)S(1)}, u32[]{:S(2)}, u32[]{:S(2)}) %all-to-all-start.1) | async-done | bytes 131104 | tf_op jit(solution)/shard_map/all_to_all | solution.py:40
  23.9 2.1 %fusion.5 = f32[64,1024]{1,0:T(8,128)S(1)} fusion(bf16[64,1024]{1,0:T(8,128)(2,1)S(1)} %bitcast.52, bf16[1,1024,1024]{2,1,0:T(8,128)(2,1)} %param.11), kind=kOutput, calls=%fused_computation.5 | convolution fusion | flops 134217728 | bytes 2490368 | tf_op jit(solution)/shard_map/dot_general | solution.py:43
  26.0 1.1 %fusion.7 = bf16[64,1024]{1,0:T(8,128)(2,1)} fusion(bf16[1,1024,1024]{2,1,0:T(8,128)(2,1)S(1)} %copy-done, f32[64,1024]{1,0:T(8,128)S(1)} %fusion.5), kind=kOutput, calls=%fused_computation.9 | convolution fusion | flops 134873088 | bytes 2490368 | tf_op jit(solution)/shard_map/dot_general | solution.py:45
  27.2 3.3 %all-to-all-start.2 = ((bf16[4,16,1024]{2,1,0:T(8,128)(2,1)}), bf16[4,16,1024]{2,1,0:T(8,128)(2,1)S(1)}, u32[]{:S(2)}, u32[]{:S(2)}) async-start(bf16[4,16,1024]{2,1,0:T(8,128)(2,1)} %bitcast.5), calls=%async_computation.2 | async-start | bytes 262144 | tf_op jit(solution)/shard_map/all_to_all | solution.py:47
  30.5 0.2 fusion.52
  30.7 4.4 %all-to-all-done.2 = bf16[4,16,1024]{2,1,0:T(8,128)(2,1)S(1)} async-done(((bf16[4,16,1024]{2,1,0:T(8,128)(2,1)}), bf16[4,16,1024]{2,1,0:T(8,128)(2,1)S(1)}, u32[]{:S(2)}, u32[]{:S(2)}) %all-to-all-start.2) | async-done | bytes 131104 | tf_op jit(solution)/shard_map/all_to_all | solution.py:47
  35.1 0.6 reshape.41
  35.7 3.3 %all-to-all-start.3 = ((bf16[8,2,1024]{2,1,0:T(2,128)(2,1)}), bf16[8,2,1024]{2,1,0:T(2,128)(2,1)S(1)}, u32[]{:S(2)}, u32[]{:S(2)}) async-start(bf16[8,2,1024]{2,1,0:T(2,128)(2,1)} %reshape.41), calls=%async_computation.3 | async-start | bytes 65536 | tf_op jit(solution)/shard_map/all_to_all | solution.py:49
  39.2 0.1 copy.67
  39.3 6.4 %all-to-all-done.3 = bf16[8,2,1024]{2,1,0:T(2,128)(2,1)S(1)} async-done(((bf16[8,2,1024]{2,1,0:T(2,128)(2,1)}), bf16[8,2,1024]{2,1,0:T(2,128)(2,1)S(1)}, u32[]{:S(2)}, u32[]{:S(2)}) %all-to-all-start.3) | async-done | bytes 32800 | tf_op jit(solution)/shard_map/all_to_all | solution.py:49
  45.7 0.2 multiply_reduce_fusion.2
  45.9 2.0 %fusion.66 = f32[4,2,256]{2,1,0:T(2,128)S(1)} fusion(bf16[4,2,1024]{2,1,0:T(2,128)(2,1)S(1)} %multiply_reduce_fusion.2, bf16[4,1024,256]{2,1,0:T(8,128)(2,1)} %param.14), kind=kOutput, calls=%fused_computation.87 | convolution fusion | flops 4194304 | bytes 2121728 | tf_op jit(solution)/shard_map/trd,tdk->trk/dot_general | solution.py:55
  47.9 0.1 multiply_reduce_fusion.3
  48.0 0.1 copy.76
  48.1 0.1 copy.68
  48.2 0.1 fusion.63
  48.4 2.2 %fusion.37 = f32[4,6,1024]{2,1,0:T(8,128)S(1)} fusion(bf16[4,1024,256]{2,1,0:T(8,128)(2,1)} %param.14, bf16[4,6,256]{2,0,1:T(4,128)(2,1)S(1)} %pad_maximum_fusion), kind=kOutput, calls=%fused_computation.41 | convolution fusion | flops 12582912 | bytes 2207744 | tf_op jit(solution)/shard_map/trk,tdk->trd/dot_general | solution.py:63
  50.8 0.1 multiply_reduce_fusion.1
  50.9 0.1 fusion.65
  51.0 0.1 copy.77
  51.1 9.1 %all_to_all.31 = bf16[8,2,1152]{2,1,0:T(2,128)(2,1)S(1)} all-to-all(bf16[8,2,1152]{2,1,0:T(2,128)(2,1)S(1)} %copy.73), channel_id=1, replica_groups=mesh['dp'=4,'expert'=8] {'expert'}, dimensions={0} | all-to-all | bytes 73728 | tf_op jit(solution)/shard_map/all_to_all | solution.py:74
  60.3 7.2 %all_to_all.32 = bf16[4,16,1152]{2,1,0:T(8,128)(2,1)S(1)} all-to-all(bf16[4,16,1152]{2,1,0:T(8,128)(2,1)S(1)} %broadcast_in_dim.20), channel_id=1, replica_groups=mesh['dp'=4,'expert'=8] {'dp'}, dimensions={0} | all-to-all | bytes 294912 | tf_op jit(solution)/shard_map/all_to_all | solution.py:76
  67.4 2.8 %convert_bitcast_fusion.1 = bf16[1,1024,1024]{1,2,0:T(8,128)(2,1)} fusion(bf16[64,1024]{1,0:T(8,128)(2,1)S(1)} %bitcast.53, f32[64,1024]{1,0:T(8,128)S(1)} %fusion.5, bf16[1,1024,1024]{2,1,0:T(8,128)(2,1)S(1)} %copy-done, bf16[64,1152]{1,0:T(8,128)(2,1)S(1)} %bitcast.55), kind=kOutput, calls=%fused_computation.8 | convolution fusion | flops 270794752 | bytes 4718592 | tf_op jit(solution)/shard_map/dot_general | solution.py:89
  70.2 2.1 %convert_bitcast_fusion = bf16[1,1024,1024]{2,1,0:T(8,128)(2,1)} fusion(bf16[64,1152]{1,0:T(8,128)(2,1)S(1)} %bitcast.56, f32[64,1024]{1,0:T(8,128)S(1)} %fusion.5), kind=kOutput, calls=%fused_computation.7 | convolution fusion | flops 135856128 | bytes 2490368 | tf_op jit(solution)/shard_map/dot_general | solution.py:86
  72.3 3.9 %copy.75 = bf16[1,1024,1024]{2,1,0:T(8,128)(2,1)} copy(bf16[1,1024,1024]{1,2,0:T(8,128)(2,1)} %convert_bitcast_fusion.1) | data formatting | bytes 4194304
  76.3 0.2 convolution_reduce_fusion
  76.5 0.6 broadcast_in_dim.23
  (28 shorter events, 0.6 us)
Async XLA Ops:
  0.6 25.3 %copy-start = (bf16[1,1024,1024]{2,1,0:T(8,128)(2,1)S(1)}, bf16[1,1024,1024]{2,1,0:T(8,128)(2,1)}, u32[]{:S(2)}) copy-start(bf16[1,1024,1024]{2,1,0:T(8,128)(2,1)} %param.12) | copy-start | bytes 6291460
  16.0 7.9 %all-to-all-start.1 = ((bf16[4,16,1024]{2,1,0:T(8,128)(2,1)}), bf16[4,16,1024]{2,1,0:T(8,128)(2,1)S(1)}, u32[]{:S(2)}, u32[]{:S(2)}) async-start(bf16[4,16,1024]{2,1,0:T(8,128)(2,1)} %broadcast_in_dim.18), calls=%async_computation.1 | async-start | bytes 262144 | tf_op jit(solution)/shard_map/all_to_all | solution.py:40
  26.0 13.2 %copy-start.3 = (s32[2,4]{1,0:T(2,128)S(1)}, s32[2,4]{1,0:T(2,128)}, u32[]{:S(2)}) copy-start(s32[2,4]{1,0:T(2,128)} %param.10) | copy-start | bytes 100
  26.0 21.9 %copy-start.1 = (f32[4,256]{1,0:T(4,128)S(1)}, f32[4,256]{1,0:T(4,128)}, u32[]{:S(2)}) copy-start(f32[4,256]{1,0:T(4,128)} %param.15) | copy-start | bytes 12292
  26.0 21.9 %copy-start.2 = (f32[4,256]{1,0:T(4,128)S(1)}, f32[4,256]{1,0:T(4,128)}, u32[]{:S(2)}) copy-start(f32[4,256]{1,0:T(4,128)} %param.16) | copy-start | bytes 12292
  26.0 22.1 %copy-start.4 = (f32[4]{0:T(128)S(1)}, f32[4]{0:T(128)}, u32[]{:S(2)}) copy-start(f32[4]{0:T(128)} %param.17) | copy-start | bytes 52
  27.2 7.9 %all-to-all-start.2 = ((bf16[4,16,1024]{2,1,0:T(8,128)(2,1)}), bf16[4,16,1024]{2,1,0:T(8,128)(2,1)S(1)}, u32[]{:S(2)}, u32[]{:S(2)}) async-start(bf16[4,16,1024]{2,1,0:T(8,128)(2,1)} %bitcast.5), calls=%async_computation.2 | async-start | bytes 262144 | tf_op jit(solution)/shard_map/all_to_all | solution.py:47
  35.7 10.0 %all-to-all-start.3 = ((bf16[8,2,1024]{2,1,0:T(2,128)(2,1)}), bf16[8,2,1024]{2,1,0:T(2,128)(2,1)S(1)}, u32[]{:S(2)}, u32[]{:S(2)}) async-start(bf16[8,2,1024]{2,1,0:T(2,128)(2,1)} %reshape.41), calls=%async_computation.3 | async-start | bytes 65536 | tf_op jit(solution)/shard_map/all_to_all | solution.py:49

commit v3 on v1

--- a/solution.py
+++ b/solution.py
@@ -18,31 +18,39 @@
     return high, middle, low
 
 
+def partners(value, axis):
+    size = lax.axis_size(axis)
+    got = [value[0]]
+    for k in range(1, size):
+        got.append(lax.ppermute(value[k], axis, [(i, i ^ k) for i in range(size)]))
+    return got
+
+
 def per_device(
     events, labels, w_in, w_out, gate_weight, tower_in, tower_bias, tower_out, tower_out_bias
 ):
     dp = lax.axis_size("dp")
     experts = lax.axis_size("expert")
-    devices = dp * experts
     own, width = events.shape
     tasks = tower_in.shape[0]
-    rows = devices * own
 
     gate_logits = jnp.einsum(
         "rd,tde->tre", events, gate_weight, preferred_element_type=jnp.float32
     )
     probs = jax.nn.softmax(gate_logits, axis=-1)
 
-    every = lax.all_to_all(
-        jnp.broadcast_to(events[None], (devices, own, width)), BOTH, 0, 0, tiled=True
-    ).reshape(rows, width)
+    slots = jnp.arange(experts) ^ lax.axis_index("expert")
+    probs = jnp.take(probs, slots, axis=2)
+
+    every = jnp.concatenate(partners([events] * experts, "expert"), 0)
+    every = jnp.concatenate(partners([every] * dp, "dp"), 0)
     pre = jnp.dot(every, w_in[0], preferred_element_type=jnp.float32)
     hidden = gelu_tanh(pre).astype(jnp.bfloat16)
     part = jnp.dot(hidden, w_out[0], preferred_element_type=jnp.float32).astype(jnp.bfloat16)
 
-    parts = lax.all_to_all(part.reshape(devices, own, width), BOTH, 0, 0, tiled=True)
-    parts = parts.reshape(dp, experts, own, width).astype(jnp.float32)
-    outs = jnp.sum(parts, 0).astype(jnp.bfloat16)
+    parts = partners(part.reshape(dp, experts * own, width), "dp")
+    outs = sum(piece.astype(jnp.float32) for piece in parts).astype(jnp.bfloat16)
+    outs = jnp.stack(partners(outs.reshape(experts, own, width), "expert"), 0)
     outs_wide = outs.astype(jnp.float32)
     mixed = jnp.sum(
         jnp.transpose(probs, (0, 2, 1))[..., None] * outs_wide[None], 1
@@ -67,9 +75,8 @@
     packed = jnp.transpose(jnp.concatenate(pieces_of(dgate), 0), (1, 2, 0))
     packed = jnp.pad(packed, ((0, 0), (0, 0), (0, 128 - 3 * tasks)))
     message = jnp.concatenate([dexpert, packed], -1)
-    message = jnp.broadcast_to(message[None], (dp, experts, own, width + 128))
-    message = message.reshape(devices, own, width + 128)
-    arrived = lax.all_to_all(message, BOTH, 0, 0, tiled=True).reshape(rows, width + 128)
+    arrived = jnp.concatenate(partners(message, "expert"), 0)
+    arrived = jnp.concatenate(partners([arrived] * dp, "dp"), 0)
     all_grads = arrived[:, :width]
     gate_rows = arrived[:, width : width + 3 * tasks]
 

time: 57.9 us -> 79.4 us (1.37)
  starting transfers between devices: 12.4 us -> 41.1 us
  local copies, waits for them, and re-layouts: 8.36 us -> 3.97 us
  waiting for transfers between devices: 21.7 us -> 19.2 us
    ppermute x0 -> x30, starting transfers between devices: none -> 41.1 us  [partners(): got.append(lax.ppermute(value[k], axis, [(i, i ^ k) for i in range(size)]))]
    all_to_all x3 -> x0, waiting for transfers between devices: 21.7 us -> none  [the longest x1 7.77 us: per_device(): lax.all_to_all(message, BOTH, 0, 0, tiled=True).reshape(rows, width + 128)]
    ppermute x0 -> x30, waiting for transfers between devices: none -> 19.2 us  [partners(): got.append(lax.ppermute(value[k], axis, [(i, i ^ k) for i in range(size)]))]
    all_to_all x3 -> x0, starting transfers between devices: 12.4 us -> none  [the longest x1 7.3 us: per_device(): lax.all_to_all(jnp.broadcast_to(events[None], (devices, own, width)), BOT...]
    unnamed x14 -> x21, local copies, waits for them, and re-layouts: 4.26 us -> 0.37 us
    broadcast_in_dim x2 -> x0, local copies, waits for them, and re-layouts: 2.3 us -> none  [the longest x1 1.56 us: per_device(): jnp.broadcast_to(events[None], (devices, own, width))]
    concatenate x1 -> x4, local copies, waits for them, and re-layouts: 0.03 us -> 1.74 us  [the longest x1 0.76 us: per_device(): every = jnp.concatenate(partners([every] * dp, 'dp'), 0)]
    sub x0 -> x1, matrix products: none -> 1.26 us  [per_device(): probs = jax.nn.softmax(gate_logits, axis=-1)]
  transfers between devices with their start and end apart: 3 -> 30, of which waited for: 3 -> 13; matrix products, arithmetic and copies ran while one was open for 3% -> 3% of each run, Pallas kernels for 0% -> 0%
where the time goes in v3:
time: 79.4 us; the launch traced here: 79.1 us
  starting transfers between devices  41.1 us (52%)
  waiting for transfers between devices  19.2 us (24%)
  matrix products  12.9 us (16%)
  local copies, waits for them, and re-layouts  3.97 us (5%)
  between operations  0.99 us (1%)
  other arithmetic  0.87 us (1%)
    ppermute x30, starting transfers between devices, partners(): got.append(lax.ppermute(value[k], axis, [(i, i ^ k) for i in range(size)]))  41.1 us
    ppermute x30, waiting for transfers between devices, partners(): got.append(lax.ppermute(value[k], axis, [(i, i ^ k) for i in range(size)]))  19.2 us
    dot_general x1, matrix products, per_device(): lax.dot_general(every, dpre, (((0,), (0,)), ((), ())), preferred_element_...  2.67 us
    dot_general x1, matrix products, per_device(): jnp.einsum('trk,tdk->trd', stacked, tower_in, preferred_element_type=jnp....  2.23 us
    dot_general x1, matrix products, per_device(): lax.dot_general(hidden, all_grads, (((0,), (0,)), ((), ())), preferred_el...  2.07 us
    dot_general x1, matrix products, per_device(): pre = jnp.dot(every, w_in[0], preferred_element_type=jnp.float32)  2.07 us
    dot_general x1, matrix products, per_device(): jnp.einsum('trd,tdk->trk', mixed, tower_in, preferred_element_type=jnp.fl...  1.97 us
  transfers between devices with their start and end apart: 30, of which 13 were waited for; matrix products, arithmetic and copies ran while one was open for 3% of the time, Pallas kernels for 0%

profile of v3, /device:TPU:0, one launch (start us, length us, event | category | flops | bytes accessed | tf_op | source)
XLA Modules:
  0.0 79.1 jit_solution(5564650043224536314)
XLA Ops:
  0.6 6.1 %collective-permute-start.6 = (bf16[2,1024]{1,0:T(2,128)(2,1)}, bf16[2,1024]{1,0:T(2,128)(2,1)S(1)}, u32[]{:S(2)}, u32[]{:S(2)}) collective-permute-start(bf16[2,1024]{1,0:T(2,128)(2,1)} %param.9), channel_id=1, source_target_pairs={{0,7},{1,6},{2,5},{3,4},{4,3},{5,2},{6,1},{7,0},{8,15},{9,14},{10,... | collective-permute-start | bytes 12296 | tf_op jit(solution)/shard_map/ppermute | solution.py:25
  7.7 2.0 %collective-permute-start.3 = (bf16[2,1024]{1,0:T(2,128)(2,1)}, bf16[2,1024]{1,0:T(2,128)(2,1)S(1)}, u32[]{:S(2)}, u32[]{:S(2)}) collective-permute-start(bf16[2,1024]{1,0:T(2,128)(2,1)} %param.9), channel_id=1, source_target_pairs={{0,4},{1,5},{2,6},{3,7},{4,0},{5,1},{6,2},{7,3},{8,12},{9,13},{10,... | collective-permute-start | bytes 12296 | tf_op jit(solution)/shard_map/ppermute | solution.py:25
  9.7 2.3 %collective-permute-start.2 = (bf16[2,1024]{1,0:T(2,128)(2,1)}, bf16[2,1024]{1,0:T(2,128)(2,1)S(1)}, u32[]{:S(2)}, u32[]{:S(2)}) collective-permute-start(bf16[2,1024]{1,0:T(2,128)(2,1)} %param.9), channel_id=1, source_target_pairs={{0,3},{1,2},{2,1},{3,0},{4,7},{5,6},{6,5},{7,4},{8,11},{9,10},{10,... | collective-permute-start | bytes 12296 | tf_op jit(solution)/shard_map/ppermute | solution.py:25
  12.0 1.3 %fusion.72 = (f32[4,2]{1,0:T(4,128)S(1)}, f32[4,2,8]{2,1,0:T(2,128)S(1)}) fusion(bf16[4,1024,8]{1,2,0:T(8,128)(2,1)} %param.13, bf16[2,1024]{1,0:T(2,128)(2,1)} %param.9), kind=kOutput, calls=%fused_computation.105 | convolution fusion | flops 131207 | bytes 69920 | tf_op jit(solution)/shard_map/sub | solution.py:40
  13.3 0.8 %collective-permute-start.1 = (bf16[2,1024]{1,0:T(2,128)(2,1)}, bf16[2,1024]{1,0:T(2,128)(2,1)S(1)}, u32[]{:S(2)}, u32[]{:S(2)}) collective-permute-start(bf16[2,1024]{1,0:T(2,128)(2,1)} %param.9), channel_id=1, source_target_pairs={{0,2},{1,3},{2,0},{3,1},{4,6},{5,7},{6,4},{7,5},{8,10},{9,11},{10,... | collective-permute-start | bytes 12296 | tf_op jit(solution)/shard_map/ppermute | solution.py:25
  14.7 2.5 %collective-permute-done.1 = bf16[2,1024]{1,0:T(2,128)(2,1)S(1)} collective-permute-done((bf16[2,1024]{1,0:T(2,128)(2,1)}, bf16[2,1024]{1,0:T(2,128)(2,1)S(1)}, u32[]{:S(2)}, u32[]{:S(2)}) %collective-permute-start.1) | collective-permute-done | bytes 4128 | tf_op jit(solution)/shard_map/ppermute | solution.py:25
  18.8 1.6 %collective-permute-start.8 = (bf16[16,1024]{1,0:T(8,128)(2,1)S(1)}, bf16[16,1024]{1,0:T(8,128)(2,1)S(1)}, u32[]{:S(2)}, u32[]{:S(2)}) collective-permute-start(bf16[16,1024]{1,0:T(8,128)(2,1)S(1)} %concatenate.27), channel_id=1, source_target_pairs={{0,16},{8,24},{16,0},{24,8},{1,17},{9,25},{17,1},{25,9},{2,18},{10... | collective-permute-start | bytes 98312 | tf_op jit(solution)/shard_map/ppermute | solution.py:25
  20.6 1.8 %collective-permute-done.9 = bf16[16,1024]{1,0:T(8,128)(2,1)S(1)} collective-permute-done((bf16[16,1024]{1,0:T(8,128)(2,1)S(1)}, bf16[16,1024]{1,0:T(8,128)(2,1)S(1)}, u32[]{:S(2)}, u32[]{:S(2)}) %collective-permute-start.9) | collective-permute-done | bytes 32800 | tf_op jit(solution)/shard_map/ppermute | solution.py:25
  23.6 2.1 %fusion.6 = f32[64,1024]{1,0:T(8,128)S(1)} fusion(bf16[64,1024]{1,0:T(8,128)(2,1)S(1)} %concatenate.28, bf16[1,1024,1024]{2,1,0:T(8,128)(2,1)} %param.11), kind=kOutput, calls=%fused_computation.7 | convolution fusion | flops 134217728 | bytes 2490368 | tf_op jit(solution)/shard_map/dot_general | solution.py:47
  26.6 1.3 %collective-permute-start.12 = (bf16[16,1024]{1,0:T(8,128)(2,1)S(1)}, bf16[16,1024]{1,0:T(8,128)(2,1)S(1)}, u32[]{:S(2)}, u32[]{:S(2)}) collective-permute-start(bf16[16,1024]{1,0:T(8,128)(2,1)S(1)} %get-tuple-element.8), channel_id=1, source_target_pairs={{0,24},{8,16},{16,8},{24,0},{1,25},{9,17},{17,9},{25,1},{2,26},{10... | collective-permute-start | bytes 98312 | tf_op jit(solution)/shard_map/ppermute | solution.py:25
  28.4 1.5 %collective-permute-done.12 = bf16[16,1024]{1,0:T(8,128)(2,1)S(1)} collective-permute-done((bf16[16,1024]{1,0:T(8,128)(2,1)S(1)}, bf16[16,1024]{1,0:T(8,128)(2,1)S(1)}, u32[]{:S(2)}, u32[]{:S(2)}) %collective-permute-start.12) | collective-permute-done | bytes 32800 | tf_op jit(solution)/shard_map/ppermute | solution.py:25
  29.9 1.9 %collective-permute-done.11 = bf16[16,1024]{1,0:T(8,128)(2,1)S(1)} collective-permute-done((bf16[16,1024]{1,0:T(8,128)(2,1)S(1)}, bf16[16,1024]{1,0:T(8,128)(2,1)S(1)}, u32[]{:S(2)}, u32[]{:S(2)}) %collective-permute-start.11) | collective-permute-done | bytes 32800 | tf_op jit(solution)/shard_map/ppermute | solution.py:25
  31.9 3.6 %collective-permute-start.19 = (bf16[2,1024]{1,0:T(2,128)(2,1)S(1)}, bf16[2,1024]{1,0:T(2,128)(2,1)S(1)}, u32[]{:S(2)}, u32[]{:S(2)}) collective-permute-start(bf16[2,1024]{1,0:T(2,128)(2,1)S(1)} %get-tuple-element.18), channel_id=1, source_target_pairs={{0,7},{1,6},{2,5},{3,4},{4,3},{5,2},{6,1},{7,0},{8,15},{9,14},{10,... | collective-permute-start | bytes 12296 | tf_op jit(solution)/shard_map/ppermute | solution.py:25
  36.5 1.4 %collective-permute-start.17 = (bf16[2,1024]{1,0:T(2,128)(2,1)S(1)}, bf16[2,1024]{1,0:T(2,128)(2,1)S(1)}, u32[]{:S(2)}, u32[]{:S(2)}) collective-permute-start(bf16[2,1024]{1,0:T(2,128)(2,1)S(1)} %get-tuple-element.20), channel_id=1, source_target_pairs={{0,5},{1,4},{2,7},{3,6},{4,1},{5,0},{6,3},{7,2},{8,13},{9,12},{10,... | collective-permute-start | bytes 12296 | tf_op jit(solution)/shard_map/ppermute | solution.py:25
  37.9 2.5 %collective-permute-start.16 = (bf16[2,1024]{1,0:T(2,128)(2,1)S(1)}, bf16[2,1024]{1,0:T(2,128)(2,1)S(1)}, u32[]{:S(2)}, u32[]{:S(2)}) collective-permute-start(bf16[2,1024]{1,0:T(2,128)(2,1)S(1)} %get-tuple-element.21), channel_id=1, source_target_pairs={{0,4},{1,5},{2,6},{3,7},{4,0},{5,1},{6,2},{7,3},{8,12},{9,13},{10,... | collective-permute-start | bytes 12296 | tf_op jit(solution)/shard_map/ppermute | solution.py:25
  40.4 1.3 %collective-permute-start.15 = (bf16[2,1024]{1,0:T(2,128)(2,1)S(1)}, bf16[2,1024]{1,0:T(2,128)(2,1)S(1)}, u32[]{:S(2)}, u32[]{:S(2)}) collective-permute-start(bf16[2,1024]{1,0:T(2,128)(2,1)S(1)} %get-tuple-element.22), channel_id=1, source_target_pairs={{0,3},{1,2},{2,1},{3,0},{4,7},{5,6},{6,5},{7,4},{8,11},{9,10},{10,... | collective-permute-start | bytes 12296 | tf_op jit(solution)/shard_map/ppermute | solution.py:25
  42.3 1.5 %collective-permute-start.13 = (bf16[2,1024]{1,0:T(2,128)(2,1)S(1)}, bf16[2,1024]{1,0:T(2,128)(2,1)S(1)}, u32[]{:S(2)}, u32[]{:S(2)}) collective-permute-start(bf16[2,1024]{1,0:T(2,128)(2,1)S(1)} %get-tuple-element.24), channel_id=1, source_target_pairs={{0,1},{1,0},{2,3},{3,2},{4,5},{5,4},{6,7},{7,6},{8,9},{9,8},{10,11... | collective-permute-start | bytes 12296 | tf_op jit(solution)/shard_map/ppermute | solution.py:25
  44.0 0.8 %collective-permute-done.15 = bf16[2,1024]{1,0:T(2,128)(2,1)S(1)} collective-permute-done((bf16[2,1024]{1,0:T(2,128)(2,1)S(1)}, bf16[2,1024]{1,0:T(2,128)(2,1)S(1)}, u32[]{:S(2)}, u32[]{:S(2)}) %collective-permute-start.15) | collective-permute-done | bytes 4128 | tf_op jit(solution)/shard_map/ppermute | solution.py:25
  46.2 2.0 %fusion.75 = f32[4,2,256]{2,1,0:T(2,128)S(1)} fusion(bf16[4,2,1024]{2,1,0:T(2,128)(2,1)S(1)} %multiply_reduce_fusion.2, bf16[4,1024,256]{2,1,0:T(8,128)(2,1)} %param.14), kind=kOutput, calls=%fused_computation.106 | convolution fusion | flops 4194304 | bytes 2121728 | tf_op jit(solution)/shard_map/trd,tdk->trk/dot_general | solution.py:59
  48.7 2.2 %fusion.42 = f32[4,6,1024]{2,1,0:T(8,128)S(1)} fusion(bf16[4,1024,256]{2,1,0:T(8,128)(2,1)} %param.14, bf16[4,6,256]{2,0,1:T(4,128)(2,1)S(1)} %pad_maximum_fusion), kind=kOutput, calls=%fused_computation.46 | convolution fusion | flops 12582912 | bytes 2207744 | tf_op jit(solution)/shard_map/trk,tdk->trd/dot_general | solution.py:67
  51.5 1.6 %collective-permute-start.20 = (bf16[2,1152]{1,0:T(2,128)(2,1)S(1)}, bf16[2,1152]{1,0:T(2,128)(2,1)S(1)}, u32[]{:S(2)}, u32[]{:S(2)}) collective-permute-start(bf16[2,1152]{1,0:T(2,128)(2,1)S(1)} %bitcast.84), channel_id=1, source_target_pairs={{0,1},{1,0},{2,3},{3,2},{4,5},{5,4},{6,7},{7,6},{8,9},{9,8},{10,11... | collective-permute-start | bytes 13832 | tf_op jit(solution)/shard_map/ppermute | solution.py:25
  53.1 1.2 %collective-permute-start.21 = (bf16[2,1152]{1,0:T(2,128)(2,1)S(1)}, bf16[2,1152]{1,0:T(2,128)(2,1)S(1)}, u32[]{:S(2)}, u32[]{:S(2)}) collective-permute-start(bf16[2,1152]{1,0:T(2,128)(2,1)S(1)} %bitcast.83), channel_id=1, source_target_pairs={{0,2},{1,3},{2,0},{3,1},{4,6},{5,7},{6,4},{7,5},{8,10},{9,11},{10,... | collective-permute-start | bytes 13832 | tf_op jit(solution)/shard_map/ppermute | solution.py:25
  54.4 0.8 %collective-permute-start.22 = (bf16[2,1152]{1,0:T(2,128)(2,1)S(1)}, bf16[2,1152]{1,0:T(2,128)(2,1)S(1)}, u32[]{:S(2)}, u32[]{:S(2)}) collective-permute-start(bf16[2,1152]{1,0:T(2,128)(2,1)S(1)} %bitcast.85), channel_id=1, source_target_pairs={{0,3},{1,2},{2,1},{3,0},{4,7},{5,6},{6,5},{7,4},{8,11},{9,10},{10,... | collective-permute-start | bytes 13832 | tf_op jit(solution)/shard_map/ppermute | solution.py:25
  55.2 2.3 %collective-permute-start.23 = (bf16[2,1152]{1,0:T(2,128)(2,1)S(1)}, bf16[2,1152]{1,0:T(2,128)(2,1)S(1)}, u32[]{:S(2)}, u32[]{:S(2)}) collective-permute-start(bf16[2,1152]{1,0:T(2,128)(2,1)S(1)} %bitcast.82), channel_id=1, source_target_pairs={{0,4},{1,5},{2,6},{3,7},{4,0},{5,1},{6,2},{7,3},{8,12},{9,13},{10,... | collective-permute-start | bytes 13832 | tf_op jit(solution)/shard_map/ppermute | solution.py:25
  57.5 1.6 %collective-permute-start.24 = (bf16[2,1152]{1,0:T(2,128)(2,1)S(1)}, bf16[2,1152]{1,0:T(2,128)(2,1)S(1)}, u32[]{:S(2)}, u32[]{:S(2)}) collective-permute-start(bf16[2,1152]{1,0:T(2,128)(2,1)S(1)} %bitcast.81), channel_id=1, source_target_pairs={{0,5},{1,4},{2,7},{3,6},{4,1},{5,0},{6,3},{7,2},{8,13},{9,12},{10,... | collective-permute-start | bytes 13832 | tf_op jit(solution)/shard_map/ppermute | solution.py:25
  59.1 3.6 %collective-permute-start.25 = (bf16[2,1152]{1,0:T(2,128)(2,1)S(1)}, bf16[2,1152]{1,0:T(2,128)(2,1)S(1)}, u32[]{:S(2)}, u32[]{:S(2)}) collective-permute-start(bf16[2,1152]{1,0:T(2,128)(2,1)S(1)} %bitcast.80), channel_id=1, source_target_pairs={{0,6},{1,7},{2,4},{3,5},{4,2},{5,3},{6,0},{7,1},{8,14},{9,15},{10,... | collective-permute-start | bytes 13832 | tf_op jit(solution)/shard_map/ppermute | solution.py:25
  62.9 1.6 %collective-permute-done.25 = bf16[2,1152]{1,0:T(2,128)(2,1)S(1)} collective-permute-done((bf16[2,1152]{1,0:T(2,128)(2,1)S(1)}, bf16[2,1152]{1,0:T(2,128)(2,1)S(1)}, u32[]{:S(2)}, u32[]{:S(2)}) %collective-permute-start.25) | collective-permute-done | bytes 4640 | tf_op jit(solution)/shard_map/ppermute | solution.py:25
  64.5 4.5 %collective-permute-done.26 = bf16[2,1152]{1,0:T(2,128)(2,1)S(1)} collective-permute-done((bf16[2,1152]{1,0:T(2,128)(2,1)S(1)}, bf16[2,1152]{1,0:T(2,128)(2,1)S(1)}, u32[]{:S(2)}, u32[]{:S(2)}) %collective-permute-start.26) | collective-permute-done | bytes 4640 | tf_op jit(solution)/shard_map/ppermute | solution.py:25
  69.8 1.2 %collective-permute-start.27 = (bf16[16,1152]{1,0:T(8,128)(2,1)S(1)}, bf16[16,1152]{1,0:T(8,128)(2,1)S(1)}, u32[]{:S(2)}, u32[]{:S(2)}) collective-permute-start(bf16[16,1152]{1,0:T(8,128)(2,1)S(1)} %concatenate.32), channel_id=1, source_target_pairs={{0,8},{8,0},{16,24},{24,16},{1,9},{9,1},{17,25},{25,17},{2,10},{10... | collective-permute-start | bytes 110600 | tf_op jit(solution)/shard_map/ppermute | solution.py:25
  71.0 1.5 %collective-permute-done.29 = bf16[16,1152]{1,0:T(8,128)(2,1)S(1)} collective-permute-done((bf16[16,1152]{1,0:T(8,128)(2,1)S(1)}, bf16[16,1152]{1,0:T(8,128)(2,1)S(1)}, u32[]{:S(2)}, u32[]{:S(2)}) %collective-permute-start.29) | collective-permute-done | bytes 36896 | tf_op jit(solution)/shard_map/ppermute | solution.py:25
  73.7 2.7 %convert_bitcast_fusion.1 = bf16[1,1024,1024]{2,1,0:T(8,128)(2,1)} fusion(bf16[64,1024]{1,0:T(8,128)(2,1)S(1)} %concatenate.28, f32[64,1024]{1,0:T(8,128)S(1)} %fusion.6, bf16[1,1024,1024]{2,1,0:T(8,128)(2,1)S(1)} %copy-done, bf16[64,1152]{1,0:T(8,128)(2,1)S(1)} %concatenate.33), kind=kOutput, calls=%fused_computation.10 | convolution fusion | flops 270794752 | bytes 4718592 | tf_op jit(solution)/shard_map/dot_general | solution.py:90
  76.3 2.1 %convert_bitcast_fusion = bf16[1,1024,1024]{2,1,0:T(8,128)(2,1)} fusion(bf16[64,1152]{1,0:T(8,128)(2,1)S(1)} %concatenate.33, f32[64,1024]{1,0:T(8,128)S(1)} %fusion.6), kind=kOutput, calls=%fused_computation.9 | convolution fusion | flops 135856128 | bytes 2490368 | tf_op jit(solution)/shard_map/dot_general | solution.py:87
  (101 shorter events, 13.0 us)
Async XLA Ops:
  0.6 25.0 %copy-start = (bf16[1,1024,1024]{2,1,0:T(8,128)(2,1)S(1)}, bf16[1,1024,1024]{2,1,0:T(8,128)(2,1)}, u32[]{:S(2)}) copy-start(bf16[1,1024,1024]{2,1,0:T(8,128)(2,1)} %param.12) | copy-start | bytes 6291460
  0.6 12.6 %collective-permute-start.6 = (bf16[2,1024]{1,0:T(2,128)(2,1)}, bf16[2,1024]{1,0:T(2,128)(2,1)S(1)}, u32[]{:S(2)}, u32[]{:S(2)}) collective-permute-start(bf16[2,1024]{1,0:T(2,128)(2,1)} %param.9), channel_id=1, source_target_pairs={{0,7},{1,6},{2,5},{3,4},{4,3},{5,2},{6,1},{7,0},{8,15},{9,14},{10,... | collective-permute-start | bytes 12296 | tf_op jit(solution)/shard_map/ppermute | solution.py:25
  6.7 7.4 %collective-permute-start.5 = (bf16[2,1024]{1,0:T(2,128)(2,1)}, bf16[2,1024]{1,0:T(2,128)(2,1)S(1)}, u32[]{:S(2)}, u32[]{:S(2)}) collective-permute-start(bf16[2,1024]{1,0:T(2,128)(2,1)} %param.9), channel_id=1, source_target_pairs={{0,6},{1,7},{2,4},{3,5},{4,2},{5,3},{6,0},{7,1},{8,14},{9,15},{10,... | collective-permute-start | bytes 12296 | tf_op jit(solution)/shard_map/ppermute | solution.py:25
  6.9 7.7 %collective-permute-start.4 = (bf16[2,1024]{1,0:T(2,128)(2,1)}, bf16[2,1024]{1,0:T(2,128)(2,1)S(1)}, u32[]{:S(2)}, u32[]{:S(2)}) collective-permute-start(bf16[2,1024]{1,0:T(2,128)(2,1)} %param.9), channel_id=1, source_target_pairs={{0,5},{1,4},{2,7},{3,6},{4,1},{5,0},{6,3},{7,2},{8,13},{9,12},{10,... | collective-permute-start | bytes 12296 | tf_op jit(solution)/shard_map/ppermute | solution.py:25
  7.7 7.0 %collective-permute-start.3 = (bf16[2,1024]{1,0:T(2,128)(2,1)}, bf16[2,1024]{1,0:T(2,128)(2,1)S(1)}, u32[]{:S(2)}, u32[]{:S(2)}) collective-permute-start(bf16[2,1024]{1,0:T(2,128)(2,1)} %param.9), channel_id=1, source_target_pairs={{0,4},{1,5},{2,6},{3,7},{4,0},{5,1},{6,2},{7,3},{8,12},{9,13},{10,... | collective-permute-start | bytes 12296 | tf_op jit(solution)/shard_map/ppermute | solution.py:25
  9.7 4.9 %collective-permute-start.2 = (bf16[2,1024]{1,0:T(2,128)(2,1)}, bf16[2,1024]{1,0:T(2,128)(2,1)S(1)}, u32[]{:S(2)}, u32[]{:S(2)}) collective-permute-start(bf16[2,1024]{1,0:T(2,128)(2,1)} %param.9), channel_id=1, source_target_pairs={{0,3},{1,2},{2,1},{3,0},{4,7},{5,6},{6,5},{7,4},{8,11},{9,10},{10,... | collective-permute-start | bytes 12296 | tf_op jit(solution)/shard_map/ppermute | solution.py:25
  13.3 3.9 %collective-permute-start.1 = (bf16[2,1024]{1,0:T(2,128)(2,1)}, bf16[2,1024]{1,0:T(2,128)(2,1)S(1)}, u32[]{:S(2)}, u32[]{:S(2)}) collective-permute-start(bf16[2,1024]{1,0:T(2,128)(2,1)} %param.9), channel_id=1, source_target_pairs={{0,2},{1,3},{2,0},{3,1},{4,6},{5,7},{6,4},{7,5},{8,10},{9,11},{10,... | collective-permute-start | bytes 12296 | tf_op jit(solution)/shard_map/ppermute | solution.py:25
  14.1 3.8 %collective-permute-start = (bf16[2,1024]{1,0:T(2,128)(2,1)}, bf16[2,1024]{1,0:T(2,128)(2,1)S(1)}, u32[]{:S(2)}, u32[]{:S(2)}) collective-permute-start(bf16[2,1024]{1,0:T(2,128)(2,1)} %param.9), channel_id=1, source_target_pairs={{0,1},{1,0},{2,3},{3,2},{4,5},{5,4},{6,7},{7,6},{8,9},{9,8},{10,11... | collective-permute-start | bytes 12296 | tf_op jit(solution)/shard_map/ppermute | solution.py:25
  18.7 3.7 %collective-permute-start.9 = (bf16[16,1024]{1,0:T(8,128)(2,1)S(1)}, bf16[16,1024]{1,0:T(8,128)(2,1)S(1)}, u32[]{:S(2)}, u32[]{:S(2)}) collective-permute-start(bf16[16,1024]{1,0:T(8,128)(2,1)S(1)} %concatenate.27), channel_id=1, source_target_pairs={{0,24},{8,16},{16,8},{24,0},{1,25},{9,17},{17,9},{25,1},{2,26},{10... | collective-permute-start | bytes 98312 | tf_op jit(solution)/shard_map/ppermute | solution.py:25
  18.8 4.0 %collective-permute-start.8 = (bf16[16,1024]{1,0:T(8,128)(2,1)S(1)}, bf16[16,1024]{1,0:T(8,128)(2,1)S(1)}, u32[]{:S(2)}, u32[]{:S(2)}) collective-permute-start(bf16[16,1024]{1,0:T(8,128)(2,1)S(1)} %concatenate.27), channel_id=1, source_target_pairs={{0,16},{8,24},{16,0},{24,8},{1,17},{9,25},{17,1},{25,9},{2,18},{10... | collective-permute-start | bytes 98312 | tf_op jit(solution)/shard_map/ppermute | solution.py:25
  20.3 2.5 %collective-permute-start.7 = (bf16[16,1024]{1,0:T(8,128)(2,1)S(1)}, bf16[16,1024]{1,0:T(8,128)(2,1)S(1)}, u32[]{:S(2)}, u32[]{:S(2)}) collective-permute-start(bf16[16,1024]{1,0:T(8,128)(2,1)S(1)} %concatenate.27), channel_id=1, source_target_pairs={{0,8},{8,0},{16,24},{24,16},{1,9},{9,1},{17,25},{25,17},{2,10},{10... | collective-permute-start | bytes 98312 | tf_op jit(solution)/shard_map/ppermute | solution.py:25
  26.2 22.2 %copy-start.4 = (f32[4]{0:T(128)S(1)}, f32[4]{0:T(128)}, u32[]{:S(2)}) copy-start(f32[4]{0:T(128)} %param.17) | copy-start | bytes 52
  26.2 2.2 %collective-permute-start.10 = (bf16[16,1024]{1,0:T(8,128)(2,1)S(1)}, bf16[16,1024]{1,0:T(8,128)(2,1)S(1)}, u32[]{:S(2)}, u32[]{:S(2)}) collective-permute-start(bf16[16,1024]{1,0:T(8,128)(2,1)S(1)} %get-tuple-element.7), channel_id=1, source_target_pairs={{0,8},{8,0},{16,24},{24,16},{1,9},{9,1},{17,25},{25,17},{2,10},{10... | collective-permute-start | bytes 98312 | tf_op jit(solution)/shard_map/ppermute | solution.py:25
  26.6 3.3 %collective-permute-start.12 = (bf16[16,1024]{1,0:T(8,128)(2,1)S(1)}, bf16[16,1024]{1,0:T(8,128)(2,1)S(1)}, u32[]{:S(2)}, u32[]{:S(2)}) collective-permute-start(bf16[16,1024]{1,0:T(8,128)(2,1)S(1)} %get-tuple-element.8), channel_id=1, source_target_pairs={{0,24},{8,16},{16,8},{24,0},{1,25},{9,17},{17,9},{25,1},{2,26},{10... | collective-permute-start | bytes 98312 | tf_op jit(solution)/shard_map/ppermute | solution.py:25
  27.9 3.9 %collective-permute-start.11 = (bf16[16,1024]{1,0:T(8,128)(2,1)S(1)}, bf16[16,1024]{1,0:T(8,128)(2,1)S(1)}, u32[]{:S(2)}, u32[]{:S(2)}) collective-permute-start(bf16[16,1024]{1,0:T(8,128)(2,1)S(1)} %get-tuple-element.9), channel_id=1, source_target_pairs={{0,16},{8,24},{16,0},{24,8},{1,17},{9,25},{17,1},{25,9},{2,18},{10... | collective-permute-start | bytes 98312 | tf_op jit(solution)/shard_map/ppermute | solution.py:25
  31.9 9.8 %collective-permute-start.19 = (bf16[2,1024]{1,0:T(2,128)(2,1)S(1)}, bf16[2,1024]{1,0:T(2,128)(2,1)S(1)}, u32[]{:S(2)}, u32[]{:S(2)}) collective-permute-start(bf16[2,1024]{1,0:T(2,128)(2,1)S(1)} %get-tuple-element.18), channel_id=1, source_target_pairs={{0,7},{1,6},{2,5},{3,4},{4,3},{5,2},{6,1},{7,0},{8,15},{9,14},{10,... | collective-permute-start | bytes 12296 | tf_op jit(solution)/shard_map/ppermute | solution.py:25
  35.5 6.9 %collective-permute-start.18 = (bf16[2,1024]{1,0:T(2,128)(2,1)S(1)}, bf16[2,1024]{1,0:T(2,128)(2,1)S(1)}, u32[]{:S(2)}, u32[]{:S(2)}) collective-permute-start(bf16[2,1024]{1,0:T(2,128)(2,1)S(1)} %get-tuple-element.19), channel_id=1, source_target_pairs={{0,6},{1,7},{2,4},{3,5},{4,2},{5,3},{6,0},{7,1},{8,14},{9,15},{10,... | collective-permute-start | bytes 12296 | tf_op jit(solution)/shard_map/ppermute | solution.py:25
  36.5 7.5 %collective-permute-start.17 = (bf16[2,1024]{1,0:T(2,128)(2,1)S(1)}, bf16[2,1024]{1,0:T(2,128)(2,1)S(1)}, u32[]{:S(2)}, u32[]{:S(2)}) collective-permute-start(bf16[2,1024]{1,0:T(2,128)(2,1)S(1)} %get-tuple-element.20), channel_id=1, source_target_pairs={{0,5},{1,4},{2,7},{3,6},{4,1},{5,0},{6,3},{7,2},{8,13},{9,12},{10,... | collective-permute-start | bytes 12296 | tf_op jit(solution)/shard_map/ppermute | solution.py:25
  37.9 6.2 %collective-permute-start.16 = (bf16[2,1024]{1,0:T(2,128)(2,1)S(1)}, bf16[2,1024]{1,0:T(2,128)(2,1)S(1)}, u32[]{:S(2)}, u32[]{:S(2)}) collective-permute-start(bf16[2,1024]{1,0:T(2,128)(2,1)S(1)} %get-tuple-element.21), channel_id=1, source_target_pairs={{0,4},{1,5},{2,6},{3,7},{4,0},{5,1},{6,2},{7,3},{8,12},{9,13},{10,... | collective-permute-start | bytes 12296 | tf_op jit(solution)/shard_map/ppermute | solution.py:25
  40.4 4.5 %collective-permute-start.15 = (bf16[2,1024]{1,0:T(2,128)(2,1)S(1)}, bf16[2,1024]{1,0:T(2,128)(2,1)S(1)}, u32[]{:S(2)}, u32[]{:S(2)}) collective-permute-start(bf16[2,1024]{1,0:T(2,128)(2,1)S(1)} %get-tuple-element.22), channel_id=1, source_target_pairs={{0,3},{1,2},{2,1},{3,0},{4,7},{5,6},{6,5},{7,4},{8,11},{9,10},{10,... | collective-permute-start | bytes 12296 | tf_op jit(solution)/shard_map/ppermute | solution.py:25
  41.7 3.6 %collective-permute-start.14 = (bf16[2,1024]{1,0:T(2,128)(2,1)S(1)}, bf16[2,1024]{1,0:T(2,128)(2,1)S(1)}, u32[]{:S(2)}, u32[]{:S(2)}) collective-permute-start(bf16[2,1024]{1,0:T(2,128)(2,1)S(1)} %get-tuple-element.23), channel_id=1, source_target_pairs={{0,2},{1,3},{2,0},{3,1},{4,6},{5,7},{6,4},{7,5},{8,10},{9,11},{10,... | collective-permute-start | bytes 12296 | tf_op jit(solution)/shard_map/ppermute | solution.py:25
  42.3 3.6 %collective-permute-start.13 = (bf16[2,1024]{1,0:T(2,128)(2,1)S(1)}, bf16[2,1024]{1,0:T(2,128)(2,1)S(1)}, u32[]{:S(2)}, u32[]{:S(2)}) collective-permute-start(bf16[2,1024]{1,0:T(2,128)(2,1)S(1)} %get-tuple-element.24), channel_id=1, source_target_pairs={{0,1},{1,0},{2,3},{3,2},{4,5},{5,4},{6,7},{7,6},{8,9},{9,8},{10,11... | collective-permute-start | bytes 12296 | tf_op jit(solution)/shard_map/ppermute | solution.py:25
  51.5 7.6 %collective-permute-start.20 = (bf16[2,1152]{1,0:T(2,128)(2,1)S(1)}, bf16[2,1152]{1,0:T(2,128)(2,1)S(1)}, u32[]{:S(2)}, u32[]{:S(2)}) collective-permute-start(bf16[2,1152]{1,0:T(2,128)(2,1)S(1)} %bitcast.84), channel_id=1, source_target_pairs={{0,1},{1,0},{2,3},{3,2},{4,5},{5,4},{6,7},{7,6},{8,9},{9,8},{10,11... | collective-permute-start | bytes 13832 | tf_op jit(solution)/shard_map/ppermute | solution.py:25
  53.1 9.6 %collective-permute-start.21 = (bf16[2,1152]{1,0:T(2,128)(2,1)S(1)}, bf16[2,1152]{1,0:T(2,128)(2,1)S(1)}, u32[]{:S(2)}, u32[]{:S(2)}) collective-permute-start(bf16[2,1152]{1,0:T(2,128)(2,1)S(1)} %bitcast.83), channel_id=1, source_target_pairs={{0,2},{1,3},{2,0},{3,1},{4,6},{5,7},{6,4},{7,5},{8,10},{9,11},{10,... | collective-permute-start | bytes 13832 | tf_op jit(solution)/shard_map/ppermute | solution.py:25
  54.4 8.5 %collective-permute-start.22 = (bf16[2,1152]{1,0:T(2,128)(2,1)S(1)}, bf16[2,1152]{1,0:T(2,128)(2,1)S(1)}, u32[]{:S(2)}, u32[]{:S(2)}) collective-permute-start(bf16[2,1152]{1,0:T(2,128)(2,1)S(1)} %bitcast.85), channel_id=1, source_target_pairs={{0,3},{1,2},{2,1},{3,0},{4,7},{5,6},{6,5},{7,4},{8,11},{9,10},{10,... | collective-permute-start | bytes 13832 | tf_op jit(solution)/shard_map/ppermute | solution.py:25
  55.2 7.7 %collective-permute-start.23 = (bf16[2,1152]{1,0:T(2,128)(2,1)S(1)}, bf16[2,1152]{1,0:T(2,128)(2,1)S(1)}, u32[]{:S(2)}, u32[]{:S(2)}) collective-permute-start(bf16[2,1152]{1,0:T(2,128)(2,1)S(1)} %bitcast.82), channel_id=1, source_target_pairs={{0,4},{1,5},{2,6},{3,7},{4,0},{5,1},{6,2},{7,3},{8,12},{9,13},{10,... | collective-permute-start | bytes 13832 | tf_op jit(solution)/shard_map/ppermute | solution.py:25
  57.5 5.4 %collective-permute-start.24 = (bf16[2,1152]{1,0:T(2,128)(2,1)S(1)}, bf16[2,1152]{1,0:T(2,128)(2,1)S(1)}, u32[]{:S(2)}, u32[]{:S(2)}) collective-permute-start(bf16[2,1152]{1,0:T(2,128)(2,1)S(1)} %bitcast.81), channel_id=1, source_target_pairs={{0,5},{1,4},{2,7},{3,6},{4,1},{5,0},{6,3},{7,2},{8,13},{9,12},{10,... | collective-permute-start | bytes 13832 | tf_op jit(solution)/shard_map/ppermute | solution.py:25
  59.1 5.4 %collective-permute-start.25 = (bf16[2,1152]{1,0:T(2,128)(2,1)S(1)}, bf16[2,1152]{1,0:T(2,128)(2,1)S(1)}, u32[]{:S(2)}, u32[]{:S(2)}) collective-permute-start(bf16[2,1152]{1,0:T(2,128)(2,1)S(1)} %bitcast.80), channel_id=1, source_target_pairs={{0,6},{1,7},{2,4},{3,5},{4,2},{5,3},{6,0},{7,1},{8,14},{9,15},{10,... | collective-permute-start | bytes 13832 | tf_op jit(solution)/shard_map/ppermute | solution.py:25
  62.7 6.3 %collective-permute-start.26 = (bf16[2,1152]{1,0:T(2,128)(2,1)S(1)}, bf16[2,1152]{1,0:T(2,128)(2,1)S(1)}, u32[]{:S(2)}, u32[]{:S(2)}) collective-permute-start(bf16[2,1152]{1,0:T(2,128)(2,1)S(1)} %bitcast.79), channel_id=1, source_target_pairs={{0,7},{1,6},{2,5},{3,4},{4,3},{5,2},{6,1},{7,0},{8,15},{9,14},{10,... | collective-permute-start | bytes 13832 | tf_op jit(solution)/shard_map/ppermute | solution.py:25
  69.1 3.4 %collective-permute-start.29 = (bf16[16,1152]{1,0:T(8,128)(2,1)S(1)}, bf16[16,1152]{1,0:T(8,128)(2,1)S(1)}, u32[]{:S(2)}, u32[]{:S(2)}) collective-permute-start(bf16[16,1152]{1,0:T(8,128)(2,1)S(1)} %concatenate.32), channel_id=1, source_target_pairs={{0,24},{8,16},{16,8},{24,0},{1,25},{9,17},{17,9},{25,1},{2,26},{10... | collective-permute-start | bytes 110600 | tf_op jit(solution)/shard_map/ppermute | solution.py:25
  69.2 4.2 %collective-permute-start.28 = (bf16[16,1152]{1,0:T(8,128)(2,1)S(1)}, bf16[16,1152]{1,0:T(8,128)(2,1)S(1)}, u32[]{:S(2)}, u32[]{:S(2)}) collective-permute-start(bf16[16,1152]{1,0:T(8,128)(2,1)S(1)} %concatenate.32), channel_id=1, source_target_pairs={{0,16},{8,24},{16,0},{24,8},{1,17},{9,25},{17,1},{25,9},{2,18},{10... | collective-permute-start | bytes 110600 | tf_op jit(solution)/shard_map/ppermute | solution.py:25
  69.8 3.5 %collective-permute-start.27 = (bf16[16,1152]{1,0:T(8,128)(2,1)S(1)}, bf16[16,1152]{1,0:T(8,128)(2,1)S(1)}, u32[]{:S(2)}, u32[]{:S(2)}) collective-permute-start(bf16[16,1152]{1,0:T(8,128)(2,1)S(1)} %concatenate.32), channel_id=1, source_target_pairs={{0,8},{8,0},{16,24},{24,16},{1,9},{9,1},{17,25},{25,17},{2,10},{10... | collective-permute-start | bytes 110600 | tf_op jit(solution)/shard_map/ppermute | solution.py:25
  (3 other events, 62.3 us)

commit v4 on v1

v4 whole, which is shorter than its diff:
```python
import functools

import jax
import jax.numpy as jnp
from jax import lax
from jax.experimental import pallas as pl
from jax.experimental.pallas import tpu as pltpu
from jax.sharding import PartitionSpec as P

BOTH = ("dp", "expert")
LANES = 128
TILE = 256
GELU_C = 0.7978845608028654
GELU_A = 0.044715
VMEM_LIMIT = 40 * 1024 * 1024


def gelu_tanh(value):
    return jax.nn.gelu(value, approximate=True)


def gelu_slope(value):
    square = value * value
    bend = jnp.tanh(GELU_C * (value + GELU_A * value * square))
    inner = GELU_C * (1.0 + 3.0 * GELU_A * square)
    return 0.5 * (1.0 + bend) + 0.5 * value * (1.0 - bend * bend) * inner


def pieces_of(value):
    high = value.astype(jnp.bfloat16)
    rest = value - high.astype(jnp.float32)
    middle = rest.astype(jnp.bfloat16)
    low = (rest - middle.astype(jnp.float32)).astype(jnp.bfloat16)
    return high, middle, low


def dot(left, right, over):
    return lax.dot_general(
        left, right, ((over[:1], over[1:]), ((), ())), preferred_element_type=jnp.float32
    )


def steps(count, flat, body):
    if flat:
        for step in range(count):
            body(step)
    else:
        lax.fori_loop(0, count, lambda step, none: (body(step), none)[1], None)


def span(step, size):
    return pl.ds(pl.multiple_of(step * size, size), size)


def params():
    return pltpu.CompilerParams(vmem_limit_bytes=VMEM_LIMIT)


def cost(flops, moved):
    return pl.CostEstimate(flops=flops, bytes_accessed=moved, transcendentals=0)


def spread_kernel(row_ref, out_ref):
    for step in range(out_ref.shape[0]):
        out_ref[step] = row_ref[...]


def spread(value, devices):
    return pl.pallas_call(
        spread_kernel,
        out_shape=jax.ShapeDtypeStruct((devices, *value.shape), value.dtype),
        compiler_params=params(),
        name="spread",
    )(value)


def fetch_kernel(*refs):
    count = (len(refs) - 1) // 2
    sems = refs[-1]
    copies = [
        pltpu.make_async_copy(refs[at], refs[count + at], sems.at[at]) for at in range(count)
    ]
    for copy in copies:
        copy.start()
    for copy in copies:
        copy.wait()


def fetch(*arrays):
    moved = sum(array.size * array.dtype.itemsize for array in arrays)
    return pl.pallas_call(
        fetch_kernel,
        in_specs=[pl.BlockSpec(memory_space=pl.ANY)] * len(arrays),
        out_specs=[pl.BlockSpec(memory_space=pltpu.VMEM)] * len(arrays),
        out_shape=[pltpu.VMEM(array.shape, array.dtype) for array in arrays],
        scratch_shapes=[pltpu.SemaphoreType.DMA((len(arrays),))],
        compiler_params=params(),
        cost_estimate=cost(0, 2 * moved),
        name="fetch",
    )(*(pltpu.with_memory_space_constraint(array, pltpu.HBM) for array in arrays))


def forward_kernel(own, every_ref, first_ref, second_ref, part_ref, pre_ref, hidden_ref):
    rows = every_ref.shape[0]
    chunk = min(rows, 64)

    def body(step):
        here = span(step, chunk)
        pre = dot(every_ref[here, :], first_ref[...], (1, 0))
        hidden = gelu_tanh(pre).astype(jnp.bfloat16)
        part = dot(hidden, second_ref[...], (1, 0)).astype(jnp.bfloat16)
        for at in range(chunk // own):
            part_ref[step * (chunk // own) + at] = part[at * own : (at + 1) * own]
        pre_ref[here, :] = pre
        hidden_ref[here, :] = hidden

    steps(rows // chunk, rows == chunk, body)


def forward(every, first, second, own):
    rows, width = every.shape
    units = first.shape[1]
    return pl.pallas_call(
        functools.partial(forward_kernel, own),
        out_shape=[
            jax.ShapeDtypeStruct((rows // own, own, width), jnp.bfloat16),
            pltpu.VMEM((rows, units), jnp.float32),
            pltpu.VMEM((rows, units), jnp.bfloat16),
        ],
        compiler_params=params(),
        cost_estimate=cost(4 * rows * width * units, 4 * width * units),
        name="forward",
    )(every, first, second)


def backward_kernel(
    tasks,
    arrived_ref,
    every_ref,
    hidden_ref,
    pre_ref,
    second_ref,
    grad_first_ref,
    grad_second_ref,
    grad_gate_ref,
    dpre_ref,
    first_buf,
    second_buf,
    sems,
):
    rows, width = every_ref.shape
    units = hidden_ref.shape[1]
    flat = rows <= 64
    across, down = units // TILE, width // TILE

    def second_copy(step):
        here = span(step, TILE)
        return pltpu.make_async_copy(
            second_buf.at[here, :], grad_second_ref.at[here, :], sems.at[step]
        )

    def first_copy(step):
        here = span(step, TILE)
        return pltpu.make_async_copy(
            first_buf.at[here, :], grad_first_ref.at[here, :], sems.at[across + step]
        )

    def second_step(step):
        here = span(step, TILE)
        second_buf[here, :] = dot(
            hidden_ref[:, here], arrived_ref[:, :width], (0, 0)
        ).astype(jnp.bfloat16)
        second_copy(step).start()

    def dpre_step(step):
        here = span(step, TILE)
        dhidden = dot(arrived_ref[:, :width], second_ref[here, :], (1, 1))
        dpre_ref[:, here] = (gelu_slope(pre_ref[:, here]) * dhidden).astype(jnp.bfloat16)

    def first_step(step):
        here = span(step, TILE)
        first_buf[here, :] = dot(every_ref[:, here], dpre_ref[...], (0, 0)).astype(jnp.bfloat16)
        first_copy(step).start()

    steps(across, flat, second_step)
    steps(across, flat, dpre_step)
    steps(down, flat, first_step)
    gate = dot(arrived_ref[:, width:], every_ref[...], (0, 0))
    total = gate[:tasks] + gate[tasks : 2 * tasks] + gate[2 * tasks : 3 * tasks]
    for task in range(tasks):
        grad_gate_ref[task] = total[task : task + 1]
    steps(across, flat, lambda step: second_copy(step).wait())
    steps(down, flat, lambda step: first_copy(step).wait())


def backward(arrived, every, hidden, pre, second, tasks):
    rows, width = every.shape
    units = hidden.shape[1]
    anywhere = pl.BlockSpec(memory_space=pl.ANY)
    inside = pl.BlockSpec(memory_space=pltpu.VMEM)
    return pl.pallas_call(
        functools.partial(backward_kernel, tasks),
        out_shape=[
            jax.ShapeDtypeStruct((width, units), jnp.bfloat16),
            jax.ShapeDtypeStruct((units, width), jnp.bfloat16),
            jax.ShapeDtypeStruct((tasks, 1, width), jnp.float32),
        ],
        in_specs=[inside] * 5,
        out_specs=[anywhere, anywhere, inside],
        scratch_shapes=[
            pltpu.VMEM((rows, units), jnp.bfloat16),
            pltpu.VMEM((width, units), jnp.bfloat16),
            pltpu.VMEM((units, width), jnp.bfloat16),
            pltpu.SemaphoreType.DMA((units // TILE + width // TILE,)),
        ],
        compiler_params=params(),
        cost_estimate=cost(6 * rows * width * units, 6 * width * units),
        name="backward",
    )(arrived, every, hidden, pre, second)


def per_device(
    events, labels, w_in, w_out, gate_weight, tower_in, tower_bias, tower_out, tower_out_bias
):
    dp = lax.axis_size("dp")
    experts = lax.axis_size("expert")
    devices = dp * experts
    own, width = events.shape
    tasks = tower_in.shape[0]
    rows = devices * own

    gate_logits = jnp.einsum(
        "rd,tde->tre", events, gate_weight, preferred_element_type=jnp.float32
    )
    probs = jax.nn.softmax(gate_logits, axis=-1)

    every = lax.all_to_all(spread(events, devices), BOTH, 0, 0, tiled=True).reshape(rows, width)
    first, second, tower_in = fetch(w_in[0], w_out[0], tower_in)
    part, pre, hidden = forward(every, first, second, own)

    parts = lax.all_to_all(part, BOTH, 0, 0, tiled=True)
    parts = parts.reshape(dp, experts, own, width).astype(jnp.float32)
    outs = jnp.sum(parts, 0).astype(jnp.bfloat16)
    outs_wide = outs.astype(jnp.float32)
    mixed = jnp.sum(
        jnp.transpose(probs, (0, 2, 1))[..., None] * outs_wide[None], 1
    ).astype(jnp.bfloat16)
    tower_pre = (
        jnp.einsum("trd,tdk->trk", mixed, tower_in, preferred_element_type=jnp.float32)
        + tower_bias[:, None, :]
    )
    active, gelu_back = jax.vjp(gelu_tanh, tower_pre)
    logit = jnp.sum(active * tower_out[:, None, :], -1) + tower_out_bias[:, None]
    dlogit = jax.nn.sigmoid(logit) - labels.T.astype(jnp.float32)
    dtower = gelu_back(dlogit[..., None] * tower_out[:, None, :])[0]
    stacked = jnp.concatenate(pieces_of(dtower), 1)
    dmixed = jnp.einsum("trk,tdk->trd", stacked, tower_in, preferred_element_type=jnp.float32)
    dmixed = jnp.sum(dmixed.reshape(tasks, 3, own, width), 1).astype(jnp.bfloat16)
    dmixed_wide = dmixed.astype(jnp.float32)
    dprob = jnp.sum(dmixed_wide[:, None] * outs_wide[None], -1)
    probs_ter = jnp.transpose(probs, (0, 2, 1))
    dgate = probs_ter * (dprob - jnp.sum(probs_ter * dprob, 1, keepdims=True))
    dexpert = jnp.sum(probs_ter[..., None] * dmixed_wide[:, None], 0).astype(jnp.bfloat16)

    packed = jnp.transpose(jnp.concatenate(pieces_of(dgate), 0), (1, 2, 0))
    packed = jnp.pad(packed, ((0, 0), (0, 0), (0, LANES - 3 * tasks)))
    message = jnp.concatenate([dexpert, packed], -1)
    message = jnp.broadcast_to(message[None], (dp, experts, own, width + LANES))
    message = message.reshape(devices, own, width + LANES)
    arrived = lax.all_to_all(message, BOTH, 0, 0, tiled=True).reshape(rows, width + LANES)
    grad_first, grad_second, grad_gate = backward(arrived, every, hidden, pre, second, tasks)
    return (grad_first[None], grad_second[None], jnp.transpose(grad_gate, (0, 2, 1)))


def solution(mesh):
    placed = (
        P(BOTH, None),
        P(BOTH, None),
        P("expert", None, "dp"),
        P("expert", "dp", None),
        P(),
        P(),
        P(),
        P(),
        P(),
    )
    return jax.shard_map(
        per_device,
        mesh=mesh,
        in_specs=placed,
        out_specs=(P("expert", None, "dp"), P("expert", "dp", None), P(None, None, "expert")),
        check_vma=False,
    )
```

time: 57.9 us -> 51.7 us (0.89)
  waiting for transfers between devices: 21.7 us -> 9.25 us
  blocking collectives: 0 us -> 10.1 us
  Pallas kernels: 0 us -> 8.6 us
  matrix products: 12.9 us -> 4.53 us
  local copies, waits for them, and re-layouts: 8.36 us -> 5.66 us
  starting transfers between devices: 12.4 us -> 11.3 us
    all_to_all x3 -> x2, waiting for transfers between devices: 21.7 us -> 9.25 us  [the longest x1 7.39 us: per_device(): parts = lax.all_to_all(part, BOTH, 0, 0, tiled=True)]
    all_to_all x0 -> x1, blocking collectives: none -> 10.1 us  [per_device(): lax.all_to_all(message, BOTH, 0, 0, tiled=True).reshape(rows, width + LANES)]
    pallas_call x0 -> x4, Pallas kernels: none -> 8.6 us  [the longest x1 3.51 us: backward(): pl.pallas_call(functools.partial(backward_kernel, tasks), out_shape=[jax....]
    dot_general x5 -> x0, matrix products: 7.54 us -> none  [the longest x1 2.77 us: per_device(): lax.dot_general(every, dpre, (((0,), (0,)), ((), ())), preferred_element_...]
    broadcast_in_dim x3 -> x1, local copies, waits for them, and re-layouts: 2.92 us -> 0.08 us  [per_device(): message = jnp.broadcast_to(message[None], (dp, experts, own, width + LANES))]
    all_to_all x3 -> x2, starting transfers between devices: 12.4 us -> 11.3 us  [the longest x1 7.3 us: per_device(): lax.all_to_all(spread(events, devices), BOTH, 0, 0, tiled=True)]
    unnamed x14 -> x23, local copies, waits for them, and re-layouts: 4.26 us -> 5.25 us
    dot_general x1, matrix products: 1.17 us -> 0.33 us  [per_device(): jnp.einsum('rd,tde->tre', events, gate_weight, preferred_element_type=jnp...]
  transfers between devices with their start and end apart: 3 -> 2, of which waited for: 3 -> 2; matrix products, arithmetic and copies ran while one was open for 3% -> 1% of each run, Pallas kernels for 0% -> 6%
where the time goes in v4:
time: 51.7 us; the launch traced here: 51.3 us
  starting transfers between devices  11.3 us (22%)
  blocking collectives  10.1 us (20%)
  waiting for transfers between devices  9.25 us (18%)
  Pallas kernels  8.6 us (17%)
  local copies, waits for them, and re-layouts  5.66 us (11%)
  matrix products  4.53 us (9%)
  other arithmetic  1.11 us (2%)
  between operations  0.81 us (2%)
    all_to_all x1, blocking collectives, per_device(): lax.all_to_all(message, BOTH, 0, 0, tiled=True).reshape(rows, width + LANES)  10.1 us
    all_to_all x1, waiting for transfers between devices, per_device(): parts = lax.all_to_all(part, BOTH, 0, 0, tiled=True)  7.39 us
    all_to_all x1, starting transfers between devices, per_device(): lax.all_to_all(spread(events, devices), BOTH, 0, 0, tiled=True)  7.3 us
    unnamed x23, local copies, waits for them, and re-layouts  5.25 us
    all_to_all x1, starting transfers between devices, per_device(): parts = lax.all_to_all(part, BOTH, 0, 0, tiled=True)  4 us
    pallas_call x1, Pallas kernels, backward(): pl.pallas_call(functools.partial(backward_kernel, tasks), out_shape=[jax....  3.51 us
    pallas_call x1, Pallas kernels, fetch(): pl.pallas_call(fetch_kernel, in_specs=[pl.BlockSpec(memory_space=pl.ANY)]...  2.89 us
    dot_general x1, matrix products, per_device(): jnp.einsum('trk,tdk->trd', stacked, tower_in, preferred_element_type=jnp....  2.23 us
  transfers between devices with their start and end apart: 2, of which 2 were waited for; matrix products, arithmetic and copies ran while one was open for 1% of the time, Pallas kernels for 6%

profile of v4, /device:TPU:0, one launch (start us, length us, event | category | flops | bytes accessed | tf_op | source)
XLA Modules:
  0.0 51.3 jit_solution(3054646141338078209)
XLA Ops:
  0.7 0.7 %copy-done.4 = bf16[2,1024]{1,0:T(2,128)(2,1)S(1)} copy-done((bf16[2,1024]{1,0:T(2,128)(2,1)S(1)}, bf16[2,1024]{1,0:T(2,128)(2,1)}, u32[]{:S(2)}) %copy-start.4) | copy-done | bytes 4120
  1.4 0.6 %spread.1 = bf16[32,2,1024]{2,1,0:T(2,128)(2,1)} custom-call(bf16[2,1024]{1,0:T(2,128)(2,1)S(1)} %copy-done.4), custom_call_target="tpu_custom_call" | custom-call | tf_op jit(solution)/shard_map/spread/pallas_call | solution.py:69
  2.0 7.3 %all-to-all-start = ((bf16[32,2,1024]{2,1,0:T(2,128)(2,1)}), bf16[32,2,1024]{2,1,0:T(2,128)(2,1)S(1)}, u32[]{:S(2)}, u32[]{:S(2)}) async-start(bf16[32,2,1024]{2,1,0:T(2,128)(2,1)} %spread.1), calls=%async_computation | async-start | bytes 262144 | tf_op jit(solution)/shard_map/all_to_all | solution.py:237
  9.3 2.9 %fetch.1 = (bf16[1024,1024]{1,0:T(8,128)(2,1)S(1)}, bf16[1024,1024]{1,0:T(8,128)(2,1)S(1)}, bf16[4,1024,256]{2,1,0:T(8,128)(2,1)S(1)}) custom-call(bf16[1024,1024]{1,0:T(8,128)(2,1)} %bitcast.28, bf16[1024,1024]{1,0:T(8,128)(2,1)} %bitcast.29, bf16[4,1024,256]{2,1,0:T(8,128)(2,1)} %refs_2_.1), custom_call_target="tpu_custom_call" | custom-call | bytes 12582912 | tf_op jit(solution)/shard_map/fetch/pallas_call | solution.py:91
  12.2 1.3 %copy-done.1 = bf16[4,1024,256]{2,1,0:T(8,128)(2,1)} copy-done((bf16[4,1024,256]{2,1,0:T(8,128)(2,1)}, bf16[4,1024,256]{2,1,0:T(8,128)(2,1)S(1)}, u32[]{:S(2)}) %copy-start.1) | copy-done | bytes 2097176
  13.6 1.3 %copy-done.2 = bf16[1024,1024]{1,0:T(8,128)(2,1)} copy-done((bf16[1024,1024]{1,0:T(8,128)(2,1)}, bf16[1024,1024]{1,0:T(8,128)(2,1)S(1)}, u32[]{:S(2)}) %copy-start.2) | copy-done | bytes 2097176
  14.9 0.3 bitcast_reduce_fusion
  15.2 1.9 %all-to-all-done = bf16[32,2,1024]{2,1,0:T(2,128)(2,1)S(1)} async-done(((bf16[32,2,1024]{2,1,0:T(2,128)(2,1)}), bf16[32,2,1024]{2,1,0:T(2,128)(2,1)S(1)}, u32[]{:S(2)}, u32[]{:S(2)}) %all-to-all-start) | async-done | bytes 131104 | tf_op jit(solution)/shard_map/all_to_all | solution.py:237
  17.1 1.6 %copy-done.3 = bf16[1024,1024]{1,0:T(8,128)(2,1)S(1)} copy-done((bf16[1024,1024]{1,0:T(8,128)(2,1)S(1)}, bf16[1024,1024]{1,0:T(8,128)(2,1)}, u32[]{:S(2)}) %copy-start.3) | copy-done | bytes 2097176
  18.7 1.6 %forward.1 = (bf16[32,2,1024]{2,1,0:T(2,128)(2,1)}, f32[64,1024]{1,0:T(8,128)S(1)}, bf16[64,1024]{1,0:T(8,128)(2,1)S(1)}) custom-call(bf16[64,1024]{1,0:T(8,128)(2,1)S(1)} %reshape.37.every_ref, bf16[1024,1024]{1,0:T(8,128)(2,1)S(1)} %copy-done.3, bf16[1024,1024]{1,0:T(8,128)(2,1)S(1)} %get-tuple-element.13.second_ref), custom_call_target="tpu_custom_call" | custom-call | flops 268435456 | bytes 4194304 | tf_op jit(solution)/shard_map/forward/pallas_call | solution.py:123
  20.3 4.0 %all-to-all-start.1 = ((bf16[32,2,1024]{2,1,0:T(2,128)(2,1)}), bf16[32,2,1024]{2,1,0:T(2,128)(2,1)S(1)}, u32[]{:S(2)}, u32[]{:S(2)}) async-start(bf16[32,2,1024]{2,1,0:T(2,128)(2,1)} %get-tuple-element.14), calls=%async_computation.1 | async-start | bytes 262144 | tf_op jit(solution)/shard_map/all_to_all | solution.py:241
  24.3 0.2 fusion.20
  24.4 0.1 copy.38
  24.5 0.1 exponential_divide_fusion
  24.6 7.4 %all-to-all-done.1 = bf16[32,2,1024]{2,1,0:T(2,128)(2,1)S(1)} async-done(((bf16[32,2,1024]{2,1,0:T(2,128)(2,1)}), bf16[32,2,1024]{2,1,0:T(2,128)(2,1)S(1)}, u32[]{:S(2)}, u32[]{:S(2)}) %all-to-all-start.1) | async-done | bytes 131104 | tf_op jit(solution)/shard_map/all_to_all | solution.py:241
  32.0 0.1 reduce_sum.76
  32.2 0.2 multiply_reduce_fusion.2
  32.3 2.0 %fusion.28 = f32[4,2,256]{2,1,0:T(2,128)S(1)} fusion(bf16[4,2,1024]{2,1,0:T(2,128)(2,1)S(1)} %multiply_reduce_fusion.2, bf16[4,1024,256]{2,1,0:T(8,128)(2,1)} %copy-done.1), kind=kOutput, calls=%fused_computation.50 | convolution fusion | flops 4194304 | bytes 2121728 | tf_op jit(solution)/shard_map/trd,tdk->trk/dot_general | solution.py:249
  34.3 0.1 multiply_reduce_fusion.3
  34.4 0.1 copy.45
  34.5 0.1 divide_subtract_fusion
  34.6 0.1 copy.39
  34.7 0.1 fusion.25
  34.8 2.2 %fusion.5 = f32[4,6,1024]{2,1,0:T(8,128)S(1)} fusion(bf16[4,1024,256]{2,1,0:T(8,128)(2,1)} %copy-done.1, bf16[4,6,256]{2,0,1:T(4,128)(2,1)S(1)} %pad_maximum_fusion), kind=kOutput, calls=%fused_computation.10 | convolution fusion | flops 12582912 | bytes 2207744 | tf_op jit(solution)/shard_map/trk,tdk->trd/dot_general | solution.py:257
  37.1 0.1 copy.41
  37.2 0.1 multiply_reduce_fusion.1
  37.3 0.1 fusion.27
  37.4 0.1 copy.46
  37.6 0.1 broadcast_in_dim.6
  37.7 10.1 %all_to_all.15 = bf16[32,2,1152]{2,1,0:T(2,128)(2,1)S(1)} all-to-all(bf16[32,2,1152]{2,1,0:T(2,128)(2,1)S(1)} %bitcast.30), channel_id=1, replica_groups=mesh['dp'=4,'expert'=8] {'dp','expert'}, dimensions={0} | all-to-all | bytes 294912 | tf_op jit(solution)/shard_map/all_to_all | solution.py:270
  47.8 0.1 reshape.41.arrived_ref
  47.8 3.5 %backward.1 = (bf16[1024,1024]{1,0:T(8,128)(2,1)}, bf16[1024,1024]{1,0:T(8,128)(2,1)}, f32[4,1,1024]{2,1,0:T(1,128)}) custom-call(bf16[64,1152]{1,0:T(8,128)(2,1)S(1)} %reshape.41.arrived_ref, bf16[64,1024]{1,0:T(8,128)(2,1)S(1)} %reshape.37.every_ref, bf16[64,1024]{1,0:T(8,128)(2,1)S(1)} %get-tuple-element.16.hidden_ref, ...), custom_call_target="tpu_custom_call" | custom-call | flops 402653184 | bytes 6291456 | tf_op jit(solution)/shard_map/backward/pallas_call | solution.py:201
  (25 shorter events, 0.2 us)
Async XLA Ops:
  0.6 14.2 %copy-start = (bf16[4,1024,8]{1,2,0:T(8,128)(2,1)S(1)}, bf16[4,1024,8]{1,2,0:T(8,128)(2,1)}, u32[]{:S(2)}) copy-start(bf16[4,1024,8]{1,2,0:T(8,128)(2,1)} %param.13) | copy-start | bytes 196612
  0.6 0.7 %copy-start.4 = (bf16[2,1024]{1,0:T(2,128)(2,1)S(1)}, bf16[2,1024]{1,0:T(2,128)(2,1)}, u32[]{:S(2)}) copy-start(bf16[2,1024]{1,0:T(2,128)(2,1)} %row_ref.1) | copy-start | bytes 12292
  2.0 15.0 %all-to-all-start = ((bf16[32,2,1024]{2,1,0:T(2,128)(2,1)}), bf16[32,2,1024]{2,1,0:T(2,128)(2,1)S(1)}, u32[]{:S(2)}, u32[]{:S(2)}) async-start(bf16[32,2,1024]{2,1,0:T(2,128)(2,1)} %spread.1), calls=%async_computation | async-start | bytes 262144 | tf_op jit(solution)/shard_map/all_to_all | solution.py:237
  9.3 5.6 %copy-start.5 = (bf16[2,1024]{1,0:T(2,128)(2,1)S(1)}, bf16[2,1024]{1,0:T(2,128)(2,1)}, u32[]{:S(2)}) copy-start(bf16[2,1024]{1,0:T(2,128)(2,1)} %row_ref.1) | copy-start | bytes 12292
  12.2 1.3 %copy-start.1 = (bf16[4,1024,256]{2,1,0:T(8,128)(2,1)}, bf16[4,1024,256]{2,1,0:T(8,128)(2,1)S(1)}, u32[]{:S(2)}) copy-start(bf16[4,1024,256]{2,1,0:T(8,128)(2,1)S(1)} %get-tuple-element.15) | copy-start | bytes 6291460
  13.6 1.3 %copy-start.2 = (bf16[1024,1024]{1,0:T(8,128)(2,1)}, bf16[1024,1024]{1,0:T(8,128)(2,1)S(1)}, u32[]{:S(2)}) copy-start(bf16[1024,1024]{1,0:T(8,128)(2,1)S(1)} %get-tuple-element.12.first_ref) | copy-start | bytes 6291460
  17.1 1.6 %copy-start.3 = (bf16[1024,1024]{1,0:T(8,128)(2,1)S(1)}, bf16[1024,1024]{1,0:T(8,128)(2,1)}, u32[]{:S(2)}) copy-start(bf16[1024,1024]{1,0:T(8,128)(2,1)} %copy-done.2) | copy-start | bytes 6291460
  18.7 5.7 %copy-start.8 = (s32[2,4]{1,0:T(2,128)S(1)}, s32[2,4]{1,0:T(2,128)}, u32[]{:S(2)}) copy-start(s32[2,4]{1,0:T(2,128)} %param.10) | copy-start | bytes 100
  20.3 14.0 %copy-start.6 = (f32[4,256]{1,0:T(4,128)S(1)}, f32[4,256]{1,0:T(4,128)}, u32[]{:S(2)}) copy-start(f32[4,256]{1,0:T(4,128)} %param.15) | copy-start | bytes 12292
  20.3 14.0 %copy-start.7 = (f32[4,256]{1,0:T(4,128)S(1)}, f32[4,256]{1,0:T(4,128)}, u32[]{:S(2)}) copy-start(f32[4,256]{1,0:T(4,128)} %param.16) | copy-start | bytes 12292
  20.3 14.2 %copy-start.9 = (f32[4]{0:T(128)S(1)}, f32[4]{0:T(128)}, u32[]{:S(2)}) copy-start(f32[4]{0:T(128)} %param.17) | copy-start | bytes 52
  20.3 11.7 %all-to-all-start.1 = ((bf16[32,2,1024]{2,1,0:T(2,128)(2,1)}), bf16[32,2,1024]{2,1,0:T(2,128)(2,1)S(1)}, u32[]{:S(2)}, u32[]{:S(2)}) async-start(bf16[32,2,1024]{2,1,0:T(2,128)(2,1)} %get-tuple-element.14), calls=%async_computation.1 | async-start | bytes 262144 | tf_op jit(solution)/shard_map/all_to_all | solution.py:241

commit v5 on v4

--- a/solution.py
+++ b/solution.py
@@ -60,18 +60,28 @@
     return pl.CostEstimate(flops=flops, bytes_accessed=moved, transcendentals=0)
 
 
-def spread_kernel(row_ref, out_ref):
-    for step in range(out_ref.shape[0]):
-        out_ref[step] = row_ref[...]
+def in_hbm(value):
+    return pltpu.with_memory_space_constraint(value, pltpu.HBM)
+
+
+def spread_kernel(row_ref, out_ref, sem):
+    def body(step):
+        pltpu.make_async_copy(row_ref, out_ref.at[step], sem).start()
+
+    steps(out_ref.shape[0], True, body)
+    pltpu.make_async_copy(out_ref, out_ref, sem).wait()
 
 
 def spread(value, devices):
     return pl.pallas_call(
         spread_kernel,
-        out_shape=jax.ShapeDtypeStruct((devices, *value.shape), value.dtype),
+        in_specs=[pl.BlockSpec(memory_space=pl.ANY)],
+        out_specs=pl.BlockSpec(memory_space=pl.ANY),
+        out_shape=pltpu.HBM((devices, *value.shape), value.dtype),
+        scratch_shapes=[pltpu.SemaphoreType.DMA],
         compiler_params=params(),
         name="spread",
-    )(value)
+    )(in_hbm(value))
 
 
 def fetch_kernel(*refs):
@@ -97,29 +107,50 @@
         compiler_params=params(),
         cost_estimate=cost(0, 2 * moved),
         name="fetch",
-    )(*(pltpu.with_memory_space_constraint(array, pltpu.HBM) for array in arrays))
-
-
-def forward_kernel(own, every_ref, first_ref, second_ref, part_ref, pre_ref, hidden_ref):
+    )(*(in_hbm(array) for array in arrays))
+
+
+def streamed(source, target, sems):
+    def block(step):
+        here = span(step, TILE)
+        return pltpu.make_async_copy(source.at[here, :], target.at[here, :], sems.at[step])
+
+    return block
+
+
+def forward_kernel(
+    own, every_ref, first_ref, second_ref, part_ref, pre_ref, hidden_ref, second_buf, sems
+):
     rows = every_ref.shape[0]
     chunk = min(rows, 64)
+    blocks = second_ref.shape[0] // TILE
+    block = streamed(second_ref, second_buf, sems)
+    for at in range(blocks):
+        block(at).start()
 
     def body(step):
         here = span(step, chunk)
         pre = dot(every_ref[here, :], first_ref[...], (1, 0))
-        hidden = gelu_tanh(pre).astype(jnp.bfloat16)
-        part = dot(hidden, second_ref[...], (1, 0)).astype(jnp.bfloat16)
+        pre_ref[here, :] = pre
+        hidden_ref[here, :] = gelu_tanh(pre).astype(jnp.bfloat16)
+
+    steps(rows // chunk, rows == chunk, body)
+    for at in range(blocks):
+        block(at).wait()
+
+    def finish(step):
+        here = span(step, chunk)
+        part = dot(hidden_ref[here, :], second_buf[...], (1, 0)).astype(jnp.bfloat16)
         for at in range(chunk // own):
             part_ref[step * (chunk // own) + at] = part[at * own : (at + 1) * own]
-        pre_ref[here, :] = pre
-        hidden_ref[here, :] = hidden
-
-    steps(rows // chunk, rows == chunk, body)
+
+    steps(rows // chunk, rows == chunk, finish)
 
 
 def forward(every, first, second, own):
     rows, width = every.shape
     units = first.shape[1]
+    inside = pl.BlockSpec(memory_space=pltpu.VMEM)
     return pl.pallas_call(
         functools.partial(forward_kernel, own),
         out_shape=[
@@ -127,14 +158,95 @@
             pltpu.VMEM((rows, units), jnp.float32),
             pltpu.VMEM((rows, units), jnp.bfloat16),
         ],
+        in_specs=[inside, inside, pl.BlockSpec(memory_space=pl.ANY)],
+        out_specs=[inside] * 3,
+        scratch_shapes=[
+            pltpu.VMEM(second.shape, second.dtype),
+            pltpu.SemaphoreType.DMA((units // TILE,)),
+        ],
         compiler_params=params(),
         cost_estimate=cost(4 * rows * width * units, 4 * width * units),
         name="forward",
-    )(every, first, second)
+    )(every, first, in_hbm(second))
+
+
+def middle_kernel(
+    shape,
+    parts_ref,
+    probs_ref,
+    tower_in_ref,
+    bias_ref,
+    weight_ref,
+    shift_ref,
+    target_ref,
+    message_ref,
+):
+    dp, experts, own = shape
+    tasks = tower_in_ref.shape[0]
+    width = parts_ref.shape[1]
+    slots = experts * own
+    rows = tasks * own
+    total = parts_ref[:slots, :].astype(jnp.float32)
+    for at in range(1, dp):
+        total = total + parts_ref[at * slots : (at + 1) * slots, :].astype(jnp.float32)
+    outs = total.astype(jnp.bfloat16)
+    probs = probs_ref[...]
+    share = jnp.concatenate([piece.astype(jnp.float32) for piece in pieces_of(probs)], 0)
+    share = share.astype(jnp.bfloat16)
+
+    def fold(value):
+        return value[:rows] + value[rows : 2 * rows] + value[2 * rows :]
+
+    def only(value, task):
+        at = lax.broadcasted_iota(jnp.int32, value.shape, 0)
+        return jnp.where(lax.rem(at, rows) // own == task, value, 0.0).astype(jnp.bfloat16)
+
+    mixed = fold(dot(share, outs, (1, 0))).astype(jnp.bfloat16).astype(jnp.float32)
+    tower = bias_ref[...]
+    for task in range(tasks):
+        tower = tower + dot(only(mixed, task), tower_in_ref[task], (1, 0))
+    weight = weight_ref[...]
+    logit = jnp.sum(gelu_tanh(tower) * weight, -1, keepdims=True) + shift_ref[...]
+    dlogit = jax.nn.sigmoid(logit) - target_ref[...]
+    dtower = gelu_slope(tower) * (dlogit * weight)
+    stack = jnp.concatenate([piece.astype(jnp.float32) for piece in pieces_of(dtower)], 0)
+    wide = dot(only(stack, 0), tower_in_ref[0], (1, 1))
+    for task in range(1, tasks):
+        wide = wide + dot(only(stack, task), tower_in_ref[task], (1, 1))
+    dmixed = fold(wide).astype(jnp.bfloat16)
+    dprob = dot(dmixed, outs, (1, 1))
+    dgate = probs * (dprob - jnp.sum(probs * dprob, -1, keepdims=True))
+    twice = dmixed.astype(jnp.float32)
+    twice = jnp.concatenate([twice, twice, twice], 0).astype(jnp.bfloat16)
+    dexpert = dot(share, twice, (0, 0)).astype(jnp.bfloat16)
+    lanes = jnp.concatenate([piece.astype(jnp.float32) for piece in pieces_of(dgate)], 0)
+    unit = lax.broadcasted_iota(jnp.int32, (3 * rows, LANES), 0) == lax.broadcasted_iota(
+        jnp.int32, (3 * rows, LANES), 1
+    )
+    lanes = dot(lanes.astype(jnp.bfloat16), unit.astype(jnp.bfloat16), (0, 0))
+    lanes = lanes.astype(jnp.bfloat16)
+    for expert in range(experts):
+        here = slice(expert * own, (expert + 1) * own)
+        for at in range(dp):
+            message_ref[at * experts + expert, :, :width] = dexpert[here]
+            message_ref[at * experts + expert, :, width:] = lanes[here]
+
+
+def middle(shape, parts, probs, tower_in, bias, weight, shift, target):
+    dp, experts, own = shape
+    width = parts.shape[1]
+    return pl.pallas_call(
+        functools.partial(middle_kernel, shape),
+        out_shape=jax.ShapeDtypeStruct((dp * experts, own, width + LANES), jnp.bfloat16),
+        compiler_params=params(),
+        cost_estimate=cost(4 * 8 * tower_in.size, 2 * tower_in.size),
+        name="middle",
+    )(parts, probs, tower_in, bias, weight, shift, target)
 
 
 def backward_kernel(
     tasks,
+    own,
     arrived_ref,
     every_ref,
     hidden_ref,
@@ -146,12 +258,17 @@
     dpre_ref,
     first_buf,
     second_buf,
+    weight_buf,
     sems,
+    weight_sems,
 ):
     rows, width = every_ref.shape
     units = hidden_ref.shape[1]
     flat = rows <= 64
     across, down = units // TILE, width // TILE
+    block = streamed(second_ref, weight_buf, weight_sems)
+    for at in range(across):
+        block(at).start()
 
     def second_copy(step):
         here = span(step, TILE)
@@ -174,7 +291,8 @@
 
     def dpre_step(step):
         here = span(step, TILE)
-        dhidden = dot(arrived_ref[:, :width], second_ref[here, :], (1, 1))
+        block(step).wait()
+        dhidden = dot(arrived_ref[:, :width], weight_buf[here, :], (1, 1))
         dpre_ref[:, here] = (gelu_slope(pre_ref[:, here]) * dhidden).astype(jnp.bfloat16)
 
     def first_step(step):
@@ -186,37 +304,39 @@
     steps(across, flat, dpre_step)
     steps(down, flat, first_step)
     gate = dot(arrived_ref[:, width:], every_ref[...], (0, 0))
-    total = gate[:tasks] + gate[tasks : 2 * tasks] + gate[2 * tasks : 3 * tasks]
     for task in range(tasks):
-        grad_gate_ref[task] = total[task : task + 1]
+        lanes = [(at * tasks + task) * own + row for at in range(3) for row in range(own)]
+        grad_gate_ref[task] = sum(gate[lane : lane + 1] for lane in lanes)
     steps(across, flat, lambda step: second_copy(step).wait())
     steps(down, flat, lambda step: first_copy(step).wait())
 
 
-def backward(arrived, every, hidden, pre, second, tasks):
+def backward(arrived, every, hidden, pre, second, tasks, own):
     rows, width = every.shape
     units = hidden.shape[1]
     anywhere = pl.BlockSpec(memory_space=pl.ANY)
     inside = pl.BlockSpec(memory_space=pltpu.VMEM)
     return pl.pallas_call(
-        functools.partial(backward_kernel, tasks),
+        functools.partial(backward_kernel, tasks, own),
         out_shape=[
             jax.ShapeDtypeStruct((width, units), jnp.bfloat16),
             jax.ShapeDtypeStruct((units, width), jnp.bfloat16),
             jax.ShapeDtypeStruct((tasks, 1, width), jnp.float32),
         ],
-        in_specs=[inside] * 5,
+        in_specs=[inside] * 4 + [anywhere],
         out_specs=[anywhere, anywhere, inside],
         scratch_shapes=[
             pltpu.VMEM((rows, units), jnp.bfloat16),
             pltpu.VMEM((width, units), jnp.bfloat16),
             pltpu.VMEM((units, width), jnp.bfloat16),
+            pltpu.VMEM((units, width), jnp.bfloat16),
             pltpu.SemaphoreType.DMA((units // TILE + width // TILE,)),
+            pltpu.SemaphoreType.DMA((units // TILE,)),
         ],
         compiler_params=params(),
         cost_estimate=cost(6 * rows * width * units, 6 * width * units),
         name="backward",
-    )(arrived, every, hidden, pre, second)
+    )(arrived, every, hidden, pre, in_hbm(second))
 
 
 def per_device(
@@ -233,42 +353,27 @@
         "rd,tde->tre", events, gate_weight, preferred_element_type=jnp.float32
     )
     probs = jax.nn.softmax(gate_logits, axis=-1)
+    probs = probs[..., None] * jnp.eye(own, dtype=jnp.float32)[None, :, None, :]
+    probs = probs.reshape(tasks * own, experts * own)
+    bias = jnp.repeat(tower_bias, own, 0)
+    weight = jnp.repeat(tower_out, own, 0)
+    shift = jnp.repeat(tower_out_bias, own)[:, None]
+    target = labels.T.astype(jnp.float32).reshape(tasks * own, 1)
 
     every = lax.all_to_all(spread(events, devices), BOTH, 0, 0, tiled=True).reshape(rows, width)
-    first, second, tower_in = fetch(w_in[0], w_out[0], tower_in)
-    part, pre, hidden = forward(every, first, second, own)
-
-    parts = lax.all_to_all(part, BOTH, 0, 0, tiled=True)
-    parts = parts.reshape(dp, experts, own, width).astype(jnp.float32)
-    outs = jnp.sum(parts, 0).astype(jnp.bfloat16)
-    outs_wide = outs.astype(jnp.float32)
-    mixed = jnp.sum(
-        jnp.transpose(probs, (0, 2, 1))[..., None] * outs_wide[None], 1
-    ).astype(jnp.bfloat16)
-    tower_pre = (
-        jnp.einsum("trd,tdk->trk", mixed, tower_in, preferred_element_type=jnp.float32)
-        + tower_bias[:, None, :]
-    )
-    active, gelu_back = jax.vjp(gelu_tanh, tower_pre)
-    logit = jnp.sum(active * tower_out[:, None, :], -1) + tower_out_bias[:, None]
-    dlogit = jax.nn.sigmoid(logit) - labels.T.astype(jnp.float32)
-    dtower = gelu_back(dlogit[..., None] * tower_out[:, None, :])[0]
-    stacked = jnp.concatenate(pieces_of(dtower), 1)
-    dmixed = jnp.einsum("trk,tdk->trd", stacked, tower_in, preferred_element_type=jnp.float32)
-    dmixed = jnp.sum(dmixed.reshape(tasks, 3, own, width), 1).astype(jnp.bfloat16)
-    dmixed_wide = dmixed.astype(jnp.float32)
-    dprob = jnp.sum(dmixed_wide[:, None] * outs_wide[None], -1)
-    probs_ter = jnp.transpose(probs, (0, 2, 1))
-    dgate = probs_ter * (dprob - jnp.sum(probs_ter * dprob, 1, keepdims=True))
-    dexpert = jnp.sum(probs_ter[..., None] * dmixed_wide[:, None], 0).astype(jnp.bfloat16)
-
-    packed = jnp.transpose(jnp.concatenate(pieces_of(dgate), 0), (1, 2, 0))
-    packed = jnp.pad(packed, ((0, 0), (0, 0), (0, LANES - 3 * tasks)))
-    message = jnp.concatenate([dexpert, packed], -1)
-    message = jnp.broadcast_to(message[None], (dp, experts, own, width + LANES))
-    message = message.reshape(devices, own, width + LANES)
+    (first,) = fetch(w_in[0])
+    part, pre, hidden = forward(every, first, w_out[0], own)
+
+    parts = lax.all_to_all(part, BOTH, 0, 0, tiled=True).reshape(rows, width)
+    (tower_here,) = fetch(tower_in)
+    message = middle(
+        (dp, experts, own), parts, probs, tower_here, bias, weight, shift, target
+    )
+
     arrived = lax.all_to_all(message, BOTH, 0, 0, tiled=True).reshape(rows, width + LANES)
-    grad_first, grad_second, grad_gate = backward(arrived, every, hidden, pre, second, tasks)
+    grad_first, grad_second, grad_gate = backward(
+        arrived, every, hidden, pre, w_out[0], tasks, own
+    )
     return (grad_first[None], grad_second[None], jnp.transpose(grad_gate, (0, 2, 1)))
 
 

time: 51.7 us -> 52.2 us (level)
  Pallas kernels: 8.6 us -> 18.7 us
  local copies, waits for them, and re-layouts: 5.66 us -> 0.62 us
  matrix products: 4.53 us -> 0.42 us
  starting transfers between devices: 11.3 us -> 9.9 us
  waiting for transfers between devices: 9.25 us -> 10.6 us
    pallas_call x2 -> x3, Pallas kernels: 4.15 us -> 12.7 us  [the longest x1 5.39 us: backward(): pl.pallas_call(functools.partial(backward_kernel, tasks, own), out_shape=...]
    unnamed x23 -> x10, local copies, waits for them, and re-layouts: 5.25 us -> 0.03 us
    dot_general x3 -> x0, matrix products: 4.53 us -> none  [the longest x1 2.23 us: per_device(): jnp.einsum('trk,tdk->trd', stacked, tower_in, preferred_element_type=jnp....]
    all_to_all x1, waiting for transfers between devices: 1.85 us -> 4.99 us  [per_device(): lax.all_to_all(spread(events, devices), BOTH, 0, 0, tiled=True)]
    all_to_all x1, waiting for transfers between devices: 7.39 us -> 5.58 us  [per_device(): parts = lax.all_to_all(part, BOTH, 0, 0, tiled=True).reshape(rows, width)]
    all_to_all x1, starting transfers between devices: 4 us -> 2.59 us  [per_device(): parts = lax.all_to_all(part, BOTH, 0, 0, tiled=True).reshape(rows, width)]
    pallas_call x1, Pallas kernels: 1.56 us -> 2.8 us  [forward(): pl.pallas_call(functools.partial(forward_kernel, own), out_shape=[jax.Sha...]
    reduce_sum x6 -> x0, other arithmetic: 0.71 us -> none  [the longest x1 0.16 us: per_device(): probs = jax.nn.softmax(gate_logits, axis=-1)]
  transfers between devices with their start and end apart: 2 -> 2, of which waited for: 2 -> 2; matrix products, arithmetic and copies ran while one was open for 1% -> 3% of each run, Pallas kernels for 6% -> 6%
where the time goes in v5:
time: 52.2 us; the launch traced here: 51.7 us
  Pallas kernels  18.7 us (36%)
  waiting for transfers between devices  10.6 us (20%)
  blocking collectives  9.99 us (19%)
  starting transfers between devices  9.9 us (19%)
  between operations  0.78 us (1%)
  other arithmetic  0.76 us (1%)
  local copies, waits for them, and re-layouts  0.62 us (1%)
    all_to_all x1, blocking collectives, per_device(): lax.all_to_all(message, BOTH, 0, 0, tiled=True).reshape(rows, width + LANES)  9.99 us
    all_to_all x1, starting transfers between devices, per_device(): lax.all_to_all(spread(events, devices), BOTH, 0, 0, tiled=True)  7.3 us
    all_to_all x1, waiting for transfers between devices, per_device(): parts = lax.all_to_all(part, BOTH, 0, 0, tiled=True).reshape(rows, width)  5.58 us
    pallas_call x1, Pallas kernels, backward(): pl.pallas_call(functools.partial(backward_kernel, tasks, own), out_shape=...  5.39 us
    pallas_call x1, Pallas kernels, spread(): pl.pallas_call(spread_kernel, in_specs=[pl.BlockSpec(memory_space=pl.ANY)...  5.09 us
    all_to_all x1, waiting for transfers between devices, per_device(): lax.all_to_all(spread(events, devices), BOTH, 0, 0, tiled=True)  4.99 us
    pallas_call x2, Pallas kernels, fetch(): pl.pallas_call(fetch_kernel, in_specs=[pl.BlockSpec(memory_space=pl.ANY)]...  3.22 us
    pallas_call x1, Pallas kernels, forward(): pl.pallas_call(functools.partial(forward_kernel, own), out_shape=[jax.Sha...  2.8 us
  transfers between devices with their start and end apart: 2, of which 2 were waited for; matrix products, arithmetic and copies ran while one was open for 3% of the time, Pallas kernels for 6%

profile of v5, /device:TPU:0, one launch (start us, length us, event | category | flops | bytes accessed | tf_op | source)
XLA Modules:
  0.0 51.7 jit_solution(12706513168295852385)
XLA Ops:
  0.6 0.0 copy-start
  0.6 5.1 %spread.1 = bf16[32,2,1024]{2,1,0:T(2,128)(2,1)} custom-call(bf16[2,1024]{1,0:T(2,128)(2,1)} %row_ref.1), custom_call_target="tpu_custom_call" | custom-call | tf_op jit(solution)/shard_map/spread/pallas_call | solution.py:76
  5.7 7.3 %all-to-all-start = ((bf16[32,2,1024]{2,1,0:T(2,128)(2,1)}), bf16[32,2,1024]{2,1,0:T(2,128)(2,1)S(1)}, u32[]{:S(2)}, u32[]{:S(2)}) async-start(bf16[32,2,1024]{2,1,0:T(2,128)(2,1)} %spread.1), calls=%async_computation | async-start | bytes 262144 | tf_op jit(solution)/shard_map/all_to_all | solution.py:363
  13.1 0.7 %convert_bitcast_fusion = f32[4,2]{0,1:T(2,128)S(1)} fusion(s32[2,4]{1,0:T(2,128)} %param.10), kind=kLoop, calls=%fused_computation.9 | loop fusion | flops 8 | bytes 64 | tf_op jit(solution)/shard_map/convert_element_type | solution.py:361
  13.7 0.0 copy-start.1
  13.7 1.6 %fetch.2.first_ref = bf16[1024,1024]{1,0:T(8,128)(2,1)S(1)} custom-call(bf16[1024,1024]{1,0:T(8,128)(2,1)} %bitcast.25), custom_call_target="tpu_custom_call" | custom-call | bytes 4194304 | tf_op jit(solution)/shard_map/fetch/pallas_call | solution.py:101
  15.4 0.0 copy-done
  15.4 0.0 copy-done.1
  15.4 0.4 fusion.5
  15.8 5.0 %all-to-all-done = bf16[32,2,1024]{2,1,0:T(2,128)(2,1)S(1)} async-done(((bf16[32,2,1024]{2,1,0:T(2,128)(2,1)}), bf16[32,2,1024]{2,1,0:T(2,128)(2,1)S(1)}, u32[]{:S(2)}, u32[]{:S(2)}) %all-to-all-start) | async-done | bytes 131104 | tf_op jit(solution)/shard_map/all_to_all | solution.py:363
  20.8 0.1 reshape.39.every_ref
  20.8 0.0 copy-start.4
  20.9 0.0 copy-start.2
  20.9 0.0 copy-start.3
  20.9 2.8 %forward.1 = (bf16[32,2,1024]{2,1,0:T(2,128)(2,1)}, f32[64,1024]{1,0:T(8,128)S(1)}, bf16[64,1024]{1,0:T(8,128)(2,1)S(1)}) custom-call(bf16[64,1024]{1,0:T(8,128)(2,1)S(1)} %reshape.39.every_ref, bf16[1024,1024]{1,0:T(8,128)(2,1)S(1)} %fetch.2.first_ref, bf16[1024,1024]{1,0:T(8,128)(2,1)} %bitcast.23), custom_call_target="tpu_custom_call" | custom-call | flops 268435456 | bytes 4194304 | tf_op jit(solution)/shard_map/forward/pallas_call | solution.py:154
  23.7 2.6 %all-to-all-start.1 = ((bf16[32,2,1024]{2,1,0:T(2,128)(2,1)}), bf16[32,2,1024]{2,1,0:T(2,128)(2,1)S(1)}, u32[]{:S(2)}, u32[]{:S(2)}) async-start(bf16[32,2,1024]{2,1,0:T(2,128)(2,1)} %get-tuple-element.9), calls=%async_computation.1 | async-start | bytes 262144 | tf_op jit(solution)/shard_map/all_to_all | solution.py:367
  26.3 0.1 copy.15
  26.4 0.1 reshape.46.target_ref
  26.5 0.0 copy-done.4
  26.5 0.1 broadcast_in_dim.21
  26.5 0.1 broadcast_in_dim_reshape.4.shift_ref
  26.6 0.0 copy-done.2
  26.6 0.0 copy-done.3
  26.7 0.1 broadcast_multiply_fusion
  26.8 0.1 mul.20.probs_ref
  26.8 1.6 %fetch.3.tower_in_ref = bf16[4,1024,256]{2,1,0:T(8,128)(2,1)S(1)} custom-call(bf16[4,1024,256]{2,1,0:T(8,128)(2,1)} %refs_0_.1), custom_call_target="tpu_custom_call" | custom-call | bytes 4194304 | tf_op jit(solution)/shard_map/fetch/pallas_call | solution.py:101
  28.4 5.6 %all-to-all-done.1 = bf16[32,2,1024]{2,1,0:T(2,128)(2,1)S(1)} async-done(((bf16[32,2,1024]{2,1,0:T(2,128)(2,1)}), bf16[32,2,1024]{2,1,0:T(2,128)(2,1)S(1)}, u32[]{:S(2)}, u32[]{:S(2)}) %all-to-all-start.1) | async-done | bytes 131104 | tf_op jit(solution)/shard_map/all_to_all | solution.py:367
  34.0 0.1 reshape.40.parts_ref
  34.1 2.2 %middle.1 = bf16[32,2,1152]{2,1,0:T(2,128)(2,1)S(1)} custom-call(bf16[64,1024]{1,0:T(8,128)(2,1)S(1)} %reshape.40.parts_ref, f32[8,16]{1,0:T(8,128)S(1)} %mul.20.probs_ref, bf16[4,1024,256]{2,1,0:T(8,128)(2,1)S(1)} %fetch.3.tower_in_ref, f32[8,256]{1,0:T(8,128)S(1)} %reshape.41.bias_ref, f32[8,256]{1,0:T(8,128)S(1)} %reshape.42.weight_ref, ...), custom_call_target="tpu_custom_call" | custom-call | flops 33554432 | bytes 2097152 | tf_op jit(solution)/shard_map/middle/pallas_call | solution.py:238
  36.3 10.0 %all_to_all.15 = bf16[32,2,1152]{2,1,0:T(2,128)(2,1)S(1)} all-to-all(bf16[32,2,1152]{2,1,0:T(2,128)(2,1)S(1)} %middle.1), channel_id=1, replica_groups=mesh['dp'=4,'expert'=8] {'dp','expert'}, dimensions={0} | all-to-all | bytes 294912 | tf_op jit(solution)/shard_map/all_to_all | solution.py:373
  46.3 0.1 reshape.44.arrived_ref
  46.4 5.4 %backward.1 = (bf16[1024,1024]{1,0:T(8,128)(2,1)}, bf16[1024,1024]{1,0:T(8,128)(2,1)}, f32[4,1,1024]{2,1,0:T(1,128)}) custom-call(bf16[64,1152]{1,0:T(8,128)(2,1)S(1)} %reshape.44.arrived_ref, bf16[64,1024]{1,0:T(8,128)(2,1)S(1)} %reshape.39.every_ref, bf16[64,1024]{1,0:T(8,128)(2,1)S(1)} %get-tuple-element.10.hidden_ref, ...), custom_call_target="tpu_custom_call" | custom-call | flops 402653184 | bytes 6291456 | tf_op jit(solution)/shard_map/backward/pallas_call | solution.py:319
  (5 shorter events, 0.0 us)
Async XLA Ops:
  0.6 14.7 %copy-start = (bf16[4,1024,8]{1,2,0:T(8,128)(2,1)S(1)}, bf16[4,1024,8]{1,2,0:T(8,128)(2,1)}, u32[]{:S(2)}) copy-start(bf16[4,1024,8]{1,2,0:T(8,128)(2,1)} %param.13) | copy-start | bytes 196612
  5.7 15.1 %all-to-all-start = ((bf16[32,2,1024]{2,1,0:T(2,128)(2,1)}), bf16[32,2,1024]{2,1,0:T(2,128)(2,1)S(1)}, u32[]{:S(2)}, u32[]{:S(2)}) async-start(bf16[32,2,1024]{2,1,0:T(2,128)(2,1)} %spread.1), calls=%async_computation | async-start | bytes 262144 | tf_op jit(solution)/shard_map/all_to_all | solution.py:363
  13.7 1.6 %copy-start.1 = (bf16[2,1024]{1,0:T(2,128)(2,1)S(1)}, bf16[2,1024]{1,0:T(2,128)(2,1)}, u32[]{:S(2)}) copy-start(bf16[2,1024]{1,0:T(2,128)(2,1)} %row_ref.1) | copy-start | bytes 12292
  20.8 5.6 %copy-start.4 = (f32[4]{0:T(128)S(1)}, f32[4]{0:T(128)}, u32[]{:S(2)}) copy-start(f32[4]{0:T(128)} %param.17) | copy-start | bytes 52
  20.9 5.8 %copy-start.2 = (f32[4,256]{1,0:T(4,128)S(1)}, f32[4,256]{1,0:T(4,128)}, u32[]{:S(2)}) copy-start(f32[4,256]{1,0:T(4,128)} %param.15) | copy-start | bytes 12292
  20.9 5.8 %copy-start.3 = (f32[4,256]{1,0:T(4,128)S(1)}, f32[4,256]{1,0:T(4,128)}, u32[]{:S(2)}) copy-start(f32[4,256]{1,0:T(4,128)} %param.16) | copy-start | bytes 12292
  23.7 10.3 %all-to-all-start.1 = ((bf16[32,2,1024]{2,1,0:T(2,128)(2,1)}), bf16[32,2,1024]{2,1,0:T(2,128)(2,1)S(1)}, u32[]{:S(2)}, u32[]{:S(2)}) async-start(bf16[32,2,1024]{2,1,0:T(2,128)(2,1)} %get-tuple-element.9), calls=%async_computation.1 | async-start | bytes 262144 | tf_op jit(solution)/shard_map/all_to_all | solution.py:367

commit v6 on v5

--- a/solution.py
+++ b/solution.py
@@ -64,50 +64,52 @@
     return pltpu.with_memory_space_constraint(value, pltpu.HBM)
 
 
-def spread_kernel(row_ref, out_ref, sem):
-    def body(step):
-        pltpu.make_async_copy(row_ref, out_ref.at[step], sem).start()
-
-    steps(out_ref.shape[0], True, body)
-    pltpu.make_async_copy(out_ref, out_ref, sem).wait()
+def spread_kernel(row_ref, out_ref):
+    for step in range(out_ref.shape[0]):
+        out_ref[step] = row_ref[...]
 
 
 def spread(value, devices):
     return pl.pallas_call(
         spread_kernel,
-        in_specs=[pl.BlockSpec(memory_space=pl.ANY)],
-        out_specs=pl.BlockSpec(memory_space=pl.ANY),
-        out_shape=pltpu.HBM((devices, *value.shape), value.dtype),
-        scratch_shapes=[pltpu.SemaphoreType.DMA],
+        out_shape=jax.ShapeDtypeStruct((devices, *value.shape), value.dtype),
         compiler_params=params(),
         name="spread",
-    )(in_hbm(value))
-
-
-def fetch_kernel(*refs):
-    count = (len(refs) - 1) // 2
-    sems = refs[-1]
-    copies = [
-        pltpu.make_async_copy(refs[at], refs[count + at], sems.at[at]) for at in range(count)
-    ]
+    )(value)
+
+
+def fetch_kernel(count, cuts, *refs):
+    sources, targets, sems = refs[:count], refs[-1 - count : -1], refs[-1]
+    copies = []
+    for at in range(count):
+        size = targets[at].shape[0] // cuts
+        for cut in range(cuts):
+            here = pl.ds(cut * size, size)
+            copies.append(
+                pltpu.make_async_copy(
+                    sources[at].at[here], targets[at].at[here], sems.at[at, cut]
+                )
+            )
     for copy in copies:
         copy.start()
     for copy in copies:
         copy.wait()
 
 
-def fetch(*arrays):
+def fetch(*arrays, sizes=None, after=(), cuts=4):
+    sizes = sizes or [array.shape[0] for array in arrays]
+    shapes = [(size, *array.shape[1:]) for size, array in zip(sizes, arrays)]
     moved = sum(array.size * array.dtype.itemsize for array in arrays)
     return pl.pallas_call(
-        fetch_kernel,
-        in_specs=[pl.BlockSpec(memory_space=pl.ANY)] * len(arrays),
+        functools.partial(fetch_kernel, len(arrays), cuts),
+        in_specs=[pl.BlockSpec(memory_space=pl.ANY)] * (len(arrays) + len(after)),
         out_specs=[pl.BlockSpec(memory_space=pltpu.VMEM)] * len(arrays),
-        out_shape=[pltpu.VMEM(array.shape, array.dtype) for array in arrays],
-        scratch_shapes=[pltpu.SemaphoreType.DMA((len(arrays),))],
+        out_shape=[pltpu.VMEM(shape, array.dtype) for shape, array in zip(shapes, arrays)],
+        scratch_shapes=[pltpu.SemaphoreType.DMA((len(arrays), cuts))],
         compiler_params=params(),
         cost_estimate=cost(0, 2 * moved),
         name="fetch",
-    )(*(in_hbm(array) for array in arrays))
+    )(*(in_hbm(array) for array in arrays), *after)
 
 
 def streamed(source, target, sems):
@@ -119,35 +121,42 @@
 
 
 def forward_kernel(
-    own, every_ref, first_ref, second_ref, part_ref, pre_ref, hidden_ref, second_buf, sems
+    own, every_ref, first_ref, upper_ref, second_ref, part_ref, pre_ref, hidden_ref, lower_buf, sems
 ):
     rows = every_ref.shape[0]
     chunk = min(rows, 64)
-    blocks = second_ref.shape[0] // TILE
-    block = streamed(second_ref, second_buf, sems)
-    for at in range(blocks):
+    half = upper_ref.shape[0]
+    block = streamed(second_ref.at[pl.ds(half, half), :], lower_buf, sems)
+    for at in range(half // TILE):
         block(at).start()
 
-    def body(step):
+    def begin(step):
         here = span(step, chunk)
         pre = dot(every_ref[here, :], first_ref[...], (1, 0))
         pre_ref[here, :] = pre
         hidden_ref[here, :] = gelu_tanh(pre).astype(jnp.bfloat16)
 
-    steps(rows // chunk, rows == chunk, body)
-    for at in range(blocks):
-        block(at).wait()
-
     def finish(step):
         here = span(step, chunk)
-        part = dot(hidden_ref[here, :], second_buf[...], (1, 0)).astype(jnp.bfloat16)
+        part = dot(hidden_ref[here, :half], upper_ref[...], (1, 0))
+        if rows == chunk:
+            arrive()
+        part = part + dot(hidden_ref[here, half:], lower_buf[...], (1, 0))
+        part = part.astype(jnp.bfloat16)
         for at in range(chunk // own):
             part_ref[step * (chunk // own) + at] = part[at * own : (at + 1) * own]
 
+    def arrive():
+        for at in range(half // TILE):
+            block(at).wait()
+
+    steps(rows // chunk, rows == chunk, begin)
+    if rows != chunk:
+        arrive()
     steps(rows // chunk, rows == chunk, finish)
 
 
-def forward(every, first, second, own):
+def forward(every, first, upper, second, own):
     rows, width = every.shape
     units = first.shape[1]
     inside = pl.BlockSpec(memory_space=pltpu.VMEM)
@@ -158,16 +167,16 @@
             pltpu.VMEM((rows, units), jnp.float32),
             pltpu.VMEM((rows, units), jnp.bfloat16),
         ],
-        in_specs=[inside, inside, pl.BlockSpec(memory_space=pl.ANY)],
+        in_specs=[inside] * 3 + [pl.BlockSpec(memory_space=pl.ANY)],
         out_specs=[inside] * 3,
         scratch_shapes=[
-            pltpu.VMEM(second.shape, second.dtype),
-            pltpu.SemaphoreType.DMA((units // TILE,)),
+            pltpu.VMEM(upper.shape, upper.dtype),
+            pltpu.SemaphoreType.DMA((upper.shape[0] // TILE,)),
         ],
         compiler_params=params(),
         cost_estimate=cost(4 * rows * width * units, 4 * width * units),
         name="forward",
-    )(every, first, in_hbm(second))
+    )(every, first, upper, in_hbm(second))
 
 
 def middle_kernel(
@@ -258,17 +267,12 @@
     dpre_ref,
     first_buf,
     second_buf,
-    weight_buf,
     sems,
-    weight_sems,
 ):
     rows, width = every_ref.shape
     units = hidden_ref.shape[1]
     flat = rows <= 64
     across, down = units // TILE, width // TILE
-    block = streamed(second_ref, weight_buf, weight_sems)
-    for at in range(across):
-        block(at).start()
 
     def second_copy(step):
         here = span(step, TILE)
@@ -291,8 +295,7 @@
 
     def dpre_step(step):
         here = span(step, TILE)
-        block(step).wait()
-        dhidden = dot(arrived_ref[:, :width], weight_buf[here, :], (1, 1))
+        dhidden = dot(arrived_ref[:, :width], second_ref[here, :], (1, 1))
         dpre_ref[:, here] = (gelu_slope(pre_ref[:, here]) * dhidden).astype(jnp.bfloat16)
 
     def first_step(step):
@@ -323,20 +326,18 @@
             jax.ShapeDtypeStruct((units, width), jnp.bfloat16),
             jax.ShapeDtypeStruct((tasks, 1, width), jnp.float32),
         ],
-        in_specs=[inside] * 4 + [anywhere],
+        in_specs=[inside] * 5,
         out_specs=[anywhere, anywhere, inside],
         scratch_shapes=[
             pltpu.VMEM((rows, units), jnp.bfloat16),
             pltpu.VMEM((width, units), jnp.bfloat16),
             pltpu.VMEM((units, width), jnp.bfloat16),
-            pltpu.VMEM((units, width), jnp.bfloat16),
             pltpu.SemaphoreType.DMA((units // TILE + width // TILE,)),
-            pltpu.SemaphoreType.DMA((units // TILE,)),
         ],
         compiler_params=params(),
         cost_estimate=cost(6 * rows * width * units, 6 * width * units),
         name="backward",
-    )(arrived, every, hidden, pre, in_hbm(second))
+    )(arrived, every, hidden, pre, second)
 
 
 def per_device(
@@ -361,18 +362,19 @@
     target = labels.T.astype(jnp.float32).reshape(tasks * own, 1)
 
     every = lax.all_to_all(spread(events, devices), BOTH, 0, 0, tiled=True).reshape(rows, width)
-    (first,) = fetch(w_in[0])
-    part, pre, hidden = forward(every, first, w_out[0], own)
+    first, upper = fetch(w_in[0], w_out[0], sizes=(w_in.shape[1], w_out.shape[1] // 2))
+    part, pre, hidden = forward(every, first, upper, w_out[0], own)
 
     parts = lax.all_to_all(part, BOTH, 0, 0, tiled=True).reshape(rows, width)
-    (tower_here,) = fetch(tower_in)
+    (tower_here,) = fetch(tower_in, after=(part,))
     message = middle(
         (dp, experts, own), parts, probs, tower_here, bias, weight, shift, target
     )
 
+    (second,) = fetch(w_out[0], after=(message,))
     arrived = lax.all_to_all(message, BOTH, 0, 0, tiled=True).reshape(rows, width + LANES)
     grad_first, grad_second, grad_gate = backward(
-        arrived, every, hidden, pre, w_out[0], tasks, own
+        arrived, every, hidden, pre, second, tasks, own
     )
     return (grad_first[None], grad_second[None], jnp.transpose(grad_gate, (0, 2, 1)))
 

time: 52.2 us -> 48.1 us (0.921)
  blocking collectives: 9.99 us -> 0 us
  waiting for transfers between devices: 10.6 us -> 16.5 us
  Pallas kernels: 18.7 us -> 14.7 us
  starting transfers between devices: 9.9 us -> 12.4 us
  local copies, waits for them, and re-layouts: 0.62 us -> 2.04 us
    all_to_all x1 -> x0, blocking collectives: 9.99 us -> none  [per_device(): lax.all_to_all(message, BOTH, 0, 0, tiled=True).reshape(rows, width + LANES)]
    all_to_all x0 -> x1, waiting for transfers between devices: none -> 6.21 us  [per_device(): lax.all_to_all(message, BOTH, 0, 0, tiled=True).reshape(rows, width + LANES)]
    pallas_call x3 -> x4, Pallas kernels: 8.3 us -> 5.71 us  [the longest x3 5.05 us: fetch(): pl.pallas_call(functools.partial(fetch_kernel, len(arrays), cuts), in_spe...]
    all_to_all x0 -> x1, starting transfers between devices: none -> 2.58 us  [per_device(): lax.all_to_all(message, BOTH, 0, 0, tiled=True).reshape(rows, width + LANES)]
    pallas_call x1, Pallas kernels: 5.39 us -> 3.51 us  [backward(): pl.pallas_call(functools.partial(backward_kernel, tasks, own), out_shape=...]
    unnamed x10 -> x16, local copies, waits for them, and re-layouts: 0.03 us -> 1.45 us
    pallas_call x1, Pallas kernels: 2.21 us -> 2.87 us  [middle(): pl.pallas_call(functools.partial(middle_kernel, shape), out_shape=jax.Sha...]
  transfers between devices with their start and end apart: 2 -> 3, of which waited for: 2 -> 3; matrix products, arithmetic and copies ran while one was open for 3% -> 3% of each run, Pallas kernels for 6% -> 11%
where the time goes in v6:
time: 48.1 us; the launch traced here: 47.7 us
  waiting for transfers between devices  16.5 us (34%)
  Pallas kernels  14.7 us (31%)
  starting transfers between devices  12.4 us (26%)
  local copies, waits for them, and re-layouts  2.04 us (4%)
  between operations  0.81 us (2%)
  other arithmetic  0.76 us (2%)
    all_to_all x1, starting transfers between devices, per_device(): lax.all_to_all(spread(events, devices), BOTH, 0, 0, tiled=True)  7.3 us
    all_to_all x1, waiting for transfers between devices, per_device(): lax.all_to_all(message, BOTH, 0, 0, tiled=True).reshape(rows, width + LANES)  6.21 us
    all_to_all x1, waiting for transfers between devices, per_device(): parts = lax.all_to_all(part, BOTH, 0, 0, tiled=True).reshape(rows, width)  5.63 us
    pallas_call x3, Pallas kernels, fetch(): pl.pallas_call(functools.partial(fetch_kernel, len(arrays), cuts), in_spe...  5.05 us
    all_to_all x1, waiting for transfers between devices, per_device(): lax.all_to_all(spread(events, devices), BOTH, 0, 0, tiled=True)  4.7 us
    pallas_call x1, Pallas kernels, backward(): pl.pallas_call(functools.partial(backward_kernel, tasks, own), out_shape=...  3.51 us
    pallas_call x1, Pallas kernels, middle(): pl.pallas_call(functools.partial(middle_kernel, shape), out_shape=jax.Sha...  2.87 us
    all_to_all x1, starting transfers between devices, per_device(): lax.all_to_all(message, BOTH, 0, 0, tiled=True).reshape(rows, width + LANES)  2.58 us
  transfers between devices with their start and end apart: 3, of which 3 were waited for; matrix products, arithmetic and copies ran while one was open for 3% of the time, Pallas kernels for 11%

profile of v6, /device:TPU:0, one launch (start us, length us, event | category | flops | bytes accessed | tf_op | source)
XLA Modules:
  0.0 47.7 jit_solution(10687359667187624279)
XLA Ops:
  0.6 0.0 copy-start
  0.6 0.0 copy-start.3
  0.7 0.7 %copy-done.3 = bf16[2,1024]{1,0:T(2,128)(2,1)S(1)} copy-done((bf16[2,1024]{1,0:T(2,128)(2,1)S(1)}, bf16[2,1024]{1,0:T(2,128)(2,1)}, u32[]{:S(2)}) %copy-start.3) | copy-done | bytes 4120
  1.4 0.7 %spread.1 = bf16[32,2,1024]{2,1,0:T(2,128)(2,1)} custom-call(bf16[2,1024]{1,0:T(2,128)(2,1)S(1)} %copy-done.3), custom_call_target="tpu_custom_call" | custom-call | tf_op jit(solution)/shard_map/spread/pallas_call | solution.py:73
  2.0 7.3 %all-to-all-start = ((bf16[32,2,1024]{2,1,0:T(2,128)(2,1)}), bf16[32,2,1024]{2,1,0:T(2,128)(2,1)S(1)}, u32[]{:S(2)}, u32[]{:S(2)}) async-start(bf16[32,2,1024]{2,1,0:T(2,128)(2,1)} %spread.1), calls=%async_computation | async-start | bytes 262144 | tf_op jit(solution)/shard_map/all_to_all | solution.py:364
  9.3 0.7 %convert_bitcast_fusion = f32[4,2]{0,1:T(2,128)S(1)} fusion(s32[2,4]{1,0:T(2,128)} %param.10), kind=kLoop, calls=%fused_computation.9 | loop fusion | flops 8 | bytes 64 | tf_op jit(solution)/shard_map/convert_element_type | solution.py:362
  10.0 1.9 %fetch.3 = (bf16[1024,1024]{1,0:T(8,128)(2,1)S(1)}, bf16[512,1024]{1,0:T(8,128)(2,1)S(1)}) custom-call(bf16[1024,1024]{1,0:T(8,128)(2,1)} %bitcast.26, bf16[1024,1024]{1,0:T(8,128)(2,1)} %bitcast.23), custom_call_target="tpu_custom_call" | custom-call | bytes 8388608 | tf_op jit(solution)/shard_map/fetch/pallas_call | solution.py:103
  11.9 0.4 fusion.5
  12.4 4.7 %all-to-all-done = bf16[32,2,1024]{2,1,0:T(2,128)(2,1)S(1)} async-done(((bf16[32,2,1024]{2,1,0:T(2,128)(2,1)}), bf16[32,2,1024]{2,1,0:T(2,128)(2,1)S(1)}, u32[]{:S(2)}, u32[]{:S(2)}) %all-to-all-start) | async-done | bytes 131104 | tf_op jit(solution)/shard_map/all_to_all | solution.py:364
  17.1 0.1 reshape.39.every_ref
  17.1 0.0 copy-start.7
  17.1 0.0 copy-start.5
  17.2 0.0 copy-start.6
  17.2 2.6 %forward.1 = (bf16[32,2,1024]{2,1,0:T(2,128)(2,1)}, f32[64,1024]{1,0:T(8,128)S(1)}, bf16[64,1024]{1,0:T(8,128)(2,1)S(1)}) custom-call(bf16[64,1024]{1,0:T(8,128)(2,1)S(1)} %reshape.39.every_ref, bf16[1024,1024]{1,0:T(8,128)(2,1)S(1)} %get-tuple-element.11.first_ref, bf16[512,1024]{1,0:T(8,128)(2,1)S(1)} %get-tuple-element.12.upper_ref, ...), custom_call_target="tpu_custom_call" | custom-call | flops 268435456 | bytes 4194304 | tf_op jit(solution)/shard_map/forward/pallas_call | solution.py:163
  19.7 0.0 copy-start.1
  19.7 0.7 %copy-done.1 = f32[64,1024]{1,0:T(8,128)} copy-done((f32[64,1024]{1,0:T(8,128)}, f32[64,1024]{1,0:T(8,128)S(1)}, u32[]{:S(2)}) %copy-start.1) | copy-done | bytes 262168
  20.4 2.6 %all-to-all-start.1 = ((bf16[32,2,1024]{2,1,0:T(2,128)(2,1)}), bf16[32,2,1024]{2,1,0:T(2,128)(2,1)S(1)}, u32[]{:S(2)}, u32[]{:S(2)}) async-start(bf16[32,2,1024]{2,1,0:T(2,128)(2,1)} %get-tuple-element.13.refs_1_), calls=%async_computation.1 | async-start | bytes 262144 | tf_op jit(solution)/shard_map/all_to_all | solution.py:368
  23.0 0.1 copy.15
  23.1 0.1 reshape.46.target_ref
  23.2 0.1 broadcast_in_dim.21
  23.3 0.1 broadcast_in_dim_reshape.4.shift_ref
  23.4 0.1 broadcast_multiply_fusion
  23.5 0.1 mul.20.probs_ref
  23.6 1.6 %fetch.4.tower_in_ref = bf16[4,1024,256]{2,1,0:T(8,128)(2,1)S(1)} custom-call(bf16[4,1024,256]{2,1,0:T(8,128)(2,1)} %refs_0_.1, bf16[32,2,1024]{2,1,0:T(2,128)(2,1)} %get-tuple-element.13.refs_1_), custom_call_target="tpu_custom_call" | custom-call | bytes 4194304 | tf_op jit(solution)/shard_map/fetch/pallas_call | solution.py:103
  25.1 5.6 %all-to-all-done.1 = bf16[32,2,1024]{2,1,0:T(2,128)(2,1)S(1)} async-done(((bf16[32,2,1024]{2,1,0:T(2,128)(2,1)}), bf16[32,2,1024]{2,1,0:T(2,128)(2,1)S(1)}, u32[]{:S(2)}, u32[]{:S(2)}) %all-to-all-start.1) | async-done | bytes 131104 | tf_op jit(solution)/shard_map/all_to_all | solution.py:368
  30.8 0.1 reshape.40.parts_ref
  30.8 2.9 %middle.1.refs_1_ = bf16[32,2,1152]{2,1,0:T(2,128)(2,1)} custom-call(bf16[64,1024]{1,0:T(8,128)(2,1)S(1)} %reshape.40.parts_ref, f32[8,16]{1,0:T(8,128)S(1)} %mul.20.probs_ref, bf16[4,1024,256]{2,1,0:T(8,128)(2,1)S(1)} %fetch.4.tower_in_ref, f32[8,256]{1,0:T(8,128)S(1)} %reshape.41.bias_ref, f32[8,256]{1,0:T(8,128)S(1)} %reshape.42.weight_ref, ...), custom_call_target="tpu_custom_call" | custom-call | flops 33554432 | bytes 2097152 | tf_op jit(solution)/shard_map/middle/pallas_call | solution.py:247
  33.7 2.6 %all-to-all-start.2 = ((bf16[32,2,1152]{2,1,0:T(2,128)(2,1)}), bf16[32,2,1152]{2,1,0:T(2,128)(2,1)S(1)}, u32[]{:S(2)}, u32[]{:S(2)}) async-start(bf16[32,2,1152]{2,1,0:T(2,128)(2,1)} %middle.1.refs_1_), calls=%async_computation.2 | async-start | bytes 294912 | tf_op jit(solution)/shard_map/all_to_all | solution.py:375
  36.3 1.6 %fetch.5.second_ref = bf16[1024,1024]{1,0:T(8,128)(2,1)S(1)} custom-call(bf16[1024,1024]{1,0:T(8,128)(2,1)} %bitcast.25, bf16[32,2,1152]{2,1,0:T(2,128)(2,1)} %middle.1.refs_1_), custom_call_target="tpu_custom_call" | custom-call | bytes 4194304 | tf_op jit(solution)/shard_map/fetch/pallas_call | solution.py:103
  37.9 6.2 %all-to-all-done.2 = bf16[32,2,1152]{2,1,0:T(2,128)(2,1)S(1)} async-done(((bf16[32,2,1152]{2,1,0:T(2,128)(2,1)}), bf16[32,2,1152]{2,1,0:T(2,128)(2,1)S(1)}, u32[]{:S(2)}, u32[]{:S(2)}) %all-to-all-start.2) | async-done | bytes 147488 | tf_op jit(solution)/shard_map/all_to_all | solution.py:375
  44.1 0.1 reshape.44.arrived_ref
  44.2 3.5 %backward.1 = (bf16[1024,1024]{1,0:T(8,128)(2,1)}, bf16[1024,1024]{1,0:T(8,128)(2,1)}, f32[4,1,1024]{2,1,0:T(1,128)}) custom-call(bf16[64,1152]{1,0:T(8,128)(2,1)S(1)} %reshape.44.arrived_ref, bf16[64,1024]{1,0:T(8,128)(2,1)S(1)} %reshape.39.every_ref, bf16[64,1024]{1,0:T(8,128)(2,1)S(1)} %get-tuple-element.14.hidden_ref, f32[64,1024]{1,0:T(8,128)S(1)} %copy-done.2, ...), custom_call_target="tpu_custom_call" | custom-call | flops 402653184 | bytes 6291456 | tf_op jit(solution)/shard_map/backward/pallas_call | solution.py:322
  (13 shorter events, 0.1 us)
Async XLA Ops:
  0.6 11.3 %copy-start = (bf16[4,1024,8]{1,2,0:T(8,128)(2,1)S(1)}, bf16[4,1024,8]{1,2,0:T(8,128)(2,1)}, u32[]{:S(2)}) copy-start(bf16[4,1024,8]{1,2,0:T(8,128)(2,1)} %param.13) | copy-start | bytes 196612
  0.6 0.7 %copy-start.3 = (bf16[2,1024]{1,0:T(2,128)(2,1)S(1)}, bf16[2,1024]{1,0:T(2,128)(2,1)}, u32[]{:S(2)}) copy-start(bf16[2,1024]{1,0:T(2,128)(2,1)} %row_ref.1) | copy-start | bytes 12292
  2.0 15.0 %all-to-all-start = ((bf16[32,2,1024]{2,1,0:T(2,128)(2,1)}), bf16[32,2,1024]{2,1,0:T(2,128)(2,1)S(1)}, u32[]{:S(2)}, u32[]{:S(2)}) async-start(bf16[32,2,1024]{2,1,0:T(2,128)(2,1)} %spread.1), calls=%async_computation | async-start | bytes 262144 | tf_op jit(solution)/shard_map/all_to_all | solution.py:364
  10.0 1.9 %copy-start.4 = (bf16[2,1024]{1,0:T(2,128)(2,1)S(1)}, bf16[2,1024]{1,0:T(2,128)(2,1)}, u32[]{:S(2)}) copy-start(bf16[2,1024]{1,0:T(2,128)(2,1)} %row_ref.1) | copy-start | bytes 12292
  17.1 6.1 %copy-start.7 = (f32[4]{0:T(128)S(1)}, f32[4]{0:T(128)}, u32[]{:S(2)}) copy-start(f32[4]{0:T(128)} %param.17) | copy-start | bytes 52
  17.1 6.2 %copy-start.5 = (f32[4,256]{1,0:T(4,128)S(1)}, f32[4,256]{1,0:T(4,128)}, u32[]{:S(2)}) copy-start(f32[4,256]{1,0:T(4,128)} %param.15) | copy-start | bytes 12292
  17.2 6.2 %copy-start.6 = (f32[4,256]{1,0:T(4,128)S(1)}, f32[4,256]{1,0:T(4,128)}, u32[]{:S(2)}) copy-start(f32[4,256]{1,0:T(4,128)} %param.16) | copy-start | bytes 12292
  19.7 0.7 %copy-start.1 = (f32[64,1024]{1,0:T(8,128)}, f32[64,1024]{1,0:T(8,128)S(1)}, u32[]{:S(2)}) copy-start(f32[64,1024]{1,0:T(8,128)S(1)} %get-tuple-element.15.pre_ref) | copy-start | bytes 786436
  20.4 10.3 %all-to-all-start.1 = ((bf16[32,2,1024]{2,1,0:T(2,128)(2,1)}), bf16[32,2,1024]{2,1,0:T(2,128)(2,1)S(1)}, u32[]{:S(2)}, u32[]{:S(2)}) async-start(bf16[32,2,1024]{2,1,0:T(2,128)(2,1)} %get-tuple-element.13.refs_1_), calls=%async_computation.1 | async-start | bytes 262144 | tf_op jit(solution)/shard_map/all_to_all | solution.py:368
  33.7 10.4 %all-to-all-start.2 = ((bf16[32,2,1152]{2,1,0:T(2,128)(2,1)}), bf16[32,2,1152]{2,1,0:T(2,128)(2,1)S(1)}, u32[]{:S(2)}, u32[]{:S(2)}) async-start(bf16[32,2,1152]{2,1,0:T(2,128)(2,1)} %middle.1.refs_1_), calls=%async_computation.2 | async-start | bytes 294912 | tf_op jit(solution)/shard_map/all_to_all | solution.py:375
  36.3 7.9 %copy-start.2 = (f32[64,1024]{1,0:T(8,128)S(1)}, f32[64,1024]{1,0:T(8,128)}, u32[]{:S(2)}) copy-start(f32[64,1024]{1,0:T(8,128)} %copy-done.1) | copy-start | bytes 786436

commit v7 on v4

v7 whole, which is shorter than its diff:
```python
import functools

import jax
import jax.numpy as jnp
from jax import lax
from jax.experimental import pallas as pl
from jax.experimental.pallas import tpu as pltpu
from jax.sharding import PartitionSpec as P

BOTH = ("dp", "expert")
LANES = 128
TILE = 256
GELU_C = 0.7978845608028654
GELU_A = 0.044715
AHEAD_FLOPS = 1 << 34
VMEM_LIMIT = 32 * 1024 * 1024


def gelu_tanh(value):
    return jax.nn.gelu(value, approximate=True)


def gelu_slope(value):
    square = value * value
    bend = jnp.tanh(GELU_C * (value + GELU_A * value * square))
    inner = GELU_C * (1.0 + 3.0 * GELU_A * square)
    return 0.5 * (1.0 + bend) + 0.5 * value * (1.0 - bend * bend) * inner


def pieces_of(value):
    high = value.astype(jnp.bfloat16)
    rest = value - high.astype(jnp.float32)
    middle = rest.astype(jnp.bfloat16)
    low = (rest - middle.astype(jnp.float32)).astype(jnp.bfloat16)
    return high, middle, low


def dot(left, right, over):
    return lax.dot_general(
        left, right, ((over[:1], over[1:]), ((), ())), preferred_element_type=jnp.float32
    )


def steps(count, flat, body):
    if flat:
        for step in range(count):
            body(step)
    else:
        lax.fori_loop(0, count, lambda step, none: (body(step), none)[1], None)


def span(step, size):
    return pl.ds(pl.multiple_of(step * size, size), size)


def params():
    return pltpu.CompilerParams(vmem_limit_bytes=VMEM_LIMIT)


def cost(flops, moved):
    return pl.CostEstimate(flops=flops, bytes_accessed=moved, transcendentals=0)


def in_vmem(value):
    return pltpu.with_memory_space_constraint(value, pltpu.VMEM)


def spread_kernel(row_ref, out_ref):
    for step in range(out_ref.shape[0]):
        out_ref[step] = row_ref[...]


def spread(value, devices):
    return pl.pallas_call(
        spread_kernel,
        out_shape=pltpu.VMEM((devices, *value.shape), value.dtype),
        compiler_params=params(),
        cost_estimate=cost(AHEAD_FLOPS, 0),
        name="spread",
    )(value)


def unpack(message_ref, rows_ref):
    own = message_ref.shape[1]
    for at in range(message_ref.shape[0]):
        rows_ref[at * own : (at + 1) * own, :] = message_ref[at].astype(jnp.float32)


def forward_kernel(
    got_ref, first_ref, second_ref, part_ref, every_ref, pre_ref, hidden_ref, wide_ref
):
    own = got_ref.shape[1]
    rows = every_ref.shape[0]
    chunk = min(rows, 64)
    unpack(got_ref, wide_ref)

    def body(step):
        here = span(step, chunk)
        every = wide_ref[here, :].astype(jnp.bfloat16)
        every_ref[here, :] = every
        pre = dot(every, first_ref[...], (1, 0))
        hidden = gelu_tanh(pre).astype(jnp.bfloat16)
        part = dot(hidden, second_ref[...], (1, 0)).astype(jnp.bfloat16)
        for at in range(chunk // own):
            part_ref[step * (chunk // own) + at] = part[at * own : (at + 1) * own]
        pre_ref[here, :] = pre
        hidden_ref[here, :] = hidden

    steps(rows // chunk, rows == chunk, body)


def forward(got, first, second):
    devices, own, width = got.shape
    rows = devices * own
    units = first.shape[1]
    return pl.pallas_call(
        forward_kernel,
        out_shape=[
            pltpu.VMEM(got.shape, jnp.bfloat16),
            pltpu.VMEM((rows, width), jnp.bfloat16),
            pltpu.VMEM((rows, units), jnp.float32),
            pltpu.VMEM((rows, units), jnp.bfloat16),
        ],
        scratch_shapes=[pltpu.VMEM((rows, width), jnp.float32)],
        compiler_params=params(),
        cost_estimate=cost(4 * rows * width * units, 4 * width * units),
        name="forward",
    )(got, in_vmem(first), in_vmem(second))


def middle_kernel(
    dp,
    parts_ref,
    events_ref,
    labels_ref,
    gate_ref,
    tower_in_ref,
    bias_ref,
    weight_ref,
    shift_ref,
    message_ref,
    outs_ref,
):
    devices, own, width = parts_ref.shape
    experts = devices // dp
    tasks = tower_in_ref.shape[0]
    slots = experts * own
    rows = tasks * own
    float32, bfloat16 = jnp.float32, jnp.bfloat16

    def iota(shape, axis):
        return lax.broadcasted_iota(jnp.int32, shape, axis)

    def spread_rows(value_of, wide, of_task):
        at = iota((rows, wide), 0)
        at = at // own if of_task else lax.rem(at, own)
        result = jnp.zeros((rows, wide), float32)
        for key in range(tasks if of_task else own):
            result = jnp.where(at == key, value_of(key), result)
        return result

    def split(value):
        return jnp.concatenate([piece.astype(float32) for piece in pieces_of(value)], 0)

    def fold(value):
        return value[:rows] + value[rows : 2 * rows] + value[2 * rows :]

    def only(value, task):
        at = lax.rem(iota(value.shape, 0), rows) // own
        return jnp.where(at == task, value, 0.0).astype(bfloat16)

    events = events_ref[...].astype(float32)
    events = spread_rows(lambda row: events[row : row + 1], width, False).astype(bfloat16)
    gates = spread_rows(lambda task: dot(events, gate_ref[task], (1, 1)), experts, True)
    gates = jnp.exp(gates - jnp.max(gates, -1, keepdims=True))
    gates = gates / jnp.sum(gates, -1, keepdims=True)
    place = (iota((experts, slots), 0) == iota((experts, slots), 1) // own).astype(bfloat16)
    same = lax.rem(iota((3 * rows, slots), 0), own) == lax.rem(iota((3 * rows, slots), 1), own)
    share = jnp.where(same, dot(split(gates).astype(bfloat16), place, (1, 0)), 0.0)
    probs = fold(share)
    share = share.astype(bfloat16)

    for expert in range(experts):
        total = parts_ref[expert].astype(float32)
        for at in range(1, dp):
            total = total + parts_ref[at * experts + expert].astype(float32)
        outs_ref[expert * own : (expert + 1) * own, :] = total
    outs = outs_ref[...].astype(bfloat16)

    mixed = fold(dot(share, outs, (1, 0))).astype(bfloat16).astype(float32)
    tower = spread_rows(lambda task: bias_ref[task : task + 1, :], bias_ref.shape[1], True)
    weight = spread_rows(lambda task: weight_ref[task : task + 1, :], bias_ref.shape[1], True)
    shift = spread_rows(lambda task: shift_ref[:, task : task + 1], 1, True)
    labels = labels_ref[...].astype(float32)
    labels = spread_rows(lambda row: labels[row : row + 1], tasks, False)
    pick = iota((rows, tasks), 0) // own == iota((rows, tasks), 1)
    target = jnp.sum(jnp.where(pick, labels, 0.0), -1, keepdims=True)
    for task in range(tasks):
        tower = tower + dot(only(mixed, task), tower_in_ref[task], (1, 0))
    logit = jnp.sum(gelu_tanh(tower) * weight, -1, keepdims=True) + shift
    dlogit = jax.nn.sigmoid(logit) - target
    stack = split(gelu_slope(tower) * (dlogit * weight))
    wide = dot(only(stack, 0), tower_in_ref[0], (1, 1))
    for task in range(1, tasks):
        wide = wide + dot(only(stack, task), tower_in_ref[task], (1, 1))
    dmixed = fold(wide).astype(bfloat16)
    dprob = dot(dmixed, outs, (1, 1))
    dgate = probs * (dprob - jnp.sum(probs * dprob, -1, keepdims=True))
    thrice = dmixed.astype(float32)
    thrice = jnp.concatenate([thrice, thrice, thrice], 0).astype(bfloat16)
    dexpert = dot(share, thrice, (0, 0)).astype(bfloat16)

    unit = (iota((3 * rows, LANES), 0) == iota((3 * rows, LANES), 1)).astype(bfloat16)
    lanes = dot(split(dgate).astype(bfloat16), unit, (0, 0)).astype(bfloat16)
    for expert in range(experts):
        here = slice(expert * own, (expert + 1) * own)
        for at in range(dp):
            message_ref[at * experts + expert, :, :width] = dexpert[here]
            message_ref[at * experts + expert, :, width:] = lanes[here]


def middle(dp, parts, events, labels, gate, tower_in, bias, weight, shift):
    devices, own, width = parts.shape
    return pl.pallas_call(
        functools.partial(middle_kernel, dp),
        out_shape=pltpu.VMEM((devices, own, width + LANES), jnp.bfloat16),
        scratch_shapes=[pltpu.VMEM((devices // dp * own, width), jnp.float32)],
        compiler_params=params(),
        cost_estimate=cost(4 * 8 * tower_in.size, 2 * tower_in.size),
        name="middle",
    )(parts, events, labels, gate, in_vmem(tower_in), bias, weight, shift)


def backward_kernel(
    tasks,
    got_ref,
    every_ref,
    hidden_ref,
    pre_ref,
    second_ref,
    grad_first_ref,
    grad_second_ref,
    grad_gate_ref,
    dpre_ref,
    first_buf,
    second_buf,
    arrived_ref,
    wide_ref,
    sems,
):
    rows, width = every_ref.shape
    own = got_ref.shape[1]
    units = hidden_ref.shape[1]
    flat = rows <= 64
    across, down = units // TILE, width // TILE

    def second_copy(step):
        here = span(step, TILE)
        return pltpu.make_async_copy(
            second_buf.at[here, :], grad_second_ref.at[here, :], sems.at[step]
        )

    def first_copy(step):
        here = span(step, TILE)
        return pltpu.make_async_copy(
            first_buf.at[here, :], grad_first_ref.at[here, :], sems.at[across + step]
        )

    def second_step(step):
        here = span(step, TILE)
        second_buf[here, :] = dot(
            hidden_ref[:, here], arrived_ref[:, :width], (0, 0)
        ).astype(jnp.bfloat16)
        second_copy(step).start()

    def dpre_step(step):
        here = span(step, TILE)
        dhidden = dot(arrived_ref[:, :width], second_ref[here, :], (1, 1))
        dpre_ref[:, here] = (gelu_slope(pre_ref[:, here]) * dhidden).astype(jnp.bfloat16)

    def first_step(step):
        here = span(step, TILE)
        first_buf[here, :] = dot(every_ref[:, here], dpre_ref[...], (0, 0)).astype(jnp.bfloat16)
        first_copy(step).start()

    unpack(got_ref, wide_ref)
    arrived_ref[...] = wide_ref[...].astype(jnp.bfloat16)
    steps(across, flat, second_step)
    steps(across, flat, dpre_step)
    steps(down, flat, first_step)
    gate = dot(arrived_ref[:, width:], every_ref[...], (0, 0))
    for task in range(tasks):
        lanes = [(at * tasks + task) * own + row for at in range(3) for row in range(own)]
        grad_gate_ref[task] = sum(gate[lane : lane + 1] for lane in lanes)
    steps(across, flat, lambda step: second_copy(step).wait())
    steps(down, flat, lambda step: first_copy(step).wait())


def backward(got, every, hidden, pre, second, tasks):
    rows, width = every.shape
    units = hidden.shape[1]
    anywhere = pl.BlockSpec(memory_space=pl.ANY)
    inside = pl.BlockSpec(memory_space=pltpu.VMEM)
    return pl.pallas_call(
        functools.partial(backward_kernel, tasks),
        out_shape=[
            jax.ShapeDtypeStruct((width, units), jnp.bfloat16),
            jax.ShapeDtypeStruct((units, width), jnp.bfloat16),
            jax.ShapeDtypeStruct((tasks, 1, width), jnp.float32),
        ],
        in_specs=[inside] * 5,
        out_specs=[anywhere, anywhere, inside],
        scratch_shapes=[
            pltpu.VMEM((rows, units), jnp.bfloat16),
            pltpu.VMEM((width, units), jnp.bfloat16),
            pltpu.VMEM((units, width), jnp.bfloat16),
            pltpu.VMEM((rows, width + LANES), jnp.bfloat16),
            pltpu.VMEM((rows, width + LANES), jnp.float32),
            pltpu.SemaphoreType.DMA((units // TILE + width // TILE,)),
        ],
        compiler_params=params(),
        cost_estimate=cost(6 * rows * width * units, 6 * width * units),
        name="backward",
    )(got, every, hidden, pre, in_vmem(second))


def per_device(
    events, labels, w_in, w_out, gate_weight, tower_in, tower_bias, tower_out, tower_out_bias
):
    dp = lax.axis_size("dp")
    devices = dp * lax.axis_size("expert")
    tasks = tower_in.shape[0]
    gate = jnp.transpose(gate_weight, (0, 2, 1))

    got = lax.all_to_all(spread(events, devices), BOTH, 0, 0, tiled=True)
    part, every, pre, hidden = forward(got, w_in[0], w_out[0])

    parts = lax.all_to_all(part, BOTH, 0, 0, tiled=True)
    message = middle(
        dp, parts, events, labels, gate, tower_in, tower_bias, tower_out, tower_out_bias[None]
    )

    got = lax.all_to_all(message, BOTH, 0, 0, tiled=True)
    grad_first, grad_second, grad_gate = backward(got, every, hidden, pre, w_out[0], tasks)
    return (grad_first[None], grad_second[None], jnp.transpose(grad_gate, (0, 2, 1)))


def solution(mesh):
    placed = (
        P(BOTH, None),
        P(BOTH, None),
        P("expert", None, "dp"),
        P("expert", "dp", None),
        P(),
        P(),
        P(),
        P(),
        P(),
    )
    return jax.shard_map(
        per_device,
        mesh=mesh,
        in_specs=placed,
        out_specs=(P("expert", None, "dp"), P("expert", "dp", None), P(None, None, "expert")),
        check_vma=False,
    )
```

time: 51.7 us -> 43.9 us (0.85)
  blocking collectives: 10.1 us -> 34.9 us
  starting transfers between devices: 11.3 us -> 0 us
  waiting for transfers between devices: 9.25 us -> 0 us
  local copies, waits for them, and re-layouts: 5.66 us -> 0.88 us
  matrix products: 4.53 us -> 0 us
  Pallas kernels: 8.6 us -> 7.15 us
  other arithmetic: 1.11 us -> 0 us
    all_to_all x1 -> x3, blocking collectives: 10.1 us -> 34.9 us  [the longest x1 14.8 us: per_device(): got = lax.all_to_all(spread(events, devices), BOTH, 0, 0, tiled=True)]
    all_to_all x2 -> x0, starting transfers between devices: 11.3 us -> none  [the longest x1 7.3 us: per_device(): lax.all_to_all(spread(events, devices), BOTH, 0, 0, tiled=True)]
    all_to_all x2 -> x0, waiting for transfers between devices: 9.25 us -> none  [the longest x1 7.39 us: per_device(): parts = lax.all_to_all(part, BOTH, 0, 0, tiled=True)]
    dot_general x3 -> x0, matrix products: 4.53 us -> none  [the longest x1 2.23 us: per_device(): jnp.einsum('trk,tdk->trd', stacked, tower_in, preferred_element_type=jnp....]
    unnamed x23 -> x20, local copies, waits for them, and re-layouts: 5.25 us -> 0.88 us
    pallas_call x3, Pallas kernels: 5.09 us -> 3.63 us  [the longest x1 2.67 us: middle(): pl.pallas_call(functools.partial(middle_kernel, dp), out_shape=pltpu.VMEM...]
    reduce_sum x6 -> x0, other arithmetic: 0.71 us -> none  [the longest x1 0.16 us: per_device(): probs = jax.nn.softmax(gate_logits, axis=-1)]
  transfers between devices with their start and end apart: 2 -> 0, of which waited for: 2 -> 0; matrix products, arithmetic and copies ran while one was open for 1% -> 0% of each run, Pallas kernels for 6% -> 0%
where the time goes in v7:
time: 43.9 us; the launch traced here: 43.7 us
  blocking collectives  34.9 us (79%)
  Pallas kernels  7.15 us (16%)
  local copies, waits for them, and re-layouts  0.88 us (2%)
  between operations  0.76 us (2%)
    all_to_all x1, blocking collectives, per_device(): got = lax.all_to_all(spread(events, devices), BOTH, 0, 0, tiled=True)  14.8 us
    all_to_all x1, blocking collectives, per_device(): got = lax.all_to_all(message, BOTH, 0, 0, tiled=True)  10.1 us
    all_to_all x1, blocking collectives, per_device(): parts = lax.all_to_all(part, BOTH, 0, 0, tiled=True)  10 us
    pallas_call x1, Pallas kernels, backward(): pl.pallas_call(functools.partial(backward_kernel, tasks), out_shape=[jax....  3.52 us
    pallas_call x1, Pallas kernels, middle(): pl.pallas_call(functools.partial(middle_kernel, dp), out_shape=pltpu.VMEM...  2.67 us
    pallas_call x1, Pallas kernels, forward(): pl.pallas_call(forward_kernel, out_shape=[pltpu.VMEM(got.shape, jnp.bfloa...  0.95 us
    unnamed x20, local copies, waits for them, and re-layouts  0.88 us

profile of v7, /device:TPU:0, one launch (start us, length us, event | category | flops | bytes accessed | tf_op | source)
XLA Modules:
  0.0 43.7 jit_solution(6193984899322080190)
XLA Ops:
  0.6 0.0 copy-start
  0.6 0.0 copy-start.2
  0.7 0.0 copy-start.4
  0.7 0.8 %copy-done.4 = bf16[2,1024]{1,0:T(2,128)(2,1)S(1)} copy-done((bf16[2,1024]{1,0:T(2,128)(2,1)S(1)}, bf16[2,1024]{1,0:T(2,128)(2,1)}, u32[]{:S(2)}) %copy-start.4) | copy-done | bytes 4120
  1.5 14.8 %all_to_all.15.got_ref = bf16[32,2,1024]{2,1,0:T(2,128)(2,1)S(1)} all-to-all(bf16[32,2,1024]{2,1,0:T(2,128)(2,1)S(1)} %spread.1), channel_id=1, replica_groups=mesh['dp'=4,'expert'=8] {'dp','expert'}, dimensions={0} | all-to-all | bytes 262144 | tf_op jit(solution)/shard_map/all_to_all | solution.py:335
  16.3 0.0 copy-done
  16.4 0.0 copy-done.2
  16.4 0.0 copy-start.1
  16.4 0.0 copy-start.3
  16.4 0.0 copy-start.5
  16.4 0.0 copy-start.6
  16.4 0.0 copy-start.7
  16.4 0.0 copy-start.8
  16.4 0.0 copy-start.9
  16.4 0.9 %forward.1 = (bf16[32,2,1024]{2,1,0:T(2,128)(2,1)S(1)}, bf16[64,1024]{1,0:T(8,128)(2,1)S(1)}, f32[64,1024]{1,0:T(8,128)S(1)}, bf16[64,1024]{1,0:T(8,128)(2,1)S(1)}) custom-call(bf16[32,2,1024]{2,1,0:T(2,128)(2,1)S(1)} %all_to_all.15.got_ref, bf16[1024,1024]{1,0:T(8,128)(2,1)S(1)} %bitcast.9, bf16[1024,1024]{1,0:T(8,128)(2,1)S(1)} %bitcast.7), custom_call_target="tpu_custom_call" | custom-call | flops 268435456 | bytes 4194304 | tf_op jit(solution)/shard_map/forward/pallas_call | solution.py:116
  17.4 10.0 %all_to_all.16.parts_ref = bf16[32,2,1024]{2,1,0:T(2,128)(2,1)S(1)} all-to-all(bf16[32,2,1024]{2,1,0:T(2,128)(2,1)S(1)} %get-tuple-element.10), channel_id=1, replica_groups=mesh['dp'=4,'expert'=8] {'dp','expert'}, dimensions={0} | all-to-all | bytes 262144 | tf_op jit(solution)/shard_map/all_to_all | solution.py:338
  27.4 0.0 copy-done.1
  27.4 0.0 copy-done.3
  27.4 0.0 copy-done.5
  27.4 0.0 copy-done.6
  27.4 0.0 copy-done.7
  27.4 0.0 copy-done.8
  27.4 0.0 copy-done.9
  27.4 2.7 %middle.1 = bf16[32,2,1152]{2,1,0:T(2,128)(2,1)S(1)} custom-call(bf16[32,2,1024]{2,1,0:T(2,128)(2,1)S(1)} %all_to_all.16.parts_ref, bf16[2,1024]{1,0:T(2,128)(2,1)S(1)} %copy-done.5, s32[2,4]{1,0:T(2,128)S(1)} %copy-done.8, bf16[4,8,1024]{2,1,0:T(8,128)(2,1)S(1)} %bitcast.10, bf16[4,1024,256]{2,1,0:T(8,128)(2,1)S(1)} %copy-done.1, f32[4,256]{1,0:T(4,128)S(1)} %copy-done.6, ...), custom_call_target="tpu_custom_call" | custom-call | flops 33554432 | bytes 2097152 | tf_op jit(solution)/shard_map/middle/pallas_call | solution.py:224
  30.1 10.1 %all_to_all.17.got_ref = bf16[32,2,1152]{2,1,0:T(2,128)(2,1)S(1)} all-to-all(bf16[32,2,1152]{2,1,0:T(2,128)(2,1)S(1)} %middle.1), channel_id=1, replica_groups=mesh['dp'=4,'expert'=8] {'dp','expert'}, dimensions={0} | all-to-all | bytes 294912 | tf_op jit(solution)/shard_map/all_to_all | solution.py:343
  40.2 3.5 %backward.1 = (bf16[1024,1024]{1,0:T(8,128)(2,1)}, bf16[1024,1024]{1,0:T(8,128)(2,1)}, f32[4,1,1024]{2,1,0:T(1,128)}) custom-call(bf16[32,2,1152]{2,1,0:T(2,128)(2,1)S(1)} %all_to_all.17.got_ref, bf16[64,1024]{1,0:T(8,128)(2,1)S(1)} %get-tuple-element.11.every_ref, bf16[64,1024]{1,0:T(8,128)(2,1)S(1)} %get-tuple-element.12.hidden_ref, ...), custom_call_target="tpu_custom_call" | custom-call | flops 402653184 | bytes 6291456 | tf_op jit(solution)/shard_map/backward/pallas_call | solution.py:304
  (1 shorter events, 0.0 us)
Async XLA Ops:
  0.6 15.7 %copy-start = (bf16[1,1024,1024]{2,1,0:T(8,128)(2,1)S(1)}, bf16[1,1024,1024]{2,1,0:T(8,128)(2,1)}, u32[]{:S(2)}) copy-start(bf16[1,1024,1024]{2,1,0:T(8,128)(2,1)} %param.12) | copy-start | bytes 6291460
  0.6 15.7 %copy-start.2 = (bf16[1,1024,1024]{2,1,0:T(8,128)(2,1)S(1)}, bf16[1,1024,1024]{2,1,0:T(8,128)(2,1)}, u32[]{:S(2)}) copy-start(bf16[1,1024,1024]{2,1,0:T(8,128)(2,1)} %param.11) | copy-start | bytes 6291460
  0.7 0.8 %copy-start.4 = (bf16[2,1024]{1,0:T(2,128)(2,1)S(1)}, bf16[2,1024]{1,0:T(2,128)(2,1)}, u32[]{:S(2)}) copy-start(bf16[2,1024]{1,0:T(2,128)(2,1)} %events_ref.1) | copy-start | bytes 12292
  16.4 11.0 %copy-start.1 = (bf16[4,1024,256]{2,1,0:T(8,128)(2,1)S(1)}, bf16[4,1024,256]{2,1,0:T(8,128)(2,1)}, u32[]{:S(2)}) copy-start(bf16[4,1024,256]{2,1,0:T(8,128)(2,1)} %tower_in_ref.1) | copy-start | bytes 6291460
  16.4 11.0 %copy-start.3 = (bf16[4,1024,8]{1,2,0:T(8,128)(2,1)S(1)}, bf16[4,1024,8]{1,2,0:T(8,128)(2,1)}, u32[]{:S(2)}) copy-start(bf16[4,1024,8]{1,2,0:T(8,128)(2,1)} %param.13) | copy-start | bytes 196612
  16.4 11.0 %copy-start.5 = (bf16[2,1024]{1,0:T(2,128)(2,1)S(1)}, bf16[2,1024]{1,0:T(2,128)(2,1)}, u32[]{:S(2)}) copy-start(bf16[2,1024]{1,0:T(2,128)(2,1)} %events_ref.1) | copy-start | bytes 12292
  16.4 11.0 %copy-start.6 = (f32[4,256]{1,0:T(4,128)S(1)}, f32[4,256]{1,0:T(4,128)}, u32[]{:S(2)}) copy-start(f32[4,256]{1,0:T(4,128)} %bias_ref.1) | copy-start | bytes 12292
  16.4 11.0 %copy-start.7 = (f32[4,256]{1,0:T(4,128)S(1)}, f32[4,256]{1,0:T(4,128)}, u32[]{:S(2)}) copy-start(f32[4,256]{1,0:T(4,128)} %weight_ref.1) | copy-start | bytes 12292
  16.4 11.0 %copy-start.8 = (s32[2,4]{1,0:T(2,128)S(1)}, s32[2,4]{1,0:T(2,128)}, u32[]{:S(2)}) copy-start(s32[2,4]{1,0:T(2,128)} %labels_ref.1) | copy-start | bytes 100
  16.4 11.0 %copy-start.9 = (f32[4]{0:T(128)S(1)}, f32[4]{0:T(128)}, u32[]{:S(2)}) copy-start(f32[4]{0:T(128)} %param.17) | copy-start | bytes 52

commit v8 on v7

v8 whole, which is shorter than its diff:
```python
import functools

import jax
import jax.numpy as jnp
from jax import lax
from jax.experimental import pallas as pl
from jax.experimental.pallas import tpu as pltpu
from jax.sharding import PartitionSpec as P

BOTH = ("dp", "expert")
LANES = 128
TILE = 256
GELU_C = 0.7978845608028654
GELU_A = 0.044715
AHEAD_FLOPS = 1 << 34
VMEM_LIMIT = 32 * 1024 * 1024


def gelu_pair(value):
    square = value * value
    bend = jnp.tanh(GELU_C * (value + GELU_A * value * square))
    inner = GELU_C * (1.0 + 3.0 * GELU_A * square)
    half = 0.5 * (1.0 + bend)
    return value * half, half + 0.5 * value * (1.0 - bend * bend) * inner


def pieces_of(value):
    high = value.astype(jnp.bfloat16)
    rest = value - high.astype(jnp.float32)
    middle = rest.astype(jnp.bfloat16)
    low = (rest - middle.astype(jnp.float32)).astype(jnp.bfloat16)
    return high, middle, low


def dot(left, right, over):
    return lax.dot_general(
        left, right, ((over[:1], over[1:]), ((), ())), preferred_element_type=jnp.float32
    )


def steps(count, flat, body):
    if flat:
        for step in range(count):
            body(step)
    else:
        lax.fori_loop(0, count, lambda step, none: (body(step), none)[1], None)


def span(step, size):
    return pl.ds(pl.multiple_of(step * size, size), size)


def params():
    return pltpu.CompilerParams(vmem_limit_bytes=VMEM_LIMIT)


def cost(flops, moved):
    return pl.CostEstimate(flops=flops, bytes_accessed=moved, transcendentals=0)


def in_vmem(value):
    return pltpu.with_memory_space_constraint(value, pltpu.VMEM)


def spread_kernel(row_ref, out_ref):
    for step in range(out_ref.shape[0]):
        out_ref[step] = row_ref[...]


def spread(value, devices):
    return pl.pallas_call(
        spread_kernel,
        out_shape=pltpu.VMEM((devices, *value.shape), value.dtype),
        compiler_params=params(),
        cost_estimate=cost(AHEAD_FLOPS, 0),
        name="spread",
    )(value)


def unpack(message_ref, rows_ref):
    own = message_ref.shape[1]
    for at in range(message_ref.shape[0]):
        rows_ref[at * own : (at + 1) * own, :] = message_ref[at].astype(jnp.float32)


def iota(shape, axis):
    return lax.broadcasted_iota(jnp.int32, shape, axis)


def by_key(value_of, rows, wide, key_of_row, keys):
    key = key_of_row(iota((rows, wide), 0))
    result = jnp.zeros((rows, wide), jnp.float32)
    for at in range(keys):
        result = jnp.where(key == at, value_of(at), result)
    return result


def split(value):
    return jnp.concatenate([piece.astype(jnp.float32) for piece in pieces_of(value)], 0)


def forward_kernel(
    got_ref,
    events_ref,
    gate_ref,
    first_ref,
    second_ref,
    part_ref,
    every_ref,
    every_turned_ref,
    hidden_turned_ref,
    slope_ref,
    share_ref,
    share_turned_ref,
    wide_ref,
):
    own = got_ref.shape[1]
    rows, width = every_ref.shape
    chunk = min(rows, LANES)
    unpack(got_ref, wide_ref)

    def body(step):
        here = span(step, chunk)
        wide = wide_ref[here, :]
        every = wide.astype(jnp.bfloat16)
        every_ref[here, :] = every
        every_turned_ref[:, here] = wide.T.astype(jnp.bfloat16)
        pre = dot(every, first_ref[...], (1, 0))
        hidden, slope = gelu_pair(pre)
        part = dot(hidden.astype(jnp.bfloat16), second_ref[...], (1, 0)).astype(jnp.bfloat16)
        for at in range(chunk // own):
            part_ref[step * (chunk // own) + at] = part[at * own : (at + 1) * own]
        slope_ref[here, :] = slope
        hidden_turned_ref[:, here] = hidden.T.astype(jnp.bfloat16)

    steps(rows // chunk, rows == chunk, body)

    tasks, experts, _ = gate_ref.shape
    pairs, slots = tasks * own, experts * own
    events = events_ref[...].astype(jnp.float32)
    events = by_key(
        lambda row: events[row : row + 1], pairs, width, lambda at: lax.rem(at, own), own
    ).astype(jnp.bfloat16)
    gates = by_key(
        lambda task: dot(events, gate_ref[task], (1, 1)), pairs, experts, lambda at: at // own, tasks
    )
    gates = jnp.exp(gates - jnp.max(gates, -1, keepdims=True))
    gates = gates / jnp.sum(gates, -1, keepdims=True)
    gates = split(gates).astype(jnp.bfloat16)
    place = (iota((experts, slots), 0) == iota((experts, slots), 1) // own).astype(jnp.bfloat16)

    def same(shape):
        return lax.rem(iota(shape, 0), own) == lax.rem(iota(shape, 1), own)

    share_ref[...] = jnp.where(same((3 * pairs, slots)), dot(gates, place, (1, 0)), 0.0)
    share_turned_ref[...] = jnp.where(same((slots, 3 * pairs)), dot(place, gates, (0, 1)), 0.0)


def forward(got, events, gate, first, second):
    devices, own, width = got.shape
    rows = devices * own
    units = first.shape[1]
    pairs, slots = gate.shape[0] * own, gate.shape[1] * own
    return pl.pallas_call(
        forward_kernel,
        out_shape=[
            pltpu.VMEM(got.shape, jnp.bfloat16),
            pltpu.VMEM((rows, width), jnp.bfloat16),
            pltpu.VMEM((width, rows), jnp.bfloat16),
            pltpu.VMEM((units, rows), jnp.bfloat16),
            pltpu.VMEM((rows, units), jnp.float32),
            pltpu.VMEM((3 * pairs, slots), jnp.float32),
            pltpu.VMEM((slots, 3 * pairs), jnp.float32),
        ],
        scratch_shapes=[pltpu.VMEM((rows, width), jnp.float32)],
        compiler_params=params(),
        cost_estimate=cost(4 * rows * width * units, 4 * width * units),
        name="forward",
    )(got, events, gate, in_vmem(first), in_vmem(second))


def middle_kernel(
    dp,
    parts_ref,
    share_ref,
    share_turned_ref,
    labels_ref,
    tower_in_ref,
    bias_ref,
    weight_ref,
    shift_ref,
    message_ref,
    outs_ref,
):
    devices, own, width = parts_ref.shape
    experts = devices // dp
    tasks, _, units = tower_in_ref.shape
    pairs = tasks * own
    float32, bfloat16 = jnp.float32, jnp.bfloat16

    def of_task(value_of, wide):
        return by_key(value_of, pairs, wide, lambda at: at // own, tasks)

    def fold(value):
        return value[:pairs] + value[pairs : 2 * pairs] + value[2 * pairs :]

    def only(value, task):
        at = lax.rem(iota(value.shape, 0), pairs) // own
        return jnp.where(at == task, value, 0.0).astype(bfloat16)

    for expert in range(experts):
        total = parts_ref[expert].astype(float32)
        for at in range(1, dp):
            total = total + parts_ref[at * experts + expert].astype(float32)
        outs_ref[expert * own : (expert + 1) * own, :] = total
    outs = outs_ref[...].astype(bfloat16)

    share = share_ref[...].astype(bfloat16)
    mixed = fold(dot(share, outs, (1, 0))).astype(bfloat16).astype(float32)
    tower = of_task(lambda task: bias_ref[task : task + 1, :], units)
    weight = of_task(lambda task: weight_ref[task : task + 1, :], units)
    shift = of_task(lambda task: shift_ref[:, task : task + 1], 1)
    labels = labels_ref[...].astype(float32)
    labels = by_key(lambda row: labels[row : row + 1], pairs, tasks, lambda at: lax.rem(at, own), own)
    pick = iota((pairs, tasks), 0) // own == iota((pairs, tasks), 1)
    target = jnp.sum(jnp.where(pick, labels, 0.0), -1, keepdims=True)
    for task in range(tasks):
        tower = tower + dot(only(mixed, task), tower_in_ref[task], (1, 0))
    active, slope = gelu_pair(tower)
    logit = jnp.sum(active * weight, -1, keepdims=True) + shift
    dlogit = jax.nn.sigmoid(logit) - target
    stack = split(slope * weight * dlogit)
    wide = dot(only(stack, 0), tower_in_ref[0], (1, 1))
    for task in range(1, tasks):
        wide = wide + dot(only(stack, task), tower_in_ref[task], (1, 1))
    dmixed = fold(wide).astype(bfloat16).astype(float32)
    thrice = jnp.concatenate([dmixed, dmixed, dmixed], 0).astype(bfloat16)

    turned = share_turned_ref[...]
    dexpert = dot(turned.astype(bfloat16), thrice, (1, 0)).astype(bfloat16)
    dprob = dot(outs, thrice, (1, 1))
    probs = turned[:, :pairs] + turned[:, pairs : 2 * pairs] + turned[:, 2 * pairs :]
    probs = jnp.concatenate([probs, probs, probs], 1)
    dgate = probs * (dprob - jnp.sum(probs * dprob, 0, keepdims=True))
    high, middle, low = pieces_of(dgate)
    group = iota(dgate.shape, 1) // pairs
    lanes = jnp.where(group == 1, middle.astype(float32), low.astype(float32))
    lanes = jnp.where(group == 0, high.astype(float32), lanes)
    lanes = jnp.concatenate([lanes, jnp.zeros((lanes.shape[0], LANES - 3 * pairs), float32)], 1)
    lanes = lanes.astype(bfloat16)
    for expert in range(experts):
        here = slice(expert * own, (expert + 1) * own)
        for at in range(dp):
            message_ref[at * experts + expert, :, :width] = dexpert[here]
            message_ref[at * experts + expert, :, width:] = lanes[here]


def middle(dp, parts, share, share_turned, labels, tower_in, bias, weight, shift):
    devices, own, width = parts.shape
    return pl.pallas_call(
        functools.partial(middle_kernel, dp),
        out_shape=pltpu.VMEM((devices, own, width + LANES), jnp.bfloat16),
        scratch_shapes=[pltpu.VMEM((devices // dp * own, width), jnp.float32)],
        compiler_params=params(),
        cost_estimate=cost(4 * 8 * tower_in.size, 2 * tower_in.size),
        name="middle",
    )(parts, share, share_turned, labels, in_vmem(tower_in), bias, weight, shift)


def backward_kernel(
    tasks,
    got_ref,
    every_ref,
    every_turned_ref,
    hidden_turned_ref,
    slope_ref,
    second_ref,
    grad_first_ref,
    grad_second_ref,
    grad_gate_ref,
    dpre_ref,
    first_buf,
    second_buf,
    arrived_ref,
    wide_ref,
    sems,
):
    rows, width = every_ref.shape
    own = got_ref.shape[1]
    units = slope_ref.shape[1]
    flat = rows <= LANES
    across, down = units // TILE, width // TILE

    def second_copy(step):
        here = span(step, TILE)
        return pltpu.make_async_copy(
            second_buf.at[here, :], grad_second_ref.at[here, :], sems.at[step]
        )

    def first_copy(step):
        here = span(step, TILE)
        return pltpu.make_async_copy(
            first_buf.at[here, :], grad_first_ref.at[here, :], sems.at[across + step]
        )

    def second_step(step):
        here = span(step, TILE)
        second_buf[here, :] = dot(
            hidden_turned_ref[here, :], arrived_ref[:, :width], (1, 0)
        ).astype(jnp.bfloat16)
        second_copy(step).start()

    def dpre_step(step):
        here = span(step, TILE)
        dhidden = dot(arrived_ref[:, :width], second_ref[here, :], (1, 1))
        dpre_ref[:, here] = (slope_ref[:, here] * dhidden).astype(jnp.bfloat16)

    def first_step(step):
        here = span(step, TILE)
        first_buf[here, :] = dot(
            every_turned_ref[here, :], dpre_ref[...], (1, 0)
        ).astype(jnp.bfloat16)
        first_copy(step).start()

    unpack(got_ref, wide_ref)
    arrived_ref[...] = wide_ref[...].astype(jnp.bfloat16)
    steps(across, flat, second_step)
    steps(across, flat, dpre_step)
    steps(down, flat, first_step)
    gate = dot(arrived_ref[:, width:], every_ref[...], (0, 0))
    for task in range(tasks):
        lanes = [(at * tasks + task) * own + row for at in range(3) for row in range(own)]
        grad_gate_ref[task] = sum(gate[lane : lane + 1] for lane in lanes)
    steps(across, flat, lambda step: second_copy(step).wait())
    steps(down, flat, lambda step: first_copy(step).wait())


def backward(got, every, every_turned, hidden_turned, slope, second, tasks):
    rows, width = every.shape
    units = slope.shape[1]
    anywhere = pl.BlockSpec(memory_space=pl.ANY)
    inside = pl.BlockSpec(memory_space=pltpu.VMEM)
    return pl.pallas_call(
        functools.partial(backward_kernel, tasks),
        out_shape=[
            jax.ShapeDtypeStruct((width, units), jnp.bfloat16),
            jax.ShapeDtypeStruct((units, width), jnp.bfloat16),
            jax.ShapeDtypeStruct((tasks, 1, width), jnp.float32),
        ],
        in_specs=[inside] * 6,
        out_specs=[anywhere, anywhere, inside],
        scratch_shapes=[
            pltpu.VMEM((rows, units), jnp.bfloat16),
            pltpu.VMEM((width, units), jnp.bfloat16),
            pltpu.VMEM((units, width), jnp.bfloat16),
            pltpu.VMEM((rows, width + LANES), jnp.bfloat16),
            pltpu.VMEM((rows, width + LANES), jnp.float32),
            pltpu.SemaphoreType.DMA((units // TILE + width // TILE,)),
        ],
        compiler_params=params(),
        cost_estimate=cost(6 * rows * width * units, 6 * width * units),
        name="backward",
    )(got, every, every_turned, hidden_turned, slope, in_vmem(second))


def per_device(
    events, labels, w_in, w_out, gate_weight, tower_in, tower_bias, tower_out, tower_out_bias
):
    dp = lax.axis_size("dp")
    devices = dp * lax.axis_size("expert")
    tasks = tower_in.shape[0]
    gate = jnp.transpose(gate_weight, (0, 2, 1))

    got = lax.all_to_all(spread(events, devices), BOTH, 0, 0, tiled=True)
    part, every, every_turned, hidden_turned, slope, share, share_turned = forward(
        got, events, gate, w_in[0], w_out[0]
    )

    parts = lax.all_to_all(part, BOTH, 0, 0, tiled=True)
    message = middle(
        dp, parts, share, share_turned, labels, tower_in, tower_bias, tower_out, tower_out_bias[None]
    )

    got = lax.all_to_all(message, BOTH, 0, 0, tiled=True)
    grad_first, grad_second, grad_gate = backward(
        got, every, every_turned, hidden_turned, slope, w_out[0], tasks
    )
    return (grad_first[None], grad_second[None], jnp.transpose(grad_gate, (0, 2, 1)))


def solution(mesh):
    placed = (
        P(BOTH, None),
        P(BOTH, None),
        P("expert", None, "dp"),
        P("expert", "dp", None),
        P(),
        P(),
        P(),
        P(),
        P(),
    )
    return jax.shard_map(
        per_device,
        mesh=mesh,
        in_specs=placed,
        out_specs=(P("expert", None, "dp"), P("expert", "dp", None), P(None, None, "expert")),
        check_vma=False,
    )
```

time: 43.9 us -> 43.7 us (level)
    pallas_call x1, Pallas kernels: 2.67 us -> 2.02 us  [middle(): pl.pallas_call(functools.partial(middle_kernel, dp), out_shape=pltpu.VMEM...]
    pallas_call x1, Pallas kernels: 0.95 us -> 1.41 us  [forward(): pl.pallas_call(forward_kernel, out_shape=[pltpu.VMEM(got.shape, jnp.bfloa...]
    unnamed x20 -> x18, local copies, waits for them, and re-layouts: 0.88 us -> 0.87 us
where the time goes in v8:
time: 43.7 us; the launch traced here: 43.5 us
  blocking collectives  34.9 us (80%)
  Pallas kernels  6.96 us (16%)
  local copies, waits for them, and re-layouts  0.87 us (2%)
  between operations  0.74 us (2%)
    all_to_all x1, blocking collectives, per_device(): got = lax.all_to_all(spread(events, devices), BOTH, 0, 0, tiled=True)  14.8 us
    all_to_all x1, blocking collectives, per_device(): got = lax.all_to_all(message, BOTH, 0, 0, tiled=True)  10.1 us
    all_to_all x1, blocking collectives, per_device(): parts = lax.all_to_all(part, BOTH, 0, 0, tiled=True)  9.99 us
    pallas_call x1, Pallas kernels, backward(): pl.pallas_call(functools.partial(backward_kernel, tasks), out_shape=[jax....  3.52 us
    pallas_call x1, Pallas kernels, middle(): pl.pallas_call(functools.partial(middle_kernel, dp), out_shape=pltpu.VMEM...  2.02 us
    pallas_call x1, Pallas kernels, forward(): pl.pallas_call(forward_kernel, out_shape=[pltpu.VMEM(got.shape, jnp.bfloa...  1.41 us
    unnamed x18, local copies, waits for them, and re-layouts  0.87 us

profile of v8, /device:TPU:0, one launch (start us, length us, event | category | flops | bytes accessed | tf_op | source)
XLA Modules:
  0.0 43.5 jit_solution(798560122597631224)
XLA Ops:
  0.6 0.0 copy-start.3
  0.6 0.0 copy-start
  0.7 0.0 copy-start.1
  0.7 0.0 copy-start.4
  0.7 0.8 %copy-done.4 = bf16[2,1024]{1,0:T(2,128)(2,1)S(1)} copy-done((bf16[2,1024]{1,0:T(2,128)(2,1)S(1)}, bf16[2,1024]{1,0:T(2,128)(2,1)}, u32[]{:S(2)}) %copy-start.4) | copy-done | bytes 4120
  1.5 14.8 %all_to_all.15.got_ref = bf16[32,2,1024]{2,1,0:T(2,128)(2,1)S(1)} all-to-all(bf16[32,2,1024]{2,1,0:T(2,128)(2,1)S(1)} %spread.1), channel_id=1, replica_groups=mesh['dp'=4,'expert'=8] {'dp','expert'}, dimensions={0} | all-to-all | bytes 262144 | tf_op jit(solution)/shard_map/all_to_all | solution.py:374
  16.4 0.0 copy-done.3
  16.4 0.0 copy-done
  16.4 0.0 copy-done.1
  16.4 0.0 copy-start.2
  16.4 0.0 copy-start.5
  16.4 0.0 copy-start.6
  16.4 0.0 copy-start.7
  16.4 0.0 copy-start.8
  16.4 1.4 %forward.1 = (bf16[32,2,1024]{2,1,0:T(2,128)(2,1)S(1)}, bf16[64,1024]{1,0:T(8,128)(2,1)S(1)}, bf16[1024,64]{1,0:T(8,128)(2,1)S(1)}, bf16[1024,64]{1,0:T(8,128)(2...) custom-call(bf16[32,2,1024]{2,1,0:T(2,128)(2,1)S(1)} %all_to_all.15.got_ref, ...), custom_call_target="tpu_custom_call" | custom-call | flops 268435456 | bytes 4194304 | tf_op jit(solution)/shard_map/forward/pallas_call | solution.py:164
  17.8 10.0 %all_to_all.16.parts_ref = bf16[32,2,1024]{2,1,0:T(2,128)(2,1)S(1)} all-to-all(bf16[32,2,1024]{2,1,0:T(2,128)(2,1)S(1)} %get-tuple-element.13), channel_id=1, replica_groups=mesh['dp'=4,'expert'=8] {'dp','expert'}, dimensions={0} | all-to-all | bytes 262144 | tf_op jit(solution)/shard_map/all_to_all | solution.py:379
  27.8 0.0 copy-done.2
  27.8 0.0 copy-done.5
  27.8 0.0 copy-done.6
  27.8 0.0 copy-done.7
  27.8 0.0 copy-done.8
  27.9 2.0 %middle.1 = bf16[32,2,1152]{2,1,0:T(2,128)(2,1)S(1)} custom-call(bf16[32,2,1024]{2,1,0:T(2,128)(2,1)S(1)} %all_to_all.16.parts_ref, f32[24,16]{1,0:T(8,128)S(1)} %get-tuple-element.14.share_ref, f32[16,24]{1,0:T(8,128)S(1)} %get-tuple-element.15.share_turned_ref, s32[2,4]{1,0:T(2,128)S(1)} %copy-done.7, bf16[4,1024,256]{2,1,0:T(8,128)(2,1)S(1)} %copy-done.2, ...), custom_call_target="tpu_custom_call" | custom-call | flops 33554432 | bytes 2097152 | tf_op jit(solution)/shard_map/middle/pallas_call | solution.py:260
  29.9 10.1 %all_to_all.17.got_ref = bf16[32,2,1152]{2,1,0:T(2,128)(2,1)S(1)} all-to-all(bf16[32,2,1152]{2,1,0:T(2,128)(2,1)S(1)} %middle.1), channel_id=1, replica_groups=mesh['dp'=4,'expert'=8] {'dp','expert'}, dimensions={0} | all-to-all | bytes 294912 | tf_op jit(solution)/shard_map/all_to_all | solution.py:384
  40.0 3.5 %backward.1 = (bf16[1024,1024]{1,0:T(8,128)(2,1)}, bf16[1024,1024]{1,0:T(8,128)(2,1)}, f32[4,1,1024]{2,1,0:T(1,128)}) custom-call(bf16[32,2,1152]{2,1,0:T(2,128)(2,1)S(1)} %all_to_all.17.got_ref, bf16[64,1024]{1,0:T(8,128)(2,1)S(1)} %get-tuple-element.16.every_ref, bf16[1024,64]{1,0:T(8,128)(2,1)S(1)} %get-tuple-element.17.every_turned_ref, ...), custom_call_target="tpu_custom_call" | custom-call | flops 402653184 | bytes 6291456 | tf_op jit(solution)/shard_map/backward/pallas_call | solution.py:343
  (1 shorter events, 0.0 us)
Async XLA Ops:
  0.6 15.7 %copy-start.3 = (bf16[4,1024,8]{1,2,0:T(8,128)(2,1)S(1)}, bf16[4,1024,8]{1,2,0:T(8,128)(2,1)}, u32[]{:S(2)}) copy-start(bf16[4,1024,8]{1,2,0:T(8,128)(2,1)} %param.13) | copy-start | bytes 196612
  0.6 15.7 %copy-start = (bf16[1,1024,1024]{2,1,0:T(8,128)(2,1)S(1)}, bf16[1,1024,1024]{2,1,0:T(8,128)(2,1)}, u32[]{:S(2)}) copy-start(bf16[1,1024,1024]{2,1,0:T(8,128)(2,1)} %param.12) | copy-start | bytes 6291460
  0.7 15.7 %copy-start.1 = (bf16[1,1024,1024]{2,1,0:T(8,128)(2,1)S(1)}, bf16[1,1024,1024]{2,1,0:T(8,128)(2,1)}, u32[]{:S(2)}) copy-start(bf16[1,1024,1024]{2,1,0:T(8,128)(2,1)} %param.11) | copy-start | bytes 6291460
  0.7 0.8 %copy-start.4 = (bf16[2,1024]{1,0:T(2,128)(2,1)S(1)}, bf16[2,1024]{1,0:T(2,128)(2,1)}, u32[]{:S(2)}) copy-start(bf16[2,1024]{1,0:T(2,128)(2,1)} %events_ref.1) | copy-start | bytes 12292
  16.4 11.5 %copy-start.2 = (bf16[4,1024,256]{2,1,0:T(8,128)(2,1)S(1)}, bf16[4,1024,256]{2,1,0:T(8,128)(2,1)}, u32[]{:S(2)}) copy-start(bf16[4,1024,256]{2,1,0:T(8,128)(2,1)} %tower_in_ref.1) | copy-start | bytes 6291460
  16.4 11.5 %copy-start.5 = (f32[4,256]{1,0:T(4,128)S(1)}, f32[4,256]{1,0:T(4,128)}, u32[]{:S(2)}) copy-start(f32[4,256]{1,0:T(4,128)} %bias_ref.1) | copy-start | bytes 12292
  16.4 11.4 %copy-start.6 = (f32[4,256]{1,0:T(4,128)S(1)}, f32[4,256]{1,0:T(4,128)}, u32[]{:S(2)}) copy-start(f32[4,256]{1,0:T(4,128)} %weight_ref.1) | copy-start | bytes 12292
  16.4 11.4 %copy-start.7 = (s32[2,4]{1,0:T(2,128)S(1)}, s32[2,4]{1,0:T(2,128)}, u32[]{:S(2)}) copy-start(s32[2,4]{1,0:T(2,128)} %labels_ref.1) | copy-start | bytes 100
  16.4 11.4 %copy-start.8 = (f32[4]{0:T(128)S(1)}, f32[4]{0:T(128)}, u32[]{:S(2)}) copy-start(f32[4]{0:T(128)} %param.17) | copy-start | bytes 52

commit v9 on v8

--- a/solution.py
+++ b/solution.py
@@ -107,31 +107,28 @@
     second_ref,
     part_ref,
     every_ref,
-    every_turned_ref,
-    hidden_turned_ref,
-    slope_ref,
+    pre_ref,
+    hidden_ref,
     share_ref,
     share_turned_ref,
     wide_ref,
 ):
     own = got_ref.shape[1]
     rows, width = every_ref.shape
-    chunk = min(rows, LANES)
+    chunk = min(rows, 64)
     unpack(got_ref, wide_ref)
 
     def body(step):
         here = span(step, chunk)
-        wide = wide_ref[here, :]
-        every = wide.astype(jnp.bfloat16)
+        every = wide_ref[here, :].astype(jnp.bfloat16)
         every_ref[here, :] = every
-        every_turned_ref[:, here] = wide.T.astype(jnp.bfloat16)
         pre = dot(every, first_ref[...], (1, 0))
-        hidden, slope = gelu_pair(pre)
-        part = dot(hidden.astype(jnp.bfloat16), second_ref[...], (1, 0)).astype(jnp.bfloat16)
+        hidden = gelu_pair(pre)[0].astype(jnp.bfloat16)
+        part = dot(hidden, second_ref[...], (1, 0)).astype(jnp.bfloat16)
         for at in range(chunk // own):
             part_ref[step * (chunk // own) + at] = part[at * own : (at + 1) * own]
-        slope_ref[here, :] = slope
-        hidden_turned_ref[:, here] = hidden.T.astype(jnp.bfloat16)
+        pre_ref[here, :] = pre
+        hidden_ref[here, :] = hidden
 
     steps(rows // chunk, rows == chunk, body)
 
@@ -166,9 +163,8 @@
         out_shape=[
             pltpu.VMEM(got.shape, jnp.bfloat16),
             pltpu.VMEM((rows, width), jnp.bfloat16),
-            pltpu.VMEM((width, rows), jnp.bfloat16),
-            pltpu.VMEM((units, rows), jnp.bfloat16),
             pltpu.VMEM((rows, units), jnp.float32),
+            pltpu.VMEM((rows, units), jnp.bfloat16),
             pltpu.VMEM((3 * pairs, slots), jnp.float32),
             pltpu.VMEM((slots, 3 * pairs), jnp.float32),
         ],
@@ -271,9 +267,8 @@
     tasks,
     got_ref,
     every_ref,
-    every_turned_ref,
-    hidden_turned_ref,
-    slope_ref,
+    hidden_ref,
+    pre_ref,
     second_ref,
     grad_first_ref,
     grad_second_ref,
@@ -287,45 +282,47 @@
 ):
     rows, width = every_ref.shape
     own = got_ref.shape[1]
-    units = slope_ref.shape[1]
-    flat = rows <= LANES
-    across, down = units // TILE, width // TILE
+    units = pre_ref.shape[1]
+    flat = rows <= 64
+    across, down = units // LANES, width // LANES
 
     def second_copy(step):
-        here = span(step, TILE)
+        here = span(step, LANES)
         return pltpu.make_async_copy(
             second_buf.at[here, :], grad_second_ref.at[here, :], sems.at[step]
         )
 
     def first_copy(step):
-        here = span(step, TILE)
+        here = span(step, LANES)
         return pltpu.make_async_copy(
             first_buf.at[here, :], grad_first_ref.at[here, :], sems.at[across + step]
         )
 
     def second_step(step):
-        here = span(step, TILE)
-        second_buf[here, :] = dot(
-            hidden_turned_ref[here, :], arrived_ref[:, :width], (1, 0)
-        ).astype(jnp.bfloat16)
+        here = span(step, LANES)
+        for at in range(width // TILE):
+            there = span(at, TILE)
+            tile = dot(hidden_ref[:, here], arrived_ref[:, there], (0, 0))
+            second_buf[here, there] = tile.astype(jnp.bfloat16)
         second_copy(step).start()
 
     def dpre_step(step):
         here = span(step, TILE)
         dhidden = dot(arrived_ref[:, :width], second_ref[here, :], (1, 1))
-        dpre_ref[:, here] = (slope_ref[:, here] * dhidden).astype(jnp.bfloat16)
+        dpre_ref[:, here] = (gelu_pair(pre_ref[:, here])[1] * dhidden).astype(jnp.bfloat16)
 
     def first_step(step):
-        here = span(step, TILE)
-        first_buf[here, :] = dot(
-            every_turned_ref[here, :], dpre_ref[...], (1, 0)
-        ).astype(jnp.bfloat16)
+        here = span(step, LANES)
+        for at in range(units // TILE):
+            there = span(at, TILE)
+            tile = dot(every_ref[:, here], dpre_ref[:, there], (0, 0))
+            first_buf[here, there] = tile.astype(jnp.bfloat16)
         first_copy(step).start()
 
     unpack(got_ref, wide_ref)
     arrived_ref[...] = wide_ref[...].astype(jnp.bfloat16)
     steps(across, flat, second_step)
-    steps(across, flat, dpre_step)
+    steps(units // TILE, flat, dpre_step)
     steps(down, flat, first_step)
     gate = dot(arrived_ref[:, width:], every_ref[...], (0, 0))
     for task in range(tasks):
@@ -335,9 +332,9 @@
     steps(down, flat, lambda step: first_copy(step).wait())
 
 
-def backward(got, every, every_turned, hidden_turned, slope, second, tasks):
+def backward(got, every, hidden, pre, second, tasks):
     rows, width = every.shape
-    units = slope.shape[1]
+    units = pre.shape[1]
     anywhere = pl.BlockSpec(memory_space=pl.ANY)
     inside = pl.BlockSpec(memory_space=pltpu.VMEM)
     return pl.pallas_call(
@@ -347,7 +344,7 @@
             jax.ShapeDtypeStruct((units, width), jnp.bfloat16),
             jax.ShapeDtypeStruct((tasks, 1, width), jnp.float32),
         ],
-        in_specs=[inside] * 6,
+        in_specs=[inside] * 5,
         out_specs=[anywhere, anywhere, inside],
         scratch_shapes=[
             pltpu.VMEM((rows, units), jnp.bfloat16),
@@ -355,12 +352,12 @@
             pltpu.VMEM((units, width), jnp.bfloat16),
             pltpu.VMEM((rows, width + LANES), jnp.bfloat16),
             pltpu.VMEM((rows, width + LANES), jnp.float32),
-            pltpu.SemaphoreType.DMA((units // TILE + width // TILE,)),
+            pltpu.SemaphoreType.DMA((units // LANES + width // LANES,)),
         ],
         compiler_params=params(),
         cost_estimate=cost(6 * rows * width * units, 6 * width * units),
         name="backward",
-    )(got, every, every_turned, hidden_turned, slope, in_vmem(second))
+    )(got, every, hidden, pre, in_vmem(second))
 
 
 def per_device(
@@ -372,9 +369,7 @@
     gate = jnp.transpose(gate_weight, (0, 2, 1))
 
     got = lax.all_to_all(spread(events, devices), BOTH, 0, 0, tiled=True)
-    part, every, every_turned, hidden_turned, slope, share, share_turned = forward(
-        got, events, gate, w_in[0], w_out[0]
-    )
+    part, every, pre, hidden, share, share_turned = forward(got, events, gate, w_in[0], w_out[0])
 
     parts = lax.all_to_all(part, BOTH, 0, 0, tiled=True)
     message = middle(
@@ -382,9 +377,7 @@
     )
 
     got = lax.all_to_all(message, BOTH, 0, 0, tiled=True)
-    grad_first, grad_second, grad_gate = backward(
-        got, every, every_turned, hidden_turned, slope, w_out[0], tasks
-    )
+    grad_first, grad_second, grad_gate = backward(got, every, hidden, pre, w_out[0], tasks)
     return (grad_first[None], grad_second[None], jnp.transpose(grad_gate, (0, 2, 1)))
 
 

time: 43.7 us -> 43.7 us (level)
  no operation moved by 1% of the time
where the time goes in v9:
time: 43.7 us; the launch traced here: 43.5 us
  blocking collectives  35 us (80%)
  Pallas kernels  6.93 us (16%)
  local copies, waits for them, and re-layouts  0.87 us (2%)
  between operations  0.74 us (2%)
    all_to_all x1, blocking collectives, per_device(): got = lax.all_to_all(spread(events, devices), BOTH, 0, 0, tiled=True)  14.8 us
    all_to_all x1, blocking collectives, per_device(): got = lax.all_to_all(message, BOTH, 0, 0, tiled=True)  10.1 us
    all_to_all x1, blocking collectives, per_device(): parts = lax.all_to_all(part, BOTH, 0, 0, tiled=True)  10 us
    pallas_call x1, Pallas kernels, backward(): pl.pallas_call(functools.partial(backward_kernel, tasks), out_shape=[jax....  3.63 us
    pallas_call x1, Pallas kernels, middle(): pl.pallas_call(functools.partial(middle_kernel, dp), out_shape=pltpu.VMEM...  2.02 us
    pallas_call x1, Pallas kernels, forward(): pl.pallas_call(forward_kernel, out_shape=[pltpu.VMEM(got.shape, jnp.bfloa...  1.27 us
    unnamed x18, local copies, waits for them, and re-layouts  0.87 us

profile of v9, /device:TPU:0, one launch (start us, length us, event | category | flops | bytes accessed | tf_op | source)
XLA Modules:
  0.0 43.5 jit_solution(707625389851997180)
XLA Ops:
  0.6 0.0 copy-start.3
  0.6 0.0 copy-start
  0.7 0.0 copy-start.1
  0.7 0.0 copy-start.4
  0.7 0.8 %copy-done.4 = bf16[2,1024]{1,0:T(2,128)(2,1)S(1)} copy-done((bf16[2,1024]{1,0:T(2,128)(2,1)S(1)}, bf16[2,1024]{1,0:T(2,128)(2,1)}, u32[]{:S(2)}) %copy-start.4) | copy-done | bytes 4120
  1.5 14.8 %all_to_all.15.got_ref = bf16[32,2,1024]{2,1,0:T(2,128)(2,1)S(1)} all-to-all(bf16[32,2,1024]{2,1,0:T(2,128)(2,1)S(1)} %spread.1), channel_id=1, replica_groups=mesh['dp'=4,'expert'=8] {'dp','expert'}, dimensions={0} | all-to-all | bytes 262144 | tf_op jit(solution)/shard_map/all_to_all | solution.py:371
  16.4 0.0 copy-done.3
  16.4 0.0 copy-done
  16.4 0.0 copy-done.1
  16.4 0.0 copy-start.2
  16.4 0.0 copy-start.5
  16.4 0.0 copy-start.6
  16.4 0.0 copy-start.7
  16.4 0.0 copy-start.8
  16.4 1.3 %forward.1 = (bf16[32,2,1024]{2,1,0:T(2,128)(2,1)S(1)}, bf16[64,1024]{1,0:T(8,128)(2,1)S(1)}, f32[64,1024]{1,0:T(8,128)S(1)}, bf16[64,1024]{1,0:T(8,128)(2,1)S(1...) custom-call(bf16[32,2,1024]{2,1,0:T(2,128)(2,1)S(1)} %all_to_all.15.got_ref, bf16[2,1024]{1,0:T(2,128)(2,1)S(1)} %copy-done.4, ...), custom_call_target="tpu_custom_call" | custom-call | flops 268435456 | bytes 4194304 | tf_op jit(solution)/shard_map/forward/pallas_call | solution.py:161
  17.7 10.0 %all_to_all.16.parts_ref = bf16[32,2,1024]{2,1,0:T(2,128)(2,1)S(1)} all-to-all(bf16[32,2,1024]{2,1,0:T(2,128)(2,1)S(1)} %get-tuple-element.12), channel_id=1, replica_groups=mesh['dp'=4,'expert'=8] {'dp','expert'}, dimensions={0} | all-to-all | bytes 262144 | tf_op jit(solution)/shard_map/all_to_all | solution.py:374
  27.7 0.0 copy-done.2
  27.7 0.0 copy-done.5
  27.7 0.0 copy-done.6
  27.7 0.0 copy-done.7
  27.7 0.0 copy-done.8
  27.7 2.0 %middle.1 = bf16[32,2,1152]{2,1,0:T(2,128)(2,1)S(1)} custom-call(bf16[32,2,1024]{2,1,0:T(2,128)(2,1)S(1)} %all_to_all.16.parts_ref, f32[24,16]{1,0:T(8,128)S(1)} %get-tuple-element.13.share_ref, f32[16,24]{1,0:T(8,128)S(1)} %get-tuple-element.14.share_turned_ref, s32[2,4]{1,0:T(2,128)S(1)} %copy-done.7, bf16[4,1024,256]{2,1,0:T(8,128)(2,1)S(1)} %copy-done.2, ...), custom_call_target="tpu_custom_call" | custom-call | flops 33554432 | bytes 2097152 | tf_op jit(solution)/shard_map/middle/pallas_call | solution.py:256
  29.8 10.1 %all_to_all.17.got_ref = bf16[32,2,1152]{2,1,0:T(2,128)(2,1)S(1)} all-to-all(bf16[32,2,1152]{2,1,0:T(2,128)(2,1)S(1)} %middle.1), channel_id=1, replica_groups=mesh['dp'=4,'expert'=8] {'dp','expert'}, dimensions={0} | all-to-all | bytes 294912 | tf_op jit(solution)/shard_map/all_to_all | solution.py:379
  39.9 3.6 %backward.1 = (bf16[1024,1024]{1,0:T(8,128)(2,1)}, bf16[1024,1024]{1,0:T(8,128)(2,1)}, f32[4,1,1024]{2,1,0:T(1,128)}) custom-call(bf16[32,2,1152]{2,1,0:T(2,128)(2,1)S(1)} %all_to_all.17.got_ref, bf16[64,1024]{1,0:T(8,128)(2,1)S(1)} %get-tuple-element.15.every_ref, bf16[64,1024]{1,0:T(8,128)(2,1)S(1)} %get-tuple-element.16.hidden_ref, ...), custom_call_target="tpu_custom_call" | custom-call | flops 402653184 | bytes 6291456 | tf_op jit(solution)/shard_map/backward/pallas_call | solution.py:340
  (1 shorter events, 0.0 us)
Async XLA Ops:
  0.6 15.7 %copy-start.3 = (bf16[4,1024,8]{1,2,0:T(8,128)(2,1)S(1)}, bf16[4,1024,8]{1,2,0:T(8,128)(2,1)}, u32[]{:S(2)}) copy-start(bf16[4,1024,8]{1,2,0:T(8,128)(2,1)} %param.13) | copy-start | bytes 196612
  0.6 15.7 %copy-start = (bf16[1,1024,1024]{2,1,0:T(8,128)(2,1)S(1)}, bf16[1,1024,1024]{2,1,0:T(8,128)(2,1)}, u32[]{:S(2)}) copy-start(bf16[1,1024,1024]{2,1,0:T(8,128)(2,1)} %param.12) | copy-start | bytes 6291460
  0.7 15.7 %copy-start.1 = (bf16[1,1024,1024]{2,1,0:T(8,128)(2,1)S(1)}, bf16[1,1024,1024]{2,1,0:T(8,128)(2,1)}, u32[]{:S(2)}) copy-start(bf16[1,1024,1024]{2,1,0:T(8,128)(2,1)} %param.11) | copy-start | bytes 6291460
  0.7 0.8 %copy-start.4 = (bf16[2,1024]{1,0:T(2,128)(2,1)S(1)}, bf16[2,1024]{1,0:T(2,128)(2,1)}, u32[]{:S(2)}) copy-start(bf16[2,1024]{1,0:T(2,128)(2,1)} %events_ref.1) | copy-start | bytes 12292
  16.4 11.4 %copy-start.2 = (bf16[4,1024,256]{2,1,0:T(8,128)(2,1)S(1)}, bf16[4,1024,256]{2,1,0:T(8,128)(2,1)}, u32[]{:S(2)}) copy-start(bf16[4,1024,256]{2,1,0:T(8,128)(2,1)} %tower_in_ref.1) | copy-start | bytes 6291460
  16.4 11.3 %copy-start.5 = (f32[4,256]{1,0:T(4,128)S(1)}, f32[4,256]{1,0:T(4,128)}, u32[]{:S(2)}) copy-start(f32[4,256]{1,0:T(4,128)} %bias_ref.1) | copy-start | bytes 12292
  16.4 11.3 %copy-start.6 = (f32[4,256]{1,0:T(4,128)S(1)}, f32[4,256]{1,0:T(4,128)}, u32[]{:S(2)}) copy-start(f32[4,256]{1,0:T(4,128)} %weight_ref.1) | copy-start | bytes 12292
  16.4 11.3 %copy-start.7 = (s32[2,4]{1,0:T(2,128)S(1)}, s32[2,4]{1,0:T(2,128)}, u32[]{:S(2)}) copy-start(s32[2,4]{1,0:T(2,128)} %labels_ref.1) | copy-start | bytes 100
  16.4 11.3 %copy-start.8 = (f32[4]{0:T(128)S(1)}, f32[4]{0:T(128)}, u32[]{:S(2)}) copy-start(f32[4]{0:T(128)} %param.17) | copy-start | bytes 52

commit v10 on v7

v10 whole, which is shorter than its diff:
```python
import functools

import jax
import jax.numpy as jnp
from jax import lax
from jax.experimental import pallas as pl
from jax.experimental.pallas import tpu as pltpu
from jax.sharding import PartitionSpec as P

BOTH = ("dp", "expert")
LANES = 128
TILE = 256
GELU_C = 0.7978845608028654
GELU_A = 0.044715
AHEAD_FLOPS = 1 << 34
VMEM_LIMIT = 32 * 1024 * 1024


def gelu_pair(value):
    square = value * value
    bend = jnp.tanh(GELU_C * (value + GELU_A * value * square))
    inner = GELU_C * (1.0 + 3.0 * GELU_A * square)
    half = 0.5 * (1.0 + bend)
    return value * half, half + 0.5 * value * (1.0 - bend * bend) * inner


def pieces_of(value):
    high = value.astype(jnp.bfloat16)
    rest = value - high.astype(jnp.float32)
    middle = rest.astype(jnp.bfloat16)
    low = (rest - middle.astype(jnp.float32)).astype(jnp.bfloat16)
    return high, middle, low


def dot(left, right, over):
    return lax.dot_general(
        left, right, ((over[:1], over[1:]), ((), ())), preferred_element_type=jnp.float32
    )


def steps(count, flat, body):
    if flat:
        for step in range(count):
            body(step)
    else:
        lax.fori_loop(0, count, lambda step, none: (body(step), none)[1], None)


def span(step, size):
    return pl.ds(pl.multiple_of(step * size, size), size)


def params():
    return pltpu.CompilerParams(vmem_limit_bytes=VMEM_LIMIT)


def cost(flops, moved):
    return pl.CostEstimate(flops=flops, bytes_accessed=moved, transcendentals=0)


def in_vmem(value):
    return pltpu.with_memory_space_constraint(value, pltpu.VMEM)


def spread_kernel(row_ref, out_ref):
    for step in range(out_ref.shape[0]):
        out_ref[step] = row_ref[...]


def spread(value, devices):
    return pl.pallas_call(
        spread_kernel,
        out_shape=pltpu.VMEM((devices, *value.shape), value.dtype),
        compiler_params=params(),
        cost_estimate=cost(AHEAD_FLOPS, 0),
        name="spread",
    )(value)


def unpack(message_ref, rows_ref):
    own = message_ref.shape[1]
    for at in range(message_ref.shape[0]):
        rows_ref[at * own : (at + 1) * own, :] = message_ref[at].astype(jnp.float32)


def iota(shape, axis):
    return lax.broadcasted_iota(jnp.int32, shape, axis)


def by_row(value, count):
    own = value.shape[0]
    row = lax.rem(iota((count, value.shape[1]), 0), own)
    result = jnp.zeros(row.shape, jnp.float32)
    for at in range(own):
        result = jnp.where(row == at, value[at : at + 1].astype(jnp.float32), result)
    return result


def forward_kernel(
    got_ref,
    events_ref,
    gate_ref,
    first_ref,
    second_ref,
    part_ref,
    every_ref,
    pre_ref,
    hidden_ref,
    prob_ref,
    wide_ref,
):
    own = got_ref.shape[1]
    rows, width = every_ref.shape
    chunk = min(rows, 64)
    unpack(got_ref, wide_ref)

    def body(step):
        here = span(step, chunk)
        every = wide_ref[here, :].astype(jnp.bfloat16)
        every_ref[here, :] = every
        pre = dot(every, first_ref[...], (1, 0))
        hidden = gelu_pair(pre)[0].astype(jnp.bfloat16)
        part = dot(hidden, second_ref[...], (1, 0)).astype(jnp.bfloat16)
        for at in range(chunk // own):
            part_ref[step * (chunk // own) + at] = part[at * own : (at + 1) * own]
        pre_ref[here, :] = pre
        hidden_ref[here, :] = hidden

    steps(rows // chunk, rows == chunk, body)

    tasks, experts, _ = gate_ref.shape
    slots = experts * own
    events = by_row(events_ref[...], slots).astype(jnp.bfloat16)
    mine = iota((slots, experts), 0) // own == iota((slots, experts), 1)
    lane = iota((slots, LANES), 1)
    probs = jnp.zeros((slots, LANES), jnp.float32)
    for task in range(tasks):
        gates = dot(events, gate_ref[task], (1, 1))
        gates = jnp.exp(gates - jnp.max(gates, -1, keepdims=True))
        prob = jnp.sum(jnp.where(mine, gates, 0.0), -1, keepdims=True)
        probs = jnp.where(lane == task, prob / jnp.sum(gates, -1, keepdims=True), probs)
    prob_ref[...] = probs


def forward(got, events, gate, first, second):
    devices, own, width = got.shape
    rows = devices * own
    units = first.shape[1]
    return pl.pallas_call(
        forward_kernel,
        out_shape=[
            pltpu.VMEM(got.shape, jnp.bfloat16),
            pltpu.VMEM((rows, width), jnp.bfloat16),
            pltpu.VMEM((rows, units), jnp.float32),
            pltpu.VMEM((rows, units), jnp.bfloat16),
            pltpu.VMEM((gate.shape[1] * own, LANES), jnp.float32),
        ],
        scratch_shapes=[pltpu.VMEM((rows, width), jnp.float32)],
        compiler_params=params(),
        cost_estimate=cost(4 * rows * width * units, 4 * width * units),
        name="forward",
    )(got, events, gate, in_vmem(first), in_vmem(second))


def middle_kernel(
    dp,
    parts_ref,
    prob_ref,
    labels_ref,
    tower_in_ref,
    bias_ref,
    weight_ref,
    shift_ref,
    message_ref,
    outs_ref,
):
    devices, own, width = parts_ref.shape
    experts = devices // dp
    slots = experts * own
    tasks = tower_in_ref.shape[0]
    float32, bfloat16 = jnp.float32, jnp.bfloat16

    for expert in range(experts):
        total = parts_ref[expert].astype(float32)
        for at in range(1, dp):
            total = total + parts_ref[at * experts + expert].astype(float32)
        outs_ref[expert * own : (expert + 1) * own, :] = total
    outs = outs_ref[...].astype(bfloat16)
    labels = by_row(labels_ref[...], slots)
    lane = iota((slots, LANES), 1)
    lanes = jnp.zeros((slots, LANES), float32)
    dexpert = jnp.zeros((slots, width), float32)
    for task in range(tasks):
        prob = prob_ref[:, task : task + 1]
        weight = weight_ref[task : task + 1, :]
        single = dot(outs, tower_in_ref[task], (1, 0))
        linear = single * prob
        shift = own
        while shift < slots:
            linear = linear + pltpu.roll(linear, shift, 0)
            shift *= 2
        active, slope = gelu_pair(linear + bias_ref[task : task + 1, :])
        logit = jnp.sum(active * weight, -1, keepdims=True) + shift_ref[:, task : task + 1]
        dlogit = jax.nn.sigmoid(logit) - labels[:, task : task + 1]
        dtower = slope * weight * dlogit
        dgate = prob * jnp.sum(dtower * (single - linear), -1, keepdims=True)
        stack = [piece.astype(float32) for piece in pieces_of(dtower)[:2]]
        stack = jnp.concatenate(stack, 0).astype(bfloat16)
        turned = dot(stack, tower_in_ref[task], (1, 1))
        dmixed = (turned[:slots] + turned[slots:]).astype(bfloat16).astype(float32)
        dexpert = dexpert + prob * dmixed
        for at, piece in enumerate(pieces_of(dgate)):
            lanes = jnp.where(lane == at * tasks + task, piece.astype(float32), lanes)
    dexpert = dexpert.astype(bfloat16)
    lanes = lanes.astype(bfloat16)
    for expert in range(experts):
        here = slice(expert * own, (expert + 1) * own)
        for at in range(dp):
            message_ref[at * experts + expert, :, :width] = dexpert[here]
            message_ref[at * experts + expert, :, width:] = lanes[here]


def middle(dp, parts, prob, labels, tower_in, bias, weight, shift):
    devices, own, width = parts.shape
    return pl.pallas_call(
        functools.partial(middle_kernel, dp),
        out_shape=pltpu.VMEM((devices, own, width + LANES), jnp.bfloat16),
        scratch_shapes=[pltpu.VMEM((devices // dp * own, width), jnp.float32)],
        compiler_params=params(),
        cost_estimate=cost(4 * 8 * tower_in.size, 2 * tower_in.size),
        name="middle",
    )(parts, prob, labels, in_vmem(tower_in), bias, weight, shift)


def backward_kernel(
    tasks,
    got_ref,
    every_ref,
    hidden_ref,
    pre_ref,
    second_ref,
    grad_first_ref,
    grad_second_ref,
    grad_gate_ref,
    dpre_ref,
    first_buf,
    second_buf,
    gate_buf,
    arrived_ref,
    wide_ref,
    sems,
):
    rows, width = every_ref.shape
    units = pre_ref.shape[1]
    flat = rows <= 64
    across, down = units // TILE, width // TILE

    def second_copy(step):
        here = span(step, TILE)
        return pltpu.make_async_copy(
            second_buf.at[here, :], grad_second_ref.at[here, :], sems.at[step]
        )

    def first_copy(step):
        here = span(step, TILE)
        return pltpu.make_async_copy(
            first_buf.at[here, :], grad_first_ref.at[here, :], sems.at[across + step]
        )

    def second_step(step):
        here = span(step, TILE)
        second_buf[here, :] = dot(
            hidden_ref[:, here], arrived_ref[:, :width], (0, 0)
        ).astype(jnp.bfloat16)
        second_copy(step).start()

    def dpre_step(step):
        here = span(step, TILE)
        dhidden = dot(arrived_ref[:, :width], second_ref[here, :], (1, 1))
        dpre_ref[:, here] = (gelu_pair(pre_ref[:, here])[1] * dhidden).astype(jnp.bfloat16)

    def first_step(step):
        here = span(step, TILE)
        first_buf[here, :] = dot(every_ref[:, here], dpre_ref[...], (0, 0)).astype(jnp.bfloat16)
        first_copy(step).start()

    unpack(got_ref, wide_ref)
    arrived_ref[...] = wide_ref[...].astype(jnp.bfloat16)
    steps(across, flat, second_step)
    gate = dot(arrived_ref[:, width:], every_ref[...], (0, 0))
    for task in range(tasks):
        lanes = [at * tasks + task for at in range(3)]
        gate_buf[task] = sum(gate[lane : lane + 1] for lane in lanes)
    gate_copy = pltpu.make_async_copy(gate_buf, grad_gate_ref, sems.at[across + down])
    gate_copy.start()
    steps(units // TILE, flat, dpre_step)
    steps(down, flat, first_step)
    gate_copy.wait()
    steps(across, flat, lambda step: second_copy(step).wait())
    steps(down, flat, lambda step: first_copy(step).wait())


def backward(got, every, hidden, pre, second, tasks):
    rows, width = every.shape
    units = pre.shape[1]
    anywhere = pl.BlockSpec(memory_space=pl.ANY)
    inside = pl.BlockSpec(memory_space=pltpu.VMEM)
    return pl.pallas_call(
        functools.partial(backward_kernel, tasks),
        out_shape=[
            jax.ShapeDtypeStruct((width, units), jnp.bfloat16),
            jax.ShapeDtypeStruct((units, width), jnp.bfloat16),
            jax.ShapeDtypeStruct((tasks, 1, width), jnp.float32),
        ],
        in_specs=[inside] * 5,
        out_specs=[anywhere] * 3,
        scratch_shapes=[
            pltpu.VMEM((rows, units), jnp.bfloat16),
            pltpu.VMEM((width, units), jnp.bfloat16),
            pltpu.VMEM((units, width), jnp.bfloat16),
            pltpu.VMEM((tasks, 1, width), jnp.float32),
            pltpu.VMEM((rows, width + LANES), jnp.bfloat16),
            pltpu.VMEM((rows, width + LANES), jnp.float32),
            pltpu.SemaphoreType.DMA((units // TILE + width // TILE + 1,)),
        ],
        compiler_params=params(),
        cost_estimate=cost(6 * rows * width * units, 6 * width * units),
        name="backward",
    )(got, every, hidden, pre, in_vmem(second))


def per_device(
    events, labels, w_in, w_out, gate_weight, tower_in, tower_bias, tower_out, tower_out_bias
):
    dp = lax.axis_size("dp")
    devices = dp * lax.axis_size("expert")
    tasks = tower_in.shape[0]
    gate = jnp.transpose(gate_weight, (0, 2, 1))

    got = lax.all_to_all(spread(events, devices), BOTH, 0, 0, tiled=True)
    part, every, pre, hidden, prob = forward(got, events, gate, w_in[0], w_out[0])

    parts = lax.all_to_all(part, BOTH, 0, 0, tiled=True)
    message = middle(
        dp, parts, prob, labels, tower_in, tower_bias, tower_out, tower_out_bias[None]
    )

    got = lax.all_to_all(message, BOTH, 0, 0, tiled=True)
    grad_first, grad_second, grad_gate = backward(got, every, hidden, pre, w_out[0], tasks)
    return (grad_first[None], grad_second[None], jnp.transpose(grad_gate, (0, 2, 1)))


def solution(mesh):
    placed = (
        P(BOTH, None),
        P(BOTH, None),
        P("expert", None, "dp"),
        P("expert", "dp", None),
        P(),
        P(),
        P(),
        P(),
        P(),
    )
    return jax.shard_map(
        per_device,
        mesh=mesh,
        in_specs=placed,
        out_specs=(P("expert", None, "dp"), P("expert", "dp", None), P(None, None, "expert")),
        check_vma=False,
    )
```

time: 43.9 us -> 43 us (0.979)
  Pallas kernels: 7.15 us -> 6.27 us
    pallas_call x1, Pallas kernels: 2.67 us -> 2.03 us  [middle(): pl.pallas_call(functools.partial(middle_kernel, dp), out_shape=pltpu.VMEM...]
    pallas_call x1, Pallas kernels: 3.52 us -> 3.06 us  [backward(): pl.pallas_call(functools.partial(backward_kernel, tasks), out_shape=[jax....]
    unnamed x20 -> x18, local copies, waits for them, and re-layouts: 0.88 us -> 0.87 us
where the time goes in v10:
time: 43 us; the launch traced here: 42.8 us
  blocking collectives  34.9 us (81%)
  Pallas kernels  6.27 us (15%)
  local copies, waits for them, and re-layouts  0.87 us (2%)
  between operations  0.75 us (2%)
    all_to_all x1, blocking collectives, per_device(): got = lax.all_to_all(spread(events, devices), BOTH, 0, 0, tiled=True)  14.8 us
    all_to_all x1, blocking collectives, per_device(): got = lax.all_to_all(message, BOTH, 0, 0, tiled=True)  10.1 us
    all_to_all x1, blocking collectives, per_device(): parts = lax.all_to_all(part, BOTH, 0, 0, tiled=True)  10 us
    pallas_call x1, Pallas kernels, backward(): pl.pallas_call(functools.partial(backward_kernel, tasks), out_shape=[jax....  3.06 us
    pallas_call x1, Pallas kernels, middle(): pl.pallas_call(functools.partial(middle_kernel, dp), out_shape=pltpu.VMEM...  2.03 us
    pallas_call x1, Pallas kernels, forward(): pl.pallas_call(forward_kernel, out_shape=[pltpu.VMEM(got.shape, jnp.bfloa...  1.17 us
    unnamed x18, local copies, waits for them, and re-layouts  0.87 us

profile of v10, /device:TPU:0, one launch (start us, length us, event | category | flops | bytes accessed | tf_op | source)
XLA Modules:
  0.0 42.8 jit_solution(12628700009560420934)
XLA Ops:
  0.6 0.0 copy-start.3
  0.6 0.0 copy-start
  0.7 0.0 copy-start.1
  0.7 0.0 copy-start.4
  0.7 0.8 %copy-done.4 = bf16[2,1024]{1,0:T(2,128)(2,1)S(1)} copy-done((bf16[2,1024]{1,0:T(2,128)(2,1)S(1)}, bf16[2,1024]{1,0:T(2,128)(2,1)}, u32[]{:S(2)}) %copy-start.4) | copy-done | bytes 4120
  1.5 14.8 %all_to_all.15.got_ref = bf16[32,2,1024]{2,1,0:T(2,128)(2,1)S(1)} all-to-all(bf16[32,2,1024]{2,1,0:T(2,128)(2,1)S(1)} %spread.1), channel_id=1, replica_groups=mesh['dp'=4,'expert'=8] {'dp','expert'}, dimensions={0} | all-to-all | bytes 262144 | tf_op jit(solution)/shard_map/all_to_all | solution.py:340
  16.4 0.0 copy-done.3
  16.4 0.0 copy-done
  16.4 0.0 copy-done.1
  16.4 0.0 copy-start.2
  16.4 0.0 copy-start.5
  16.4 0.0 copy-start.6
  16.4 0.0 copy-start.7
  16.4 0.0 copy-start.8
  16.4 1.2 %forward.1 = (bf16[32,2,1024]{2,1,0:T(2,128)(2,1)S(1)}, bf16[64,1024]{1,0:T(8,128)(2,1)S(1)}, f32[64,1024]{1,0:T(8,128)S(1)}, bf16[64,1024]{1,0:T(8,128)(2,1)S(1)}, f32[16,128]{1,0:T(8,128)S(1)}) custom-call(bf16[32,2,1024]{2,1,0:T(2,128)(2,1)S(1)} %all_to_all.15.got_ref, bf16[2,1024]{1,0:T(2,128)(2,1)S(1)} %copy-done.4, bf16[4,8,1024]{2,1,0:T(8,128)(2,1)S(1)} %bitcast.10, ...), custom_call_target="tpu_custom_call" | custom-call | flops 268435456 | bytes 4194304 | tf_op jit(solution)/shard_map/forward/pallas_call | solution.py:149
  17.6 10.0 %all_to_all.16.parts_ref = bf16[32,2,1024]{2,1,0:T(2,128)(2,1)S(1)} all-to-all(bf16[32,2,1024]{2,1,0:T(2,128)(2,1)S(1)} %get-tuple-element.11), channel_id=1, replica_groups=mesh['dp'=4,'expert'=8] {'dp','expert'}, dimensions={0} | all-to-all | bytes 262144 | tf_op jit(solution)/shard_map/all_to_all | solution.py:343
  27.6 0.0 copy-done.2
  27.6 0.0 copy-done.5
  27.6 0.0 copy-done.6
  27.6 0.0 copy-done.7
  27.6 0.0 copy-done.8
  27.6 2.0 %middle.1 = bf16[32,2,1152]{2,1,0:T(2,128)(2,1)S(1)} custom-call(bf16[32,2,1024]{2,1,0:T(2,128)(2,1)S(1)} %all_to_all.16.parts_ref, f32[16,128]{1,0:T(8,128)S(1)} %get-tuple-element.12.prob_ref, s32[2,4]{1,0:T(2,128)S(1)} %copy-done.7, bf16[4,1024,256]{2,1,0:T(8,128)(2,1)S(1)} %copy-done.2, f32[4,256]{1,0:T(4,128)S(1)} %copy-done.5, f32[4,256]{1,0:T(4,128)S(1)} %copy-done.6, ...), custom_call_target="tpu_custom_call" | custom-call | flops 33554432 | bytes 2097152 | tf_op jit(solution)/shard_map/middle/pallas_call | solution.py:225
  29.7 10.1 %all_to_all.17.got_ref = bf16[32,2,1152]{2,1,0:T(2,128)(2,1)S(1)} all-to-all(bf16[32,2,1152]{2,1,0:T(2,128)(2,1)S(1)} %middle.1), channel_id=1, replica_groups=mesh['dp'=4,'expert'=8] {'dp','expert'}, dimensions={0} | all-to-all | bytes 294912 | tf_op jit(solution)/shard_map/all_to_all | solution.py:348
  39.8 3.1 %backward.1 = (bf16[1024,1024]{1,0:T(8,128)(2,1)}, bf16[1024,1024]{1,0:T(8,128)(2,1)}, f32[4,1,1024]{2,1,0:T(1,128)}) custom-call(bf16[32,2,1152]{2,1,0:T(2,128)(2,1)S(1)} %all_to_all.17.got_ref, bf16[64,1024]{1,0:T(8,128)(2,1)S(1)} %get-tuple-element.13.every_ref, bf16[64,1024]{1,0:T(8,128)(2,1)S(1)} %get-tuple-element.14.hidden_ref, ...), custom_call_target="tpu_custom_call" | custom-call | flops 402653184 | bytes 6291456 | tf_op jit(solution)/shard_map/backward/pallas_call | solution.py:308
  (1 shorter events, 0.0 us)
Async XLA Ops:
  0.6 15.7 %copy-start.3 = (bf16[4,1024,8]{1,2,0:T(8,128)(2,1)S(1)}, bf16[4,1024,8]{1,2,0:T(8,128)(2,1)}, u32[]{:S(2)}) copy-start(bf16[4,1024,8]{1,2,0:T(8,128)(2,1)} %param.13) | copy-start | bytes 196612
  0.6 15.7 %copy-start = (bf16[1,1024,1024]{2,1,0:T(8,128)(2,1)S(1)}, bf16[1,1024,1024]{2,1,0:T(8,128)(2,1)}, u32[]{:S(2)}) copy-start(bf16[1,1024,1024]{2,1,0:T(8,128)(2,1)} %param.12) | copy-start | bytes 6291460
  0.7 15.7 %copy-start.1 = (bf16[1,1024,1024]{2,1,0:T(8,128)(2,1)S(1)}, bf16[1,1024,1024]{2,1,0:T(8,128)(2,1)}, u32[]{:S(2)}) copy-start(bf16[1,1024,1024]{2,1,0:T(8,128)(2,1)} %param.11) | copy-start | bytes 6291460
  0.7 0.8 %copy-start.4 = (bf16[2,1024]{1,0:T(2,128)(2,1)S(1)}, bf16[2,1024]{1,0:T(2,128)(2,1)}, u32[]{:S(2)}) copy-start(bf16[2,1024]{1,0:T(2,128)(2,1)} %events_ref.1) | copy-start | bytes 12292
  16.4 11.2 %copy-start.2 = (bf16[4,1024,256]{2,1,0:T(8,128)(2,1)S(1)}, bf16[4,1024,256]{2,1,0:T(8,128)(2,1)}, u32[]{:S(2)}) copy-start(bf16[4,1024,256]{2,1,0:T(8,128)(2,1)} %tower_in_ref.1) | copy-start | bytes 6291460
  16.4 11.2 %copy-start.5 = (f32[4,256]{1,0:T(4,128)S(1)}, f32[4,256]{1,0:T(4,128)}, u32[]{:S(2)}) copy-start(f32[4,256]{1,0:T(4,128)} %bias_ref.1) | copy-start | bytes 12292
  16.4 11.2 %copy-start.6 = (f32[4,256]{1,0:T(4,128)S(1)}, f32[4,256]{1,0:T(4,128)}, u32[]{:S(2)}) copy-start(f32[4,256]{1,0:T(4,128)} %weight_ref.1) | copy-start | bytes 12292
  16.4 11.2 %copy-start.7 = (s32[2,4]{1,0:T(2,128)S(1)}, s32[2,4]{1,0:T(2,128)}, u32[]{:S(2)}) copy-start(s32[2,4]{1,0:T(2,128)} %labels_ref.1) | copy-start | bytes 100
  16.4 11.2 %copy-start.8 = (f32[4]{0:T(128)S(1)}, f32[4]{0:T(128)}, u32[]{:S(2)}) copy-start(f32[4]{0:T(128)} %param.17) | copy-start | bytes 52

commit v11 on v10

--- a/solution.py
+++ b/solution.py
@@ -128,21 +128,23 @@
 
     steps(rows // chunk, rows == chunk, body)
 
-    tasks, experts, _ = gate_ref.shape
-    slots = experts * own
+    slots = prob_ref.shape[0]
+    experts = slots // own
+    tasks = gate_ref.shape[0] // experts
     events = by_row(events_ref[...], slots).astype(jnp.bfloat16)
     mine = iota((slots, experts), 0) // own == iota((slots, experts), 1)
     lane = iota((slots, LANES), 1)
     probs = jnp.zeros((slots, LANES), jnp.float32)
+    logits = dot(events, gate_ref[...], (1, 1))
     for task in range(tasks):
-        gates = dot(events, gate_ref[task], (1, 1))
+        gates = logits[:, task * experts : (task + 1) * experts]
         gates = jnp.exp(gates - jnp.max(gates, -1, keepdims=True))
         prob = jnp.sum(jnp.where(mine, gates, 0.0), -1, keepdims=True)
         probs = jnp.where(lane == task, prob / jnp.sum(gates, -1, keepdims=True), probs)
     prob_ref[...] = probs
 
 
-def forward(got, events, gate, first, second):
+def forward(got, events, gate, first, second, experts):
     devices, own, width = got.shape
     rows = devices * own
     units = first.shape[1]
@@ -153,7 +155,7 @@
             pltpu.VMEM((rows, width), jnp.bfloat16),
             pltpu.VMEM((rows, units), jnp.float32),
             pltpu.VMEM((rows, units), jnp.bfloat16),
-            pltpu.VMEM((gate.shape[1] * own, LANES), jnp.float32),
+            pltpu.VMEM((experts * own, LANES), jnp.float32),
         ],
         scratch_shapes=[pltpu.VMEM((rows, width), jnp.float32)],
         compiler_params=params(),
@@ -172,20 +174,16 @@
     weight_ref,
     shift_ref,
     message_ref,
-    outs_ref,
 ):
-    devices, own, width = parts_ref.shape
-    experts = devices // dp
-    slots = experts * own
+    slots, width = parts_ref.shape[0] // dp, parts_ref.shape[1]
+    own = labels_ref.shape[0]
     tasks = tower_in_ref.shape[0]
     float32, bfloat16 = jnp.float32, jnp.bfloat16
 
-    for expert in range(experts):
-        total = parts_ref[expert].astype(float32)
-        for at in range(1, dp):
-            total = total + parts_ref[at * experts + expert].astype(float32)
-        outs_ref[expert * own : (expert + 1) * own, :] = total
-    outs = outs_ref[...].astype(bfloat16)
+    total = parts_ref[:slots, :].astype(float32)
+    for at in range(1, dp):
+        total = total + parts_ref[at * slots : (at + 1) * slots, :].astype(float32)
+    outs = total.astype(bfloat16)
     labels = by_row(labels_ref[...], slots)
     lane = iota((slots, LANES), 1)
     lanes = jnp.zeros((slots, LANES), float32)
@@ -213,19 +211,16 @@
             lanes = jnp.where(lane == at * tasks + task, piece.astype(float32), lanes)
     dexpert = dexpert.astype(bfloat16)
     lanes = lanes.astype(bfloat16)
-    for expert in range(experts):
-        here = slice(expert * own, (expert + 1) * own)
-        for at in range(dp):
-            message_ref[at * experts + expert, :, :width] = dexpert[here]
-            message_ref[at * experts + expert, :, width:] = lanes[here]
+    for at in range(dp):
+        message_ref[at * slots : (at + 1) * slots, :width] = dexpert
+        message_ref[at * slots : (at + 1) * slots, width:] = lanes
 
 
 def middle(dp, parts, prob, labels, tower_in, bias, weight, shift):
-    devices, own, width = parts.shape
+    rows, width = parts.shape
     return pl.pallas_call(
         functools.partial(middle_kernel, dp),
-        out_shape=pltpu.VMEM((devices, own, width + LANES), jnp.bfloat16),
-        scratch_shapes=[pltpu.VMEM((devices // dp * own, width), jnp.float32)],
+        out_shape=pltpu.VMEM((rows, width + LANES), jnp.bfloat16),
         compiler_params=params(),
         cost_estimate=cost(4 * 8 * tower_in.size, 2 * tower_in.size),
         name="middle",
@@ -333,18 +328,20 @@
     events, labels, w_in, w_out, gate_weight, tower_in, tower_bias, tower_out, tower_out_bias
 ):
     dp = lax.axis_size("dp")
-    devices = dp * lax.axis_size("expert")
+    experts = lax.axis_size("expert")
+    devices = dp * experts
     tasks = tower_in.shape[0]
-    gate = jnp.transpose(gate_weight, (0, 2, 1))
+    gate = jnp.transpose(gate_weight, (0, 2, 1)).reshape(tasks * experts, events.shape[1])
 
     got = lax.all_to_all(spread(events, devices), BOTH, 0, 0, tiled=True)
-    part, every, pre, hidden, prob = forward(got, events, gate, w_in[0], w_out[0])
-
-    parts = lax.all_to_all(part, BOTH, 0, 0, tiled=True)
+    part, every, pre, hidden, prob = forward(got, events, gate, w_in[0], w_out[0], experts)
+
+    parts = lax.all_to_all(part, BOTH, 0, 0, tiled=True).reshape(-1, events.shape[1])
     message = middle(
         dp, parts, prob, labels, tower_in, tower_bias, tower_out, tower_out_bias[None]
     )
 
+    message = message.reshape(devices, events.shape[0], -1)
     got = lax.all_to_all(message, BOTH, 0, 0, tiled=True)
     grad_first, grad_second, grad_gate = backward(got, every, hidden, pre, w_out[0], tasks)
     return (grad_first[None], grad_second[None], jnp.transpose(grad_gate, (0, 2, 1)))

time: 43 us -> 44.8 us (1.042)
  local copies, waits for them, and re-layouts: 0.87 us -> 2.57 us
    unnamed x18, local copies, waits for them, and re-layouts: 0.87 us -> 2.45 us
where the time goes in v11:
time: 44.8 us; the launch traced here: 44.5 us
  blocking collectives  34.9 us (78%)
  Pallas kernels  6.26 us (14%)
  local copies, waits for them, and re-layouts  2.57 us (6%)
  between operations  0.76 us (2%)
    all_to_all x1, blocking collectives, per_device(): got = lax.all_to_all(spread(events, devices), BOTH, 0, 0, tiled=True)  14.8 us
    all_to_all x1, blocking collectives, per_device(): got = lax.all_to_all(message, BOTH, 0, 0, tiled=True)  10.1 us
    all_to_all x1, blocking collectives, per_device(): lax.all_to_all(part, BOTH, 0, 0, tiled=True).reshape(-1, events.shape[1])  10 us
    pallas_call x1, Pallas kernels, backward(): pl.pallas_call(functools.partial(backward_kernel, tasks), out_shape=[jax....  3.04 us
    unnamed x18, local copies, waits for them, and re-layouts  2.45 us
    pallas_call x1, Pallas kernels, middle(): pl.pallas_call(functools.partial(middle_kernel, dp), out_shape=pltpu.VMEM...  2 us
    pallas_call x1, Pallas kernels, forward(): pl.pallas_call(forward_kernel, out_shape=[pltpu.VMEM(got.shape, jnp.bfloa...  1.2 us

profile of v11, /device:TPU:0, one launch (start us, length us, event | category | flops | bytes accessed | tf_op | source)
XLA Modules:
  0.0 44.5 jit_solution(4932936813531365882)
XLA Ops:
  0.6 0.0 copy-start.3
  0.6 0.0 copy-start
  0.7 0.0 copy-start.1
  0.7 0.0 copy-start.4
  0.7 0.8 %copy-done.4 = bf16[2,1024]{1,0:T(2,128)(2,1)S(1)} copy-done((bf16[2,1024]{1,0:T(2,128)(2,1)S(1)}, bf16[2,1024]{1,0:T(2,128)(2,1)}, u32[]{:S(2)}) %copy-start.4) | copy-done | bytes 4120
  1.5 14.8 %all_to_all.15.got_ref = bf16[32,2,1024]{2,1,0:T(2,128)(2,1)S(1)} all-to-all(bf16[32,2,1024]{2,1,0:T(2,128)(2,1)S(1)} %spread.1), channel_id=1, replica_groups=mesh['dp'=4,'expert'=8] {'dp','expert'}, dimensions={0} | all-to-all | bytes 262144 | tf_op jit(solution)/shard_map/all_to_all | solution.py:336
  16.4 0.0 copy-done.3
  16.4 0.0 copy-done
  16.4 0.0 copy-done.1
  16.4 0.0 copy-start.5
  16.4 0.0 copy-start.6
  16.4 0.0 copy-start.7
  16.4 0.0 copy-start.8
  16.4 1.2 %forward.1 = (bf16[32,2,1024]{2,1,0:T(2,128)(2,1)S(1)}, bf16[64,1024]{1,0:T(8,128)(2,1)S(1)}, f32[64,1024]{1,0:T(8,128)S(1)}, bf16[64,1024]{1,0:T(8,128)(2,1)S(1)}, f32[16,128]{1,0:T(8,128)S(1)}) custom-call(bf16[32,2,1024]{2,1,0:T(2,128)(2,1)S(1)} %all_to_all.15.got_ref, bf16[2,1024]{1,0:T(2,128)(2,1)S(1)} %copy-done.4, bf16[32,1024]{1,0:T(8,128)(2,1)S(1)} %bitcast.12, ...), custom_call_target="tpu_custom_call" | custom-call | flops 268435456 | bytes 4194304 | tf_op jit(solution)/shard_map/forward/pallas_call | solution.py:151
  17.6 10.0 %all_to_all.16 = bf16[32,2,1024]{2,1,0:T(2,128)(2,1)S(1)} all-to-all(bf16[32,2,1024]{2,1,0:T(2,128)(2,1)S(1)} %get-tuple-element.11), channel_id=1, replica_groups=mesh['dp'=4,'expert'=8] {'dp','expert'}, dimensions={0} | all-to-all | bytes 262144 | tf_op jit(solution)/shard_map/all_to_all | solution.py:339
  27.6 0.1 reshape.16.parts_ref
  27.7 0.0 copy-done.5
  27.7 0.0 copy-done.6
  27.7 0.0 copy-done.7
  27.7 0.0 copy-done.8
  27.7 0.0 copy-start.2
  27.7 1.6 %copy-done.2 = bf16[4,1024,256]{2,1,0:T(8,128)(2,1)S(1)} copy-done((bf16[4,1024,256]{2,1,0:T(8,128)(2,1)S(1)}, bf16[4,1024,256]{2,1,0:T(8,128)(2,1)}, u32[]{:S(2)}) %copy-start.2) | copy-done | bytes 2097176
  29.3 2.0 %middle.1 = bf16[64,1152]{1,0:T(8,128)(2,1)S(1)} custom-call(bf16[64,1024]{1,0:T(8,128)(2,1)S(1)} %reshape.16.parts_ref, f32[16,128]{1,0:T(8,128)S(1)} %get-tuple-element.12.prob_ref, s32[2,4]{1,0:T(2,128)S(1)} %copy-done.7, bf16[4,1024,256]{2,1,0:T(8,128)(2,1)S(1)} %copy-done.2, f32[4,256]{1,0:T(4,128)S(1)} %copy-done.5, f32[4,256]{1,0:T(4,128)S(1)} %copy-done.6, ...), custom_call_target="tpu_custom_call" | custom-call | flops 33554432 | bytes 2097152 | tf_op jit(solution)/shard_map/middle/pallas_call | solution.py:221
  31.3 0.1 reshape.17
  31.4 10.1 %all_to_all.17.got_ref = bf16[32,2,1152]{2,1,0:T(2,128)(2,1)S(1)} all-to-all(bf16[32,2,1152]{2,1,0:T(2,128)(2,1)S(1)} %reshape.17), channel_id=1, replica_groups=mesh['dp'=4,'expert'=8] {'dp','expert'}, dimensions={0} | all-to-all | bytes 294912 | tf_op jit(solution)/shard_map/all_to_all | solution.py:345
  41.5 3.0 %backward.1 = (bf16[1024,1024]{1,0:T(8,128)(2,1)}, bf16[1024,1024]{1,0:T(8,128)(2,1)}, f32[4,1,1024]{2,1,0:T(1,128)}) custom-call(bf16[32,2,1152]{2,1,0:T(2,128)(2,1)S(1)} %all_to_all.17.got_ref, bf16[64,1024]{1,0:T(8,128)(2,1)S(1)} %get-tuple-element.13.every_ref, bf16[64,1024]{1,0:T(8,128)(2,1)S(1)} %get-tuple-element.14.hidden_ref, ...), custom_call_target="tpu_custom_call" | custom-call | flops 402653184 | bytes 6291456 | tf_op jit(solution)/shard_map/backward/pallas_call | solution.py:303
  (1 shorter events, 0.0 us)
Async XLA Ops:
  0.6 15.7 %copy-start.3 = (bf16[4,1024,8]{1,2,0:T(8,128)(2,1)S(1)}, bf16[4,1024,8]{1,2,0:T(8,128)(2,1)}, u32[]{:S(2)}) copy-start(bf16[4,1024,8]{1,2,0:T(8,128)(2,1)} %param.13) | copy-start | bytes 196612
  0.6 15.7 %copy-start = (bf16[1,1024,1024]{2,1,0:T(8,128)(2,1)S(1)}, bf16[1,1024,1024]{2,1,0:T(8,128)(2,1)}, u32[]{:S(2)}) copy-start(bf16[1,1024,1024]{2,1,0:T(8,128)(2,1)} %param.12) | copy-start | bytes 6291460
  0.7 15.7 %copy-start.1 = (bf16[1,1024,1024]{2,1,0:T(8,128)(2,1)S(1)}, bf16[1,1024,1024]{2,1,0:T(8,128)(2,1)}, u32[]{:S(2)}) copy-start(bf16[1,1024,1024]{2,1,0:T(8,128)(2,1)} %param.11) | copy-start | bytes 6291460
  0.7 0.8 %copy-start.4 = (bf16[2,1024]{1,0:T(2,128)(2,1)S(1)}, bf16[2,1024]{1,0:T(2,128)(2,1)}, u32[]{:S(2)}) copy-start(bf16[2,1024]{1,0:T(2,128)(2,1)} %events_ref.1) | copy-start | bytes 12292
  16.4 11.3 %copy-start.5 = (f32[4,256]{1,0:T(4,128)S(1)}, f32[4,256]{1,0:T(4,128)}, u32[]{:S(2)}) copy-start(f32[4,256]{1,0:T(4,128)} %bias_ref.1) | copy-start | bytes 12292
  16.4 11.3 %copy-start.6 = (f32[4,256]{1,0:T(4,128)S(1)}, f32[4,256]{1,0:T(4,128)}, u32[]{:S(2)}) copy-start(f32[4,256]{1,0:T(4,128)} %weight_ref.1) | copy-start | bytes 12292
  16.4 11.3 %copy-start.7 = (s32[2,4]{1,0:T(2,128)S(1)}, s32[2,4]{1,0:T(2,128)}, u32[]{:S(2)}) copy-start(s32[2,4]{1,0:T(2,128)} %labels_ref.1) | copy-start | bytes 100
  16.4 11.3 %copy-start.8 = (f32[4]{0:T(128)S(1)}, f32[4]{0:T(128)}, u32[]{:S(2)}) copy-start(f32[4]{0:T(128)} %param.17) | copy-start | bytes 52
  27.7 1.6 %copy-start.2 = (bf16[4,1024,256]{2,1,0:T(8,128)(2,1)S(1)}, bf16[4,1024,256]{2,1,0:T(8,128)(2,1)}, u32[]{:S(2)}) copy-start(bf16[4,1024,256]{2,1,0:T(8,128)(2,1)} %tower_in_ref.1) | copy-start | bytes 6291460

commit v12 on v10

--- a/solution.py
+++ b/solution.py
@@ -112,6 +112,21 @@
     own = got_ref.shape[1]
     rows, width = every_ref.shape
     chunk = min(rows, 64)
+    slots = prob_ref.shape[0]
+    experts = slots // own
+    tasks = gate_ref.shape[0] // experts
+    events = by_row(events_ref[...], slots).astype(jnp.bfloat16)
+    mine = iota((slots, experts), 0) // own == iota((slots, experts), 1)
+    lane = iota((slots, LANES), 1)
+    probs = jnp.zeros((slots, LANES), jnp.float32)
+    logits = dot(events, gate_ref[...], (1, 1))
+    for task in range(tasks):
+        gates = logits[:, task * experts : (task + 1) * experts]
+        gates = jnp.exp(gates - jnp.max(gates, -1, keepdims=True))
+        prob = jnp.sum(jnp.where(mine, gates, 0.0), -1, keepdims=True)
+        probs = jnp.where(lane == task, prob / jnp.sum(gates, -1, keepdims=True), probs)
+    prob_ref[...] = probs
+
     unpack(got_ref, wide_ref)
 
     def body(step):
@@ -128,21 +143,8 @@
 
     steps(rows // chunk, rows == chunk, body)
 
-    tasks, experts, _ = gate_ref.shape
-    slots = experts * own
-    events = by_row(events_ref[...], slots).astype(jnp.bfloat16)
-    mine = iota((slots, experts), 0) // own == iota((slots, experts), 1)
-    lane = iota((slots, LANES), 1)
-    probs = jnp.zeros((slots, LANES), jnp.float32)
-    for task in range(tasks):
-        gates = dot(events, gate_ref[task], (1, 1))
-        gates = jnp.exp(gates - jnp.max(gates, -1, keepdims=True))
-        prob = jnp.sum(jnp.where(mine, gates, 0.0), -1, keepdims=True)
-        probs = jnp.where(lane == task, prob / jnp.sum(gates, -1, keepdims=True), probs)
-    prob_ref[...] = probs
-
-
-def forward(got, events, gate, first, second):
+
+def forward(got, events, gate, first, second, experts):
     devices, own, width = got.shape
     rows = devices * own
     units = first.shape[1]
@@ -153,7 +155,7 @@
             pltpu.VMEM((rows, width), jnp.bfloat16),
             pltpu.VMEM((rows, units), jnp.float32),
             pltpu.VMEM((rows, units), jnp.bfloat16),
-            pltpu.VMEM((gate.shape[1] * own, LANES), jnp.float32),
+            pltpu.VMEM((experts * own, LANES), jnp.float32),
         ],
         scratch_shapes=[pltpu.VMEM((rows, width), jnp.float32)],
         compiler_params=params(),
@@ -188,29 +190,50 @@
     outs = outs_ref[...].astype(bfloat16)
     labels = by_row(labels_ref[...], slots)
     lane = iota((slots, LANES), 1)
+    units = tower_in_ref.shape[2]
+
+    def wide(ref):
+        return jnp.concatenate([ref[task : task + 1, :] for task in range(tasks)], 1)
+
+    def lanes_of(value, task):
+        return value[:, task * units : (task + 1) * units]
+
+    def each(columns):
+        return jnp.concatenate(
+            [jnp.broadcast_to(column, (slots, units)) for column in columns], 1
+        )
+
+    probs = [prob_ref[:, task : task + 1] for task in range(tasks)]
+    single = jnp.concatenate(
+        [dot(outs, tower_in_ref[task], (1, 0)) for task in range(tasks)], 1
+    )
+    linear = single * each(probs)
+    shift = own
+    while shift < slots:
+        linear = linear + pltpu.roll(linear, shift, 0)
+        shift *= 2
+    active, slope = gelu_pair(linear + wide(bias_ref))
+    weight = wide(weight_ref)
+    active, slope = active * weight, slope * weight
+    dlogit = []
+    for task in range(tasks):
+        logit = jnp.sum(lanes_of(active, task), -1, keepdims=True) + shift_ref[:, task : task + 1]
+        dlogit.append(jax.nn.sigmoid(logit) - labels[:, task : task + 1])
+    dtower = slope * each(dlogit)
+    stack = [piece.astype(float32) for piece in pieces_of(dtower)[:2]]
+    stack = jnp.concatenate(stack, 0).astype(bfloat16)
+    turned = [
+        dot(lanes_of(stack, task), tower_in_ref[task], (1, 1)) for task in range(tasks)
+    ]
+    rest = dtower * (single - linear)
     lanes = jnp.zeros((slots, LANES), float32)
     dexpert = jnp.zeros((slots, width), float32)
     for task in range(tasks):
-        prob = prob_ref[:, task : task + 1]
-        weight = weight_ref[task : task + 1, :]
-        single = dot(outs, tower_in_ref[task], (1, 0))
-        linear = single * prob
-        shift = own
-        while shift < slots:
-            linear = linear + pltpu.roll(linear, shift, 0)
-            shift *= 2
-        active, slope = gelu_pair(linear + bias_ref[task : task + 1, :])
-        logit = jnp.sum(active * weight, -1, keepdims=True) + shift_ref[:, task : task + 1]
-        dlogit = jax.nn.sigmoid(logit) - labels[:, task : task + 1]
-        dtower = slope * weight * dlogit
-        dgate = prob * jnp.sum(dtower * (single - linear), -1, keepdims=True)
-        stack = [piece.astype(float32) for piece in pieces_of(dtower)[:2]]
-        stack = jnp.concatenate(stack, 0).astype(bfloat16)
-        turned = dot(stack, tower_in_ref[task], (1, 1))
-        dmixed = (turned[:slots] + turned[slots:]).astype(bfloat16).astype(float32)
-        dexpert = dexpert + prob * dmixed
+        dgate = probs[task] * jnp.sum(lanes_of(rest, task), -1, keepdims=True)
         for at, piece in enumerate(pieces_of(dgate)):
             lanes = jnp.where(lane == at * tasks + task, piece.astype(float32), lanes)
+        dmixed = (turned[task][:slots] + turned[task][slots:]).astype(bfloat16)
+        dexpert = dexpert + probs[task] * dmixed.astype(float32)
     dexpert = dexpert.astype(bfloat16)
     lanes = lanes.astype(bfloat16)
     for expert in range(experts):
@@ -333,12 +356,13 @@
     events, labels, w_in, w_out, gate_weight, tower_in, tower_bias, tower_out, tower_out_bias
 ):
     dp = lax.axis_size("dp")
-    devices = dp * lax.axis_size("expert")
+    experts = lax.axis_size("expert")
+    devices = dp * experts
     tasks = tower_in.shape[0]
-    gate = jnp.transpose(gate_weight, (0, 2, 1))
+    gate = jnp.transpose(gate_weight, (0, 2, 1)).reshape(tasks * experts, events.shape[1])
 
     got = lax.all_to_all(spread(events, devices), BOTH, 0, 0, tiled=True)
-    part, every, pre, hidden, prob = forward(got, events, gate, w_in[0], w_out[0])
+    part, every, pre, hidden, prob = forward(got, events, gate, w_in[0], w_out[0], experts)
 
     parts = lax.all_to_all(part, BOTH, 0, 0, tiled=True)
     message = middle(

time: 43 us -> 42.1 us (0.979)
  Pallas kernels: 6.27 us -> 5.3 us
    pallas_call x1, Pallas kernels: 2.03 us -> 1.25 us  [middle(): pl.pallas_call(functools.partial(middle_kernel, dp), out_shape=pltpu.VMEM...]
where the time goes in v12:
time: 42.1 us; the launch traced here: 41.9 us
  blocking collectives  34.9 us (83%)
  Pallas kernels  5.3 us (13%)
  local copies, waits for them, and re-layouts  0.87 us (2%)
  between operations  0.75 us (2%)
    all_to_all x1, blocking collectives, per_device(): got = lax.all_to_all(spread(events, devices), BOTH, 0, 0, tiled=True)  14.8 us
    all_to_all x1, blocking collectives, per_device(): got = lax.all_to_all(message, BOTH, 0, 0, tiled=True)  10.1 us
    all_to_all x1, blocking collectives, per_device(): parts = lax.all_to_all(part, BOTH, 0, 0, tiled=True)  10 us
    pallas_call x1, Pallas kernels, backward(): pl.pallas_call(functools.partial(backward_kernel, tasks), out_shape=[jax....  3.06 us
    pallas_call x1, Pallas kernels, middle(): pl.pallas_call(functools.partial(middle_kernel, dp), out_shape=pltpu.VMEM...  1.25 us
    pallas_call x1, Pallas kernels, forward(): pl.pallas_call(forward_kernel, out_shape=[pltpu.VMEM(got.shape, jnp.bfloa...  0.98 us
    unnamed x18, local copies, waits for them, and re-layouts  0.87 us

profile of v12, /device:TPU:0, one launch (start us, length us, event | category | flops | bytes accessed | tf_op | source)
XLA Modules:
  0.0 41.9 jit_solution(3571380128096284834)
XLA Ops:
  0.6 0.0 copy-start.3
  0.6 0.0 copy-start
  0.7 0.0 copy-start.1
  0.7 0.0 copy-start.4
  0.7 0.8 %copy-done.4 = bf16[2,1024]{1,0:T(2,128)(2,1)S(1)} copy-done((bf16[2,1024]{1,0:T(2,128)(2,1)S(1)}, bf16[2,1024]{1,0:T(2,128)(2,1)}, u32[]{:S(2)}) %copy-start.4) | copy-done | bytes 4120
  1.5 14.8 %all_to_all.15.got_ref = bf16[32,2,1024]{2,1,0:T(2,128)(2,1)S(1)} all-to-all(bf16[32,2,1024]{2,1,0:T(2,128)(2,1)S(1)} %spread.1), channel_id=1, replica_groups=mesh['dp'=4,'expert'=8] {'dp','expert'}, dimensions={0} | all-to-all | bytes 262144 | tf_op jit(solution)/shard_map/all_to_all | solution.py:364
  16.4 0.0 copy-done.3
  16.4 0.0 copy-done
  16.4 0.0 copy-done.1
  16.4 0.0 copy-start.2
  16.4 0.0 copy-start.5
  16.4 0.0 copy-start.6
  16.4 0.0 copy-start.7
  16.4 0.0 copy-start.8
  16.4 1.0 %forward.1 = (bf16[32,2,1024]{2,1,0:T(2,128)(2,1)S(1)}, bf16[64,1024]{1,0:T(8,128)(2,1)S(1)}, f32[64,1024]{1,0:T(8,128)S(1)}, bf16[64,1024]{1,0:T(8,128)(2,1)S(1)}, f32[16,128]{1,0:T(8,128)S(1)}) custom-call(bf16[32,2,1024]{2,1,0:T(2,128)(2,1)S(1)} %all_to_all.15.got_ref, bf16[2,1024]{1,0:T(2,128)(2,1)S(1)} %copy-done.4, bf16[32,1024]{1,0:T(8,128)(2,1)S(1)} %bitcast.12, ...), custom_call_target="tpu_custom_call" | custom-call | flops 268435456 | bytes 4194304 | tf_op jit(solution)/shard_map/forward/pallas_call | solution.py:151
  17.4 10.0 %all_to_all.16.parts_ref = bf16[32,2,1024]{2,1,0:T(2,128)(2,1)S(1)} all-to-all(bf16[32,2,1024]{2,1,0:T(2,128)(2,1)S(1)} %get-tuple-element.11), channel_id=1, replica_groups=mesh['dp'=4,'expert'=8] {'dp','expert'}, dimensions={0} | all-to-all | bytes 262144 | tf_op jit(solution)/shard_map/all_to_all | solution.py:367
  27.4 0.0 copy-done.2
  27.4 0.0 copy-done.5
  27.4 0.0 copy-done.6
  27.4 0.0 copy-done.7
  27.4 0.0 copy-done.8
  27.4 1.2 %middle.1 = bf16[32,2,1152]{2,1,0:T(2,128)(2,1)S(1)} custom-call(bf16[32,2,1024]{2,1,0:T(2,128)(2,1)S(1)} %all_to_all.16.parts_ref, f32[16,128]{1,0:T(8,128)S(1)} %get-tuple-element.12.prob_ref, s32[2,4]{1,0:T(2,128)S(1)} %copy-done.7, bf16[4,1024,256]{2,1,0:T(8,128)(2,1)S(1)} %copy-done.2, f32[4,256]{1,0:T(4,128)S(1)} %copy-done.5, f32[4,256]{1,0:T(4,128)S(1)} %copy-done.6, ...), custom_call_target="tpu_custom_call" | custom-call | flops 33554432 | bytes 2097152 | tf_op jit(solution)/shard_map/middle/pallas_call | solution.py:248
  28.7 10.1 %all_to_all.17.got_ref = bf16[32,2,1152]{2,1,0:T(2,128)(2,1)S(1)} all-to-all(bf16[32,2,1152]{2,1,0:T(2,128)(2,1)S(1)} %middle.1), channel_id=1, replica_groups=mesh['dp'=4,'expert'=8] {'dp','expert'}, dimensions={0} | all-to-all | bytes 294912 | tf_op jit(solution)/shard_map/all_to_all | solution.py:372
  38.8 3.1 %backward.1 = (bf16[1024,1024]{1,0:T(8,128)(2,1)}, bf16[1024,1024]{1,0:T(8,128)(2,1)}, f32[4,1,1024]{2,1,0:T(1,128)}) custom-call(bf16[32,2,1152]{2,1,0:T(2,128)(2,1)S(1)} %all_to_all.17.got_ref, bf16[64,1024]{1,0:T(8,128)(2,1)S(1)} %get-tuple-element.13.every_ref, bf16[64,1024]{1,0:T(8,128)(2,1)S(1)} %get-tuple-element.14.hidden_ref, ...), custom_call_target="tpu_custom_call" | custom-call | flops 402653184 | bytes 6291456 | tf_op jit(solution)/shard_map/backward/pallas_call | solution.py:331
  (1 shorter events, 0.0 us)
Async XLA Ops:
  0.6 15.7 %copy-start.3 = (bf16[4,1024,8]{1,2,0:T(8,128)(2,1)S(1)}, bf16[4,1024,8]{1,2,0:T(8,128)(2,1)}, u32[]{:S(2)}) copy-start(bf16[4,1024,8]{1,2,0:T(8,128)(2,1)} %param.13) | copy-start | bytes 196612
  0.6 15.7 %copy-start = (bf16[1,1024,1024]{2,1,0:T(8,128)(2,1)S(1)}, bf16[1,1024,1024]{2,1,0:T(8,128)(2,1)}, u32[]{:S(2)}) copy-start(bf16[1,1024,1024]{2,1,0:T(8,128)(2,1)} %param.12) | copy-start | bytes 6291460
  0.7 15.7 %copy-start.1 = (bf16[1,1024,1024]{2,1,0:T(8,128)(2,1)S(1)}, bf16[1,1024,1024]{2,1,0:T(8,128)(2,1)}, u32[]{:S(2)}) copy-start(bf16[1,1024,1024]{2,1,0:T(8,128)(2,1)} %param.11) | copy-start | bytes 6291460
  0.7 0.8 %copy-start.4 = (bf16[2,1024]{1,0:T(2,128)(2,1)S(1)}, bf16[2,1024]{1,0:T(2,128)(2,1)}, u32[]{:S(2)}) copy-start(bf16[2,1024]{1,0:T(2,128)(2,1)} %events_ref.1) | copy-start | bytes 12292
  16.4 11.1 %copy-start.2 = (bf16[4,1024,256]{2,1,0:T(8,128)(2,1)S(1)}, bf16[4,1024,256]{2,1,0:T(8,128)(2,1)}, u32[]{:S(2)}) copy-start(bf16[4,1024,256]{2,1,0:T(8,128)(2,1)} %tower_in_ref.1) | copy-start | bytes 6291460
  16.4 11.0 %copy-start.5 = (f32[4,256]{1,0:T(4,128)S(1)}, f32[4,256]{1,0:T(4,128)}, u32[]{:S(2)}) copy-start(f32[4,256]{1,0:T(4,128)} %bias_ref.1) | copy-start | bytes 12292
  16.4 11.0 %copy-start.6 = (f32[4,256]{1,0:T(4,128)S(1)}, f32[4,256]{1,0:T(4,128)}, u32[]{:S(2)}) copy-start(f32[4,256]{1,0:T(4,128)} %weight_ref.1) | copy-start | bytes 12292
  16.4 11.0 %copy-start.7 = (s32[2,4]{1,0:T(2,128)S(1)}, s32[2,4]{1,0:T(2,128)}, u32[]{:S(2)}) copy-start(s32[2,4]{1,0:T(2,128)} %labels_ref.1) | copy-start | bytes 100
  16.4 11.0 %copy-start.8 = (f32[4]{0:T(128)S(1)}, f32[4]{0:T(128)}, u32[]{:S(2)}) copy-start(f32[4]{0:T(128)} %param.17) | copy-start | bytes 52

commit v13 on v12

--- a/solution.py
+++ b/solution.py
@@ -72,8 +72,24 @@
         spread_kernel,
         out_shape=pltpu.VMEM((devices, *value.shape), value.dtype),
         compiler_params=params(),
+        name="spread",
+    )(value)
+
+
+def ahead_kernel(value_ref, same_ref):
+    del value_ref, same_ref
+
+
+def ahead(value):
+    return pl.pallas_call(
+        ahead_kernel,
+        in_specs=[pl.BlockSpec(memory_space=pl.ANY)],
+        out_specs=pl.BlockSpec(memory_space=pl.ANY),
+        out_shape=pltpu.VMEM(value.shape, value.dtype),
+        input_output_aliases={0: 0},
+        compiler_params=params(),
         cost_estimate=cost(AHEAD_FLOPS, 0),
-        name="spread",
+        name="ahead",
     )(value)
 
 
@@ -133,13 +149,17 @@
         here = span(step, chunk)
         every = wide_ref[here, :].astype(jnp.bfloat16)
         every_ref[here, :] = every
-        pre = dot(every, first_ref[...], (1, 0))
-        hidden = gelu_pair(pre)[0].astype(jnp.bfloat16)
-        part = dot(hidden, second_ref[...], (1, 0)).astype(jnp.bfloat16)
+        blocks = [slice(at, at + TILE) for at in range(0, first_ref.shape[1], TILE)]
+        pre = [dot(every, first_ref[:, block], (1, 0)) for block in blocks]
+        part = 0.0
+        for block, value in zip(blocks, pre):
+            hidden = gelu_pair(value)[0].astype(jnp.bfloat16)
+            part = part + dot(hidden, second_ref[block, :], (1, 0))
+            pre_ref[here, block] = value
+            hidden_ref[here, block] = hidden
+        part = part.astype(jnp.bfloat16)
         for at in range(chunk // own):
             part_ref[step * (chunk // own) + at] = part[at * own : (at + 1) * own]
-        pre_ref[here, :] = pre
-        hidden_ref[here, :] = hidden
 
     steps(rows // chunk, rows == chunk, body)
 
@@ -276,26 +296,16 @@
     rows, width = every_ref.shape
     units = pre_ref.shape[1]
     flat = rows <= 64
-    across, down = units // TILE, width // TILE
-
-    def second_copy(step):
-        here = span(step, TILE)
-        return pltpu.make_async_copy(
-            second_buf.at[here, :], grad_second_ref.at[here, :], sems.at[step]
-        )
-
-    def first_copy(step):
-        here = span(step, TILE)
-        return pltpu.make_async_copy(
-            first_buf.at[here, :], grad_first_ref.at[here, :], sems.at[across + step]
-        )
+    blocks = units // TILE
+    tops = width // TILE
+    second_cuts = [1, blocks - 1]
+    first_cuts = [tops - tops // 2, tops // 2 - tops // 4, tops // 4]
 
     def second_step(step):
         here = span(step, TILE)
         second_buf[here, :] = dot(
             hidden_ref[:, here], arrived_ref[:, :width], (0, 0)
         ).astype(jnp.bfloat16)
-        second_copy(step).start()
 
     def dpre_step(step):
         here = span(step, TILE)
@@ -305,22 +315,33 @@
     def first_step(step):
         here = span(step, TILE)
         first_buf[here, :] = dot(every_ref[:, here], dpre_ref[...], (0, 0)).astype(jnp.bfloat16)
-        first_copy(step).start()
+
+    copies = []
+
+    def send(source, target):
+        copies.append(pltpu.make_async_copy(source, target, sems.at[len(copies)]))
+        copies[-1].start()
+
+    def gradient(make, buf, target, cuts, at):
+        for cut in filter(None, cuts):
+            steps(cut, flat, lambda step: make(step + at))
+            here = pl.ds(at * TILE, cut * TILE)
+            send(buf.at[here, :], target.at[here, :])
+            at += cut
 
     unpack(got_ref, wide_ref)
     arrived_ref[...] = wide_ref[...].astype(jnp.bfloat16)
-    steps(across, flat, second_step)
+    gradient(second_step, second_buf, grad_second_ref, second_cuts[:1], 0)
+    steps(blocks, flat, dpre_step)
+    gradient(second_step, second_buf, grad_second_ref, second_cuts[1:], second_cuts[0])
     gate = dot(arrived_ref[:, width:], every_ref[...], (0, 0))
     for task in range(tasks):
         lanes = [at * tasks + task for at in range(3)]
         gate_buf[task] = sum(gate[lane : lane + 1] for lane in lanes)
-    gate_copy = pltpu.make_async_copy(gate_buf, grad_gate_ref, sems.at[across + down])
-    gate_copy.start()
-    steps(units // TILE, flat, dpre_step)
-    steps(down, flat, first_step)
-    gate_copy.wait()
-    steps(across, flat, lambda step: second_copy(step).wait())
-    steps(down, flat, lambda step: first_copy(step).wait())
+    send(gate_buf, grad_gate_ref)
+    gradient(first_step, first_buf, grad_first_ref, first_cuts, 0)
+    for copy in copies:
+        copy.wait()
 
 
 def backward(got, every, hidden, pre, second, tasks):
@@ -344,7 +365,7 @@
             pltpu.VMEM((tasks, 1, width), jnp.float32),
             pltpu.VMEM((rows, width + LANES), jnp.bfloat16),
             pltpu.VMEM((rows, width + LANES), jnp.float32),
-            pltpu.SemaphoreType.DMA((units // TILE + width // TILE + 1,)),
+            pltpu.SemaphoreType.DMA((6,)),
         ],
         compiler_params=params(),
         cost_estimate=cost(6 * rows * width * units, 6 * width * units),
@@ -361,7 +382,7 @@
     tasks = tower_in.shape[0]
     gate = jnp.transpose(gate_weight, (0, 2, 1)).reshape(tasks * experts, events.shape[1])
 
-    got = lax.all_to_all(spread(events, devices), BOTH, 0, 0, tiled=True)
+    got = lax.all_to_all(ahead(spread(events, devices)), BOTH, 0, 0, tiled=True)
     part, every, pre, hidden, prob = forward(got, events, gate, w_in[0], w_out[0], experts)
 
     parts = lax.all_to_all(part, BOTH, 0, 0, tiled=True)

time: 42.1 us -> 42.1 us (level)
  no operation moved by 1% of the time
where the time goes in v13:
time: 42.1 us; the launch traced here: 41.9 us
  blocking collectives  34.9 us (83%)
  Pallas kernels  5.47 us (13%)
  between operations  0.75 us (2%)
  local copies, waits for them, and re-layouts  0.73 us (2%)
    all_to_all x1, blocking collectives, per_device(): got = lax.all_to_all(ahead(spread(events, devices)), BOTH, 0, 0, tiled=True)  14.8 us
    all_to_all x1, blocking collectives, per_device(): got = lax.all_to_all(message, BOTH, 0, 0, tiled=True)  10.1 us
    all_to_all x1, blocking collectives, per_device(): parts = lax.all_to_all(part, BOTH, 0, 0, tiled=True)  10 us
    pallas_call x1, Pallas kernels, backward(): pl.pallas_call(functools.partial(backward_kernel, tasks), out_shape=[jax....  3.25 us
    pallas_call x1, Pallas kernels, middle(): pl.pallas_call(functools.partial(middle_kernel, dp), out_shape=pltpu.VMEM...  1.25 us
    pallas_call x1, Pallas kernels, forward(): pl.pallas_call(forward_kernel, out_shape=[pltpu.VMEM(got.shape, jnp.bfloa...  0.96 us

profile of v13, /device:TPU:0, one launch (start us, length us, event | category | flops | bytes accessed | tf_op | source)
XLA Modules:
  0.0 41.9 jit_solution(10986019767773733118)
XLA Ops:
  0.6 0.0 copy-start.4
  0.6 0.7 %copy-done.4 = bf16[2,1024]{1,0:T(2,128)(2,1)S(1)} copy-done((bf16[2,1024]{1,0:T(2,128)(2,1)S(1)}, bf16[2,1024]{1,0:T(2,128)(2,1)}, u32[]{:S(2)}) %copy-start.4) | copy-done | bytes 4120
  1.3 0.0 copy-start
  1.3 0.0 copy-start.1
  1.4 0.0 copy-start.3
  1.4 14.8 %all_to_all.15.got_ref = bf16[32,2,1024]{2,1,0:T(2,128)(2,1)S(1)} all-to-all(bf16[32,2,1024]{2,1,0:T(2,128)(2,1)S(1)} %ahead.1), channel_id=1, replica_groups=mesh['dp'=4,'expert'=8] {'dp','expert'}, dimensions={0} | all-to-all | bytes 262144 | tf_op jit(solution)/shard_map/all_to_all | solution.py:385
  16.2 0.0 copy-done
  16.2 0.0 copy-done.1
  16.2 0.0 copy-done.3
  16.2 0.0 copy-start.2
  16.2 0.0 copy-start.5
  16.3 0.0 copy-start.6
  16.3 0.0 copy-start.7
  16.3 0.0 copy-start.8
  16.3 1.0 %forward.1 = (bf16[32,2,1024]{2,1,0:T(2,128)(2,1)S(1)}, bf16[64,1024]{1,0:T(8,128)(2,1)S(1)}, f32[64,1024]{1,0:T(8,128)S(1)}, bf16[64,1024]{1,0:T(8,128)(2,1)S(1)}, f32[16,128]{1,0:T(8,128)S(1)}) custom-call(bf16[32,2,1024]{2,1,0:T(2,128)(2,1)S(1)} %all_to_all.15.got_ref, bf16[2,1024]{1,0:T(2,128)(2,1)S(1)} %copy-done.4, bf16[32,1024]{1,0:T(8,128)(2,1)S(1)} %bitcast.12, ...), custom_call_target="tpu_custom_call" | custom-call | flops 268435456 | bytes 4194304 | tf_op jit(solution)/shard_map/forward/pallas_call | solution.py:171
  17.3 10.0 %all_to_all.16.parts_ref = bf16[32,2,1024]{2,1,0:T(2,128)(2,1)S(1)} all-to-all(bf16[32,2,1024]{2,1,0:T(2,128)(2,1)S(1)} %get-tuple-element.11), channel_id=1, replica_groups=mesh['dp'=4,'expert'=8] {'dp','expert'}, dimensions={0} | all-to-all | bytes 262144 | tf_op jit(solution)/shard_map/all_to_all | solution.py:388
  27.3 0.0 copy-done.2
  27.3 0.0 copy-done.5
  27.3 0.0 copy-done.6
  27.3 0.0 copy-done.7
  27.3 0.0 copy-done.8
  27.3 1.2 %middle.1 = bf16[32,2,1152]{2,1,0:T(2,128)(2,1)S(1)} custom-call(bf16[32,2,1024]{2,1,0:T(2,128)(2,1)S(1)} %all_to_all.16.parts_ref, f32[16,128]{1,0:T(8,128)S(1)} %get-tuple-element.12.prob_ref, s32[2,4]{1,0:T(2,128)S(1)} %copy-done.7, bf16[4,1024,256]{2,1,0:T(8,128)(2,1)S(1)} %copy-done.2, f32[4,256]{1,0:T(4,128)S(1)} %copy-done.5, f32[4,256]{1,0:T(4,128)S(1)} %copy-done.6, ...), custom_call_target="tpu_custom_call" | custom-call | flops 33554432 | bytes 2097152 | tf_op jit(solution)/shard_map/middle/pallas_call | solution.py:268
  28.5 10.1 %all_to_all.17.got_ref = bf16[32,2,1152]{2,1,0:T(2,128)(2,1)S(1)} all-to-all(bf16[32,2,1152]{2,1,0:T(2,128)(2,1)S(1)} %middle.1), channel_id=1, replica_groups=mesh['dp'=4,'expert'=8] {'dp','expert'}, dimensions={0} | all-to-all | bytes 294912 | tf_op jit(solution)/shard_map/all_to_all | solution.py:393
  38.6 3.3 %backward.1 = (bf16[1024,1024]{1,0:T(8,128)(2,1)}, bf16[1024,1024]{1,0:T(8,128)(2,1)}, f32[4,1,1024]{2,1,0:T(1,128)}) custom-call(bf16[32,2,1152]{2,1,0:T(2,128)(2,1)S(1)} %all_to_all.17.got_ref, bf16[64,1024]{1,0:T(8,128)(2,1)S(1)} %get-tuple-element.13.every_ref, bf16[64,1024]{1,0:T(8,128)(2,1)S(1)} %get-tuple-element.14.hidden_ref, ...), custom_call_target="tpu_custom_call" | custom-call | flops 402653184 | bytes 6291456 | tf_op jit(solution)/shard_map/backward/pallas_call | solution.py:352
  (2 shorter events, 0.0 us)
Async XLA Ops:
  0.6 0.7 %copy-start.4 = (bf16[2,1024]{1,0:T(2,128)(2,1)S(1)}, bf16[2,1024]{1,0:T(2,128)(2,1)}, u32[]{:S(2)}) copy-start(bf16[2,1024]{1,0:T(2,128)(2,1)} %events_ref.1) | copy-start | bytes 12292
  1.3 14.9 %copy-start = (bf16[1,1024,1024]{2,1,0:T(8,128)(2,1)S(1)}, bf16[1,1024,1024]{2,1,0:T(8,128)(2,1)}, u32[]{:S(2)}) copy-start(bf16[1,1024,1024]{2,1,0:T(8,128)(2,1)} %param.12) | copy-start | bytes 6291460
  1.3 14.9 %copy-start.1 = (bf16[1,1024,1024]{2,1,0:T(8,128)(2,1)S(1)}, bf16[1,1024,1024]{2,1,0:T(8,128)(2,1)}, u32[]{:S(2)}) copy-start(bf16[1,1024,1024]{2,1,0:T(8,128)(2,1)} %param.11) | copy-start | bytes 6291460
  1.4 14.9 %copy-start.3 = (bf16[4,1024,8]{1,2,0:T(8,128)(2,1)S(1)}, bf16[4,1024,8]{1,2,0:T(8,128)(2,1)}, u32[]{:S(2)}) copy-start(bf16[4,1024,8]{1,2,0:T(8,128)(2,1)} %param.13) | copy-start | bytes 196612
  16.2 11.0 %copy-start.2 = (bf16[4,1024,256]{2,1,0:T(8,128)(2,1)S(1)}, bf16[4,1024,256]{2,1,0:T(8,128)(2,1)}, u32[]{:S(2)}) copy-start(bf16[4,1024,256]{2,1,0:T(8,128)(2,1)} %tower_in_ref.1) | copy-start | bytes 6291460
  16.2 11.0 %copy-start.5 = (f32[4,256]{1,0:T(4,128)S(1)}, f32[4,256]{1,0:T(4,128)}, u32[]{:S(2)}) copy-start(f32[4,256]{1,0:T(4,128)} %bias_ref.1) | copy-start | bytes 12292
  16.3 11.0 %copy-start.6 = (f32[4,256]{1,0:T(4,128)S(1)}, f32[4,256]{1,0:T(4,128)}, u32[]{:S(2)}) copy-start(f32[4,256]{1,0:T(4,128)} %weight_ref.1) | copy-start | bytes 12292
  16.3 11.0 %copy-start.7 = (s32[2,4]{1,0:T(2,128)S(1)}, s32[2,4]{1,0:T(2,128)}, u32[]{:S(2)}) copy-start(s32[2,4]{1,0:T(2,128)} %labels_ref.1) | copy-start | bytes 100
  16.3 11.0 %copy-start.8 = (f32[4]{0:T(128)S(1)}, f32[4]{0:T(128)}, u32[]{:S(2)}) copy-start(f32[4]{0:T(128)} %param.17) | copy-start | bytes 52

commit v14 on v13

--- a/solution.py
+++ b/solution.py
@@ -289,6 +289,8 @@
     first_buf,
     second_buf,
     gate_buf,
+    hidden_turned,
+    every_turned,
     arrived_ref,
     wide_ref,
     sems,
@@ -297,49 +299,61 @@
     units = pre_ref.shape[1]
     flat = rows <= 64
     blocks = units // TILE
-    tops = width // TILE
-    second_cuts = [1, blocks - 1]
-    first_cuts = [tops - tops // 2, tops // 2 - tops // 4, tops // 4]
-
-    def second_step(step):
-        here = span(step, TILE)
-        second_buf[here, :] = dot(
-            hidden_ref[:, here], arrived_ref[:, :width], (0, 0)
-        ).astype(jnp.bfloat16)
+    copies = []
+
+    def turn(source, target):
+        def block(step):
+            here = span(step, LANES)
+            target[here, :] = source[:, here].astype(jnp.float32).T.astype(jnp.bfloat16)
+
+        steps(source.shape[1] // LANES, flat, block)
+
+    def gradient(left, right, buf, target, cuts):
+        at = 0
+        for cut in cuts:
+
+            def block(step, at=at):
+                here = span(step + at, LANES)
+                for across in range(buf.shape[1] // TILE):
+                    there = span(across, TILE)
+                    buf[here, there] = dot(left[here, :], right[:, there], (1, 0)).astype(
+                        jnp.bfloat16
+                    )
+
+            steps(cut, flat, block)
+            here = pl.ds(at * LANES, cut * LANES)
+            send(buf.at[here, :], target.at[here, :])
+            at += cut
+
+    def send(source, target):
+        copies.append(pltpu.make_async_copy(source, target, sems.at[len(copies)]))
+        copies[-1].start()
 
     def dpre_step(step):
         here = span(step, TILE)
         dhidden = dot(arrived_ref[:, :width], second_ref[here, :], (1, 1))
         dpre_ref[:, here] = (gelu_pair(pre_ref[:, here])[1] * dhidden).astype(jnp.bfloat16)
 
-    def first_step(step):
-        here = span(step, TILE)
-        first_buf[here, :] = dot(every_ref[:, here], dpre_ref[...], (0, 0)).astype(jnp.bfloat16)
-
-    copies = []
-
-    def send(source, target):
-        copies.append(pltpu.make_async_copy(source, target, sems.at[len(copies)]))
-        copies[-1].start()
-
-    def gradient(make, buf, target, cuts, at):
-        for cut in filter(None, cuts):
-            steps(cut, flat, lambda step: make(step + at))
-            here = pl.ds(at * TILE, cut * TILE)
-            send(buf.at[here, :], target.at[here, :])
-            at += cut
-
+    turn(hidden_ref, hidden_turned)
     unpack(got_ref, wide_ref)
     arrived_ref[...] = wide_ref[...].astype(jnp.bfloat16)
-    gradient(second_step, second_buf, grad_second_ref, second_cuts[:1], 0)
-    steps(blocks, flat, dpre_step)
-    gradient(second_step, second_buf, grad_second_ref, second_cuts[1:], second_cuts[0])
+    gradient(
+        hidden_turned, arrived_ref, second_buf, grad_second_ref, [2] * (units // LANES // 2)
+    )
+    turn(every_ref, every_turned)
     gate = dot(arrived_ref[:, width:], every_ref[...], (0, 0))
     for task in range(tasks):
         lanes = [at * tasks + task for at in range(3)]
         gate_buf[task] = sum(gate[lane : lane + 1] for lane in lanes)
     send(gate_buf, grad_gate_ref)
-    gradient(first_step, first_buf, grad_first_ref, first_cuts, 0)
+    steps(blocks, flat, dpre_step)
+    gradient(
+        every_turned,
+        dpre_ref,
+        first_buf,
+        grad_first_ref,
+        [2] * (width // LANES // 2 - 1) + [1, 1],
+    )
     for copy in copies:
         copy.wait()
 
@@ -363,9 +377,11 @@
             pltpu.VMEM((width, units), jnp.bfloat16),
             pltpu.VMEM((units, width), jnp.bfloat16),
             pltpu.VMEM((tasks, 1, width), jnp.float32),
+            pltpu.VMEM((units, rows), jnp.bfloat16),
+            pltpu.VMEM((width, rows), jnp.bfloat16),
             pltpu.VMEM((rows, width + LANES), jnp.bfloat16),
             pltpu.VMEM((rows, width + LANES), jnp.float32),
-            pltpu.SemaphoreType.DMA((6,)),
+            pltpu.SemaphoreType.DMA((units // TILE + width // TILE + 2,)),
         ],
         compiler_params=params(),
         cost_estimate=cost(6 * rows * width * units, 6 * width * units),

time: 42.1 us -> 42 us (level)
  no operation moved by 1% of the time
where the time goes in v14:
time: 42 us; the launch traced here: 41.8 us
  blocking collectives  34.9 us (83%)
  Pallas kernels  5.38 us (13%)
  between operations  0.75 us (2%)
  local copies, waits for them, and re-layouts  0.73 us (2%)
    all_to_all x1, blocking collectives, per_device(): got = lax.all_to_all(ahead(spread(events, devices)), BOTH, 0, 0, tiled=True)  14.8 us
    all_to_all x1, blocking collectives, per_device(): got = lax.all_to_all(message, BOTH, 0, 0, tiled=True)  10.1 us
    all_to_all x1, blocking collectives, per_device(): parts = lax.all_to_all(part, BOTH, 0, 0, tiled=True)  10 us
    pallas_call x1, Pallas kernels, backward(): pl.pallas_call(functools.partial(backward_kernel, tasks), out_shape=[jax....  3.17 us
    pallas_call x1, Pallas kernels, middle(): pl.pallas_call(functools.partial(middle_kernel, dp), out_shape=pltpu.VMEM...  1.25 us
    pallas_call x1, Pallas kernels, forward(): pl.pallas_call(forward_kernel, out_shape=[pltpu.VMEM(got.shape, jnp.bfloa...  0.96 us

profile of v14, /device:TPU:0, one launch (start us, length us, event | category | flops | bytes accessed | tf_op | source)
XLA Modules:
  0.0 41.8 jit_solution(10069886788580922695)
XLA Ops:
  0.6 0.0 copy-start.4
  0.6 0.7 %copy-done.4 = bf16[2,1024]{1,0:T(2,128)(2,1)S(1)} copy-done((bf16[2,1024]{1,0:T(2,128)(2,1)S(1)}, bf16[2,1024]{1,0:T(2,128)(2,1)}, u32[]{:S(2)}) %copy-start.4) | copy-done | bytes 4120
  1.3 0.0 copy-start
  1.3 0.0 copy-start.1
  1.4 0.0 copy-start.3
  1.4 14.8 %all_to_all.15.got_ref = bf16[32,2,1024]{2,1,0:T(2,128)(2,1)S(1)} all-to-all(bf16[32,2,1024]{2,1,0:T(2,128)(2,1)S(1)} %ahead.1), channel_id=1, replica_groups=mesh['dp'=4,'expert'=8] {'dp','expert'}, dimensions={0} | all-to-all | bytes 262144 | tf_op jit(solution)/shard_map/all_to_all | solution.py:401
  16.2 0.0 copy-done
  16.2 0.0 copy-done.1
  16.2 0.0 copy-done.3
  16.2 0.0 copy-start.2
  16.2 0.0 copy-start.5
  16.3 0.0 copy-start.6
  16.3 0.0 copy-start.7
  16.3 0.0 copy-start.8
  16.3 1.0 %forward.1 = (bf16[32,2,1024]{2,1,0:T(2,128)(2,1)S(1)}, bf16[64,1024]{1,0:T(8,128)(2,1)S(1)}, f32[64,1024]{1,0:T(8,128)S(1)}, bf16[64,1024]{1,0:T(8,128)(2,1)S(1)}, f32[16,128]{1,0:T(8,128)S(1)}) custom-call(bf16[32,2,1024]{2,1,0:T(2,128)(2,1)S(1)} %all_to_all.15.got_ref, bf16[2,1024]{1,0:T(2,128)(2,1)S(1)} %copy-done.4, bf16[32,1024]{1,0:T(8,128)(2,1)S(1)} %bitcast.12, ...), custom_call_target="tpu_custom_call" | custom-call | flops 268435456 | bytes 4194304 | tf_op jit(solution)/shard_map/forward/pallas_call | solution.py:171
  17.3 10.0 %all_to_all.16.parts_ref = bf16[32,2,1024]{2,1,0:T(2,128)(2,1)S(1)} all-to-all(bf16[32,2,1024]{2,1,0:T(2,128)(2,1)S(1)} %get-tuple-element.11), channel_id=1, replica_groups=mesh['dp'=4,'expert'=8] {'dp','expert'}, dimensions={0} | all-to-all | bytes 262144 | tf_op jit(solution)/shard_map/all_to_all | solution.py:404
  27.3 0.0 copy-done.2
  27.3 0.0 copy-done.5
  27.3 0.0 copy-done.6
  27.3 0.0 copy-done.7
  27.3 0.0 copy-done.8
  27.3 1.2 %middle.1 = bf16[32,2,1152]{2,1,0:T(2,128)(2,1)S(1)} custom-call(bf16[32,2,1024]{2,1,0:T(2,128)(2,1)S(1)} %all_to_all.16.parts_ref, f32[16,128]{1,0:T(8,128)S(1)} %get-tuple-element.12.prob_ref, s32[2,4]{1,0:T(2,128)S(1)} %copy-done.7, bf16[4,1024,256]{2,1,0:T(8,128)(2,1)S(1)} %copy-done.2, f32[4,256]{1,0:T(4,128)S(1)} %copy-done.5, f32[4,256]{1,0:T(4,128)S(1)} %copy-done.6, ...), custom_call_target="tpu_custom_call" | custom-call | flops 33554432 | bytes 2097152 | tf_op jit(solution)/shard_map/middle/pallas_call | solution.py:268
  28.5 10.1 %all_to_all.17.got_ref = bf16[32,2,1152]{2,1,0:T(2,128)(2,1)S(1)} all-to-all(bf16[32,2,1152]{2,1,0:T(2,128)(2,1)S(1)} %middle.1), channel_id=1, replica_groups=mesh['dp'=4,'expert'=8] {'dp','expert'}, dimensions={0} | all-to-all | bytes 294912 | tf_op jit(solution)/shard_map/all_to_all | solution.py:409
  38.6 3.2 %backward.1 = (bf16[1024,1024]{1,0:T(8,128)(2,1)}, bf16[1024,1024]{1,0:T(8,128)(2,1)}, f32[4,1,1024]{2,1,0:T(1,128)}) custom-call(bf16[32,2,1152]{2,1,0:T(2,128)(2,1)S(1)} %all_to_all.17.got_ref, bf16[64,1024]{1,0:T(8,128)(2,1)S(1)} %get-tuple-element.13.every_ref, bf16[64,1024]{1,0:T(8,128)(2,1)S(1)} %get-tuple-element.14.hidden_ref, ...), custom_call_target="tpu_custom_call" | custom-call | flops 402653184 | bytes 6291456 | tf_op jit(solution)/shard_map/backward/pallas_call | solution.py:366
  (2 shorter events, 0.0 us)
Async XLA Ops:
  0.6 0.7 %copy-start.4 = (bf16[2,1024]{1,0:T(2,128)(2,1)S(1)}, bf16[2,1024]{1,0:T(2,128)(2,1)}, u32[]{:S(2)}) copy-start(bf16[2,1024]{1,0:T(2,128)(2,1)} %events_ref.1) | copy-start | bytes 12292
  1.3 14.9 %copy-start = (bf16[1,1024,1024]{2,1,0:T(8,128)(2,1)S(1)}, bf16[1,1024,1024]{2,1,0:T(8,128)(2,1)}, u32[]{:S(2)}) copy-start(bf16[1,1024,1024]{2,1,0:T(8,128)(2,1)} %param.12) | copy-start | bytes 6291460
  1.3 14.9 %copy-start.1 = (bf16[1,1024,1024]{2,1,0:T(8,128)(2,1)S(1)}, bf16[1,1024,1024]{2,1,0:T(8,128)(2,1)}, u32[]{:S(2)}) copy-start(bf16[1,1024,1024]{2,1,0:T(8,128)(2,1)} %param.11) | copy-start | bytes 6291460
  1.4 14.9 %copy-start.3 = (bf16[4,1024,8]{1,2,0:T(8,128)(2,1)S(1)}, bf16[4,1024,8]{1,2,0:T(8,128)(2,1)}, u32[]{:S(2)}) copy-start(bf16[4,1024,8]{1,2,0:T(8,128)(2,1)} %param.13) | copy-start | bytes 196612
  16.2 11.0 %copy-start.2 = (bf16[4,1024,256]{2,1,0:T(8,128)(2,1)S(1)}, bf16[4,1024,256]{2,1,0:T(8,128)(2,1)}, u32[]{:S(2)}) copy-start(bf16[4,1024,256]{2,1,0:T(8,128)(2,1)} %tower_in_ref.1) | copy-start | bytes 6291460
  16.2 11.0 %copy-start.5 = (f32[4,256]{1,0:T(4,128)S(1)}, f32[4,256]{1,0:T(4,128)}, u32[]{:S(2)}) copy-start(f32[4,256]{1,0:T(4,128)} %bias_ref.1) | copy-start | bytes 12292
  16.3 11.0 %copy-start.6 = (f32[4,256]{1,0:T(4,128)S(1)}, f32[4,256]{1,0:T(4,128)}, u32[]{:S(2)}) copy-start(f32[4,256]{1,0:T(4,128)} %weight_ref.1) | copy-start | bytes 12292
  16.3 11.0 %copy-start.7 = (s32[2,4]{1,0:T(2,128)S(1)}, s32[2,4]{1,0:T(2,128)}, u32[]{:S(2)}) copy-start(s32[2,4]{1,0:T(2,128)} %labels_ref.1) | copy-start | bytes 100
  16.3 11.0 %copy-start.8 = (f32[4]{0:T(128)S(1)}, f32[4]{0:T(128)}, u32[]{:S(2)}) copy-start(f32[4]{0:T(128)} %param.17) | copy-start | bytes 52

commit v15 on v14

--- a/solution.py
+++ b/solution.py
@@ -202,15 +202,27 @@
     tasks = tower_in_ref.shape[0]
     float32, bfloat16 = jnp.float32, jnp.bfloat16
 
-    for expert in range(experts):
-        total = parts_ref[expert].astype(float32)
-        for at in range(1, dp):
-            total = total + parts_ref[at * experts + expert].astype(float32)
-        outs_ref[expert * own : (expert + 1) * own, :] = total
-    outs = outs_ref[...].astype(bfloat16)
+    features = [slice(at, at + TILE) for at in range(0, width, TILE)]
+    singles = [0.0] * tasks
+    for block in features:
+        for expert in range(experts):
+            total = parts_ref[expert, :, block].astype(float32)
+            for at in range(1, dp):
+                total = total + parts_ref[at * experts + expert, :, block].astype(float32)
+            outs_ref[expert * own : (expert + 1) * own, block] = total
+        outs = outs_ref[:, block].astype(bfloat16)
+        for task in range(tasks):
+            singles[task] = singles[task] + dot(outs, tower_in_ref[task, block, :], (1, 0))
+
     labels = by_row(labels_ref[...], slots)
     lane = iota((slots, LANES), 1)
     units = tower_in_ref.shape[2]
+
+    def store(value, block):
+        for expert in range(experts):
+            here = slice(expert * own, (expert + 1) * own)
+            for at in range(dp):
+                message_ref[at * experts + expert, :, block] = value[here]
 
     def wide(ref):
         return jnp.concatenate([ref[task : task + 1, :] for task in range(tasks)], 1)
@@ -224,9 +236,7 @@
         )
 
     probs = [prob_ref[:, task : task + 1] for task in range(tasks)]
-    single = jnp.concatenate(
-        [dot(outs, tower_in_ref[task], (1, 0)) for task in range(tasks)], 1
-    )
+    single = jnp.concatenate(singles, 1)
     linear = single * each(probs)
     shift = own
     while shift < slots:
@@ -242,25 +252,20 @@
     dtower = slope * each(dlogit)
     stack = [piece.astype(float32) for piece in pieces_of(dtower)[:2]]
     stack = jnp.concatenate(stack, 0).astype(bfloat16)
-    turned = [
-        dot(lanes_of(stack, task), tower_in_ref[task], (1, 1)) for task in range(tasks)
-    ]
     rest = dtower * (single - linear)
     lanes = jnp.zeros((slots, LANES), float32)
-    dexpert = jnp.zeros((slots, width), float32)
     for task in range(tasks):
         dgate = probs[task] * jnp.sum(lanes_of(rest, task), -1, keepdims=True)
         for at, piece in enumerate(pieces_of(dgate)):
             lanes = jnp.where(lane == at * tasks + task, piece.astype(float32), lanes)
-        dmixed = (turned[task][:slots] + turned[task][slots:]).astype(bfloat16)
-        dexpert = dexpert + probs[task] * dmixed.astype(float32)
-    dexpert = dexpert.astype(bfloat16)
-    lanes = lanes.astype(bfloat16)
-    for expert in range(experts):
-        here = slice(expert * own, (expert + 1) * own)
-        for at in range(dp):
-            message_ref[at * experts + expert, :, :width] = dexpert[here]
-            message_ref[at * experts + expert, :, width:] = lanes[here]
+    store(lanes.astype(bfloat16), slice(width, width + LANES))
+    for block in features:
+        dexpert = jnp.zeros((slots, TILE), float32)
+        for task in range(tasks):
+            turned = dot(lanes_of(stack, task), tower_in_ref[task, block, :], (1, 1))
+            dmixed = (turned[:slots] + turned[slots:]).astype(bfloat16)
+            dexpert = dexpert + probs[task] * dmixed.astype(float32)
+        store(dexpert.astype(bfloat16), block)
 
 
 def middle(dp, parts, prob, labels, tower_in, bias, weight, shift):
@@ -289,8 +294,6 @@
     first_buf,
     second_buf,
     gate_buf,
-    hidden_turned,
-    every_turned,
     arrived_ref,
     wide_ref,
     sems,
@@ -301,27 +304,11 @@
     blocks = units // TILE
     copies = []
 
-    def turn(source, target):
-        def block(step):
-            here = span(step, LANES)
-            target[here, :] = source[:, here].astype(jnp.float32).T.astype(jnp.bfloat16)
-
-        steps(source.shape[1] // LANES, flat, block)
-
     def gradient(left, right, buf, target, cuts):
         at = 0
         for cut in cuts:
-
-            def block(step, at=at):
-                here = span(step + at, LANES)
-                for across in range(buf.shape[1] // TILE):
-                    there = span(across, TILE)
-                    buf[here, there] = dot(left[here, :], right[:, there], (1, 0)).astype(
-                        jnp.bfloat16
-                    )
-
-            steps(cut, flat, block)
             here = pl.ds(at * LANES, cut * LANES)
+            buf[here, :] = dot(left[:, here], right(), (0, 0)).astype(jnp.bfloat16)
             send(buf.at[here, :], target.at[here, :])
             at += cut
 
@@ -334,25 +321,25 @@
         dhidden = dot(arrived_ref[:, :width], second_ref[here, :], (1, 1))
         dpre_ref[:, here] = (gelu_pair(pre_ref[:, here])[1] * dhidden).astype(jnp.bfloat16)
 
-    turn(hidden_ref, hidden_turned)
     unpack(got_ref, wide_ref)
     arrived_ref[...] = wide_ref[...].astype(jnp.bfloat16)
+    pairs = units // LANES // 2 - 1
     gradient(
-        hidden_turned, arrived_ref, second_buf, grad_second_ref, [2] * (units // LANES // 2)
-    )
-    turn(every_ref, every_turned)
+        hidden_ref,
+        lambda: arrived_ref[:, :width],
+        second_buf,
+        grad_second_ref,
+        [1] + [2] * pairs + [1],
+    )
     gate = dot(arrived_ref[:, width:], every_ref[...], (0, 0))
     for task in range(tasks):
         lanes = [at * tasks + task for at in range(3)]
         gate_buf[task] = sum(gate[lane : lane + 1] for lane in lanes)
     send(gate_buf, grad_gate_ref)
     steps(blocks, flat, dpre_step)
+    pairs = width // LANES // 2 - 1
     gradient(
-        every_turned,
-        dpre_ref,
-        first_buf,
-        grad_first_ref,
-        [2] * (width // LANES // 2 - 1) + [1, 1],
+        every_ref, lambda: dpre_ref[...], first_buf, grad_first_ref, [2] * pairs + [1, 1]
     )
     for copy in copies:
         copy.wait()
@@ -377,11 +364,9 @@
             pltpu.VMEM((width, units), jnp.bfloat16),
             pltpu.VMEM((units, width), jnp.bfloat16),
             pltpu.VMEM((tasks, 1, width), jnp.float32),
-            pltpu.VMEM((units, rows), jnp.bfloat16),
-            pltpu.VMEM((width, rows), jnp.bfloat16),
             pltpu.VMEM((rows, width + LANES), jnp.bfloat16),
             pltpu.VMEM((rows, width + LANES), jnp.float32),
-            pltpu.SemaphoreType.DMA((units // TILE + width // TILE + 2,)),
+            pltpu.SemaphoreType.DMA((units // TILE + width // TILE + 3,)),
         ],
         compiler_params=params(),
         cost_estimate=cost(6 * rows * width * units, 6 * width * units),

time: 42 us -> 41.9 us (level)
  no operation moved by 1% of the time
where the time goes in v15:
time: 41.9 us; the launch traced here: 41.7 us
  blocking collectives  34.9 us (83%)
  Pallas kernels  5.27 us (13%)
  between operations  0.75 us (2%)
  local copies, waits for them, and re-layouts  0.73 us (2%)
    all_to_all x1, blocking collectives, per_device(): got = lax.all_to_all(ahead(spread(events, devices)), BOTH, 0, 0, tiled=True)  14.8 us
    all_to_all x1, blocking collectives, per_device(): got = lax.all_to_all(message, BOTH, 0, 0, tiled=True)  10.1 us
    all_to_all x1, blocking collectives, per_device(): parts = lax.all_to_all(part, BOTH, 0, 0, tiled=True)  10 us
    pallas_call x1, Pallas kernels, backward(): pl.pallas_call(functools.partial(backward_kernel, tasks), out_shape=[jax....  3.08 us
    pallas_call x1, Pallas kernels, middle(): pl.pallas_call(functools.partial(middle_kernel, dp), out_shape=pltpu.VMEM...  1.23 us
    pallas_call x1, Pallas kernels, forward(): pl.pallas_call(forward_kernel, out_shape=[pltpu.VMEM(got.shape, jnp.bfloa...  0.96 us

profile of v15, /device:TPU:0, one launch (start us, length us, event | category | flops | bytes accessed | tf_op | source)
XLA Modules:
  0.0 41.7 jit_solution(3273250268479424106)
XLA Ops:
  0.6 0.0 copy-start.4
  0.6 0.7 %copy-done.4 = bf16[2,1024]{1,0:T(2,128)(2,1)S(1)} copy-done((bf16[2,1024]{1,0:T(2,128)(2,1)S(1)}, bf16[2,1024]{1,0:T(2,128)(2,1)}, u32[]{:S(2)}) %copy-start.4) | copy-done | bytes 4120
  1.3 0.0 copy-start
  1.3 0.0 copy-start.1
  1.4 0.0 copy-start.3
  1.4 14.8 %all_to_all.15.got_ref = bf16[32,2,1024]{2,1,0:T(2,128)(2,1)S(1)} all-to-all(bf16[32,2,1024]{2,1,0:T(2,128)(2,1)S(1)} %ahead.1), channel_id=1, replica_groups=mesh['dp'=4,'expert'=8] {'dp','expert'}, dimensions={0} | all-to-all | bytes 262144 | tf_op jit(solution)/shard_map/all_to_all | solution.py:386
  16.2 0.0 copy-done
  16.2 0.0 copy-done.1
  16.2 0.0 copy-done.3
  16.2 0.0 copy-start.2
  16.2 0.0 copy-start.5
  16.3 0.0 copy-start.6
  16.3 0.0 copy-start.7
  16.3 0.0 copy-start.8
  16.3 1.0 %forward.1 = (bf16[32,2,1024]{2,1,0:T(2,128)(2,1)S(1)}, bf16[64,1024]{1,0:T(8,128)(2,1)S(1)}, f32[64,1024]{1,0:T(8,128)S(1)}, bf16[64,1024]{1,0:T(8,128)(2,1)S(1)}, f32[16,128]{1,0:T(8,128)S(1)}) custom-call(bf16[32,2,1024]{2,1,0:T(2,128)(2,1)S(1)} %all_to_all.15.got_ref, bf16[2,1024]{1,0:T(2,128)(2,1)S(1)} %copy-done.4, bf16[32,1024]{1,0:T(8,128)(2,1)S(1)} %bitcast.12, ...), custom_call_target="tpu_custom_call" | custom-call | flops 268435456 | bytes 4194304 | tf_op jit(solution)/shard_map/forward/pallas_call | solution.py:171
  17.3 10.0 %all_to_all.16.parts_ref = bf16[32,2,1024]{2,1,0:T(2,128)(2,1)S(1)} all-to-all(bf16[32,2,1024]{2,1,0:T(2,128)(2,1)S(1)} %get-tuple-element.11), channel_id=1, replica_groups=mesh['dp'=4,'expert'=8] {'dp','expert'}, dimensions={0} | all-to-all | bytes 262144 | tf_op jit(solution)/shard_map/all_to_all | solution.py:389
  27.3 0.0 copy-done.2
  27.3 0.0 copy-done.5
  27.3 0.0 copy-done.6
  27.3 0.0 copy-done.7
  27.3 0.0 copy-done.8
  27.3 1.2 %middle.1 = bf16[32,2,1152]{2,1,0:T(2,128)(2,1)S(1)} custom-call(bf16[32,2,1024]{2,1,0:T(2,128)(2,1)S(1)} %all_to_all.16.parts_ref, f32[16,128]{1,0:T(8,128)S(1)} %get-tuple-element.12.prob_ref, s32[2,4]{1,0:T(2,128)S(1)} %copy-done.7, bf16[4,1024,256]{2,1,0:T(8,128)(2,1)S(1)} %copy-done.2, f32[4,256]{1,0:T(4,128)S(1)} %copy-done.5, f32[4,256]{1,0:T(4,128)S(1)} %copy-done.6, ...), custom_call_target="tpu_custom_call" | custom-call | flops 33554432 | bytes 2097152 | tf_op jit(solution)/shard_map/middle/pallas_call | solution.py:273
  28.5 10.1 %all_to_all.17.got_ref = bf16[32,2,1152]{2,1,0:T(2,128)(2,1)S(1)} all-to-all(bf16[32,2,1152]{2,1,0:T(2,128)(2,1)S(1)} %middle.1), channel_id=1, replica_groups=mesh['dp'=4,'expert'=8] {'dp','expert'}, dimensions={0} | all-to-all | bytes 294912 | tf_op jit(solution)/shard_map/all_to_all | solution.py:394
  38.6 3.1 %backward.1 = (bf16[1024,1024]{1,0:T(8,128)(2,1)}, bf16[1024,1024]{1,0:T(8,128)(2,1)}, f32[4,1,1024]{2,1,0:T(1,128)}) custom-call(bf16[32,2,1152]{2,1,0:T(2,128)(2,1)S(1)} %all_to_all.17.got_ref, bf16[64,1024]{1,0:T(8,128)(2,1)S(1)} %get-tuple-element.13.every_ref, bf16[64,1024]{1,0:T(8,128)(2,1)S(1)} %get-tuple-element.14.hidden_ref, ...), custom_call_target="tpu_custom_call" | custom-call | flops 402653184 | bytes 6291456 | tf_op jit(solution)/shard_map/backward/pallas_call | solution.py:353
  (2 shorter events, 0.0 us)
Async XLA Ops:
  0.6 0.7 %copy-start.4 = (bf16[2,1024]{1,0:T(2,128)(2,1)S(1)}, bf16[2,1024]{1,0:T(2,128)(2,1)}, u32[]{:S(2)}) copy-start(bf16[2,1024]{1,0:T(2,128)(2,1)} %events_ref.1) | copy-start | bytes 12292
  1.3 14.9 %copy-start = (bf16[1,1024,1024]{2,1,0:T(8,128)(2,1)S(1)}, bf16[1,1024,1024]{2,1,0:T(8,128)(2,1)}, u32[]{:S(2)}) copy-start(bf16[1,1024,1024]{2,1,0:T(8,128)(2,1)} %param.12) | copy-start | bytes 6291460
  1.3 14.9 %copy-start.1 = (bf16[1,1024,1024]{2,1,0:T(8,128)(2,1)S(1)}, bf16[1,1024,1024]{2,1,0:T(8,128)(2,1)}, u32[]{:S(2)}) copy-start(bf16[1,1024,1024]{2,1,0:T(8,128)(2,1)} %param.11) | copy-start | bytes 6291460
  1.4 14.9 %copy-start.3 = (bf16[4,1024,8]{1,2,0:T(8,128)(2,1)S(1)}, bf16[4,1024,8]{1,2,0:T(8,128)(2,1)}, u32[]{:S(2)}) copy-start(bf16[4,1024,8]{1,2,0:T(8,128)(2,1)} %param.13) | copy-start | bytes 196612
  16.2 11.0 %copy-start.2 = (bf16[4,1024,256]{2,1,0:T(8,128)(2,1)S(1)}, bf16[4,1024,256]{2,1,0:T(8,128)(2,1)}, u32[]{:S(2)}) copy-start(bf16[4,1024,256]{2,1,0:T(8,128)(2,1)} %tower_in_ref.1) | copy-start | bytes 6291460
  16.2 11.0 %copy-start.5 = (f32[4,256]{1,0:T(4,128)S(1)}, f32[4,256]{1,0:T(4,128)}, u32[]{:S(2)}) copy-start(f32[4,256]{1,0:T(4,128)} %bias_ref.1) | copy-start | bytes 12292
  16.3 11.0 %copy-start.6 = (f32[4,256]{1,0:T(4,128)S(1)}, f32[4,256]{1,0:T(4,128)}, u32[]{:S(2)}) copy-start(f32[4,256]{1,0:T(4,128)} %weight_ref.1) | copy-start | bytes 12292
  16.3 11.0 %copy-start.7 = (s32[2,4]{1,0:T(2,128)S(1)}, s32[2,4]{1,0:T(2,128)}, u32[]{:S(2)}) copy-start(s32[2,4]{1,0:T(2,128)} %labels_ref.1) | copy-start | bytes 100
  16.3 11.0 %copy-start.8 = (f32[4]{0:T(128)S(1)}, f32[4]{0:T(128)}, u32[]{:S(2)}) copy-start(f32[4]{0:T(128)} %param.17) | copy-start | bytes 52

commit v16 on v15

--- a/solution.py
+++ b/solution.py
@@ -8,6 +8,7 @@
 from jax.sharding import PartitionSpec as P
 
 BOTH = ("dp", "expert")
+SLOTS = ("expert", "dp")
 LANES = 128
 TILE = 256
 GELU_C = 0.7978845608028654
@@ -206,9 +207,9 @@
     singles = [0.0] * tasks
     for block in features:
         for expert in range(experts):
-            total = parts_ref[expert, :, block].astype(float32)
+            total = parts_ref[expert * dp, :, block].astype(float32)
             for at in range(1, dp):
-                total = total + parts_ref[at * experts + expert, :, block].astype(float32)
+                total = total + parts_ref[expert * dp + at, :, block].astype(float32)
             outs_ref[expert * own : (expert + 1) * own, block] = total
         outs = outs_ref[:, block].astype(bfloat16)
         for task in range(tasks):
@@ -222,7 +223,7 @@
         for expert in range(experts):
             here = slice(expert * own, (expert + 1) * own)
             for at in range(dp):
-                message_ref[at * experts + expert, :, block] = value[here]
+                message_ref[expert * dp + at, :, block] = value[here]
 
     def wide(ref):
         return jnp.concatenate([ref[task : task + 1, :] for task in range(tasks)], 1)
@@ -383,15 +384,15 @@
     tasks = tower_in.shape[0]
     gate = jnp.transpose(gate_weight, (0, 2, 1)).reshape(tasks * experts, events.shape[1])
 
-    got = lax.all_to_all(ahead(spread(events, devices)), BOTH, 0, 0, tiled=True)
+    got = lax.all_to_all(ahead(spread(events, devices)), SLOTS, 0, 0, tiled=True)
     part, every, pre, hidden, prob = forward(got, events, gate, w_in[0], w_out[0], experts)
 
-    parts = lax.all_to_all(part, BOTH, 0, 0, tiled=True)
+    parts = lax.all_to_all(part, SLOTS, 0, 0, tiled=True)
     message = middle(
         dp, parts, prob, labels, tower_in, tower_bias, tower_out, tower_out_bias[None]
     )
 
-    got = lax.all_to_all(message, BOTH, 0, 0, tiled=True)
+    got = lax.all_to_all(message, SLOTS, 0, 0, tiled=True)
     grad_first, grad_second, grad_gate = backward(got, every, hidden, pre, w_out[0], tasks)
     return (grad_first[None], grad_second[None], jnp.transpose(grad_gate, (0, 2, 1)))
 

time: 41.9 us -> 42.5 us (1.014)
  blocking collectives: 34.9 us -> 35.5 us
    all_to_all x3, blocking collectives: 34.9 us -> 35.5 us  [the longest x1 15.3 us: per_device(): lax.all_to_all(ahead(spread(events, devices)), SLOTS, 0, 0, tiled=True)]
where the time goes in v16:
time: 42.5 us; the launch traced here: 42.3 us
  blocking collectives  35.5 us (84%)
  Pallas kernels  5.27 us (12%)
  between operations  0.75 us (2%)
  local copies, waits for them, and re-layouts  0.73 us (2%)
    all_to_all x1, blocking collectives, per_device(): lax.all_to_all(ahead(spread(events, devices)), SLOTS, 0, 0, tiled=True)  15.3 us
    all_to_all x1, blocking collectives, per_device(): got = lax.all_to_all(message, SLOTS, 0, 0, tiled=True)  10.2 us
    all_to_all x1, blocking collectives, per_device(): parts = lax.all_to_all(part, SLOTS, 0, 0, tiled=True)  10 us
    pallas_call x1, Pallas kernels, backward(): pl.pallas_call(functools.partial(backward_kernel, tasks), out_shape=[jax....  3.08 us
    pallas_call x1, Pallas kernels, middle(): pl.pallas_call(functools.partial(middle_kernel, dp), out_shape=pltpu.VMEM...  1.22 us
    pallas_call x1, Pallas kernels, forward(): pl.pallas_call(forward_kernel, out_shape=[pltpu.VMEM(got.shape, jnp.bfloa...  0.96 us

profile of v16, /device:TPU:0, one launch (start us, length us, event | category | flops | bytes accessed | tf_op | source)
XLA Modules:
  0.0 42.3 jit_solution(8818190159327255615)
XLA Ops:
  0.6 0.0 copy-start.4
  0.6 0.7 %copy-done.4 = bf16[2,1024]{1,0:T(2,128)(2,1)S(1)} copy-done((bf16[2,1024]{1,0:T(2,128)(2,1)S(1)}, bf16[2,1024]{1,0:T(2,128)(2,1)}, u32[]{:S(2)}) %copy-start.4) | copy-done | bytes 4120
  1.3 0.0 copy-start
  1.3 0.0 copy-start.1
  1.4 0.0 copy-start.3
  1.4 15.3 %all_to_all.15.got_ref = bf16[32,2,1024]{2,1,0:T(2,128)(2,1)S(1)} all-to-all(bf16[32,2,1024]{2,1,0:T(2,128)(2,1)S(1)} %ahead.1), channel_id=1, replica_groups=mesh['dp'=4,'expert'=8] {'expert','dp'}, dimensions={0} | all-to-all | bytes 262144 | tf_op jit(solution)/shard_map/all_to_all | solution.py:387
  16.7 0.0 copy-done
  16.7 0.0 copy-done.1
  16.7 0.0 copy-done.3
  16.7 0.0 copy-start.2
  16.7 0.0 copy-start.5
  16.7 0.0 copy-start.6
  16.8 0.0 copy-start.7
  16.8 0.0 copy-start.8
  16.8 1.0 %forward.1 = (bf16[32,2,1024]{2,1,0:T(2,128)(2,1)S(1)}, bf16[64,1024]{1,0:T(8,128)(2,1)S(1)}, f32[64,1024]{1,0:T(8,128)S(1)}, bf16[64,1024]{1,0:T(8,128)(2,1)S(1)}, f32[16,128]{1,0:T(8,128)S(1)}) custom-call(bf16[32,2,1024]{2,1,0:T(2,128)(2,1)S(1)} %all_to_all.15.got_ref, bf16[2,1024]{1,0:T(2,128)(2,1)S(1)} %copy-done.4, bf16[32,1024]{1,0:T(8,128)(2,1)S(1)} %bitcast.12, ...), custom_call_target="tpu_custom_call" | custom-call | flops 268435456 | bytes 4194304 | tf_op jit(solution)/shard_map/forward/pallas_call | solution.py:172
  17.7 10.0 %all_to_all.16.parts_ref = bf16[32,2,1024]{2,1,0:T(2,128)(2,1)S(1)} all-to-all(bf16[32,2,1024]{2,1,0:T(2,128)(2,1)S(1)} %get-tuple-element.11), channel_id=1, replica_groups=mesh['dp'=4,'expert'=8] {'expert','dp'}, dimensions={0} | all-to-all | bytes 262144 | tf_op jit(solution)/shard_map/all_to_all | solution.py:390
  27.7 0.0 copy-done.2
  27.8 0.0 copy-done.5
  27.8 0.0 copy-done.6
  27.8 0.0 copy-done.7
  27.8 0.0 copy-done.8
  27.8 1.2 %middle.1 = bf16[32,2,1152]{2,1,0:T(2,128)(2,1)S(1)} custom-call(bf16[32,2,1024]{2,1,0:T(2,128)(2,1)S(1)} %all_to_all.16.parts_ref, f32[16,128]{1,0:T(8,128)S(1)} %get-tuple-element.12.prob_ref, s32[2,4]{1,0:T(2,128)S(1)} %copy-done.7, bf16[4,1024,256]{2,1,0:T(8,128)(2,1)S(1)} %copy-done.2, f32[4,256]{1,0:T(4,128)S(1)} %copy-done.5, f32[4,256]{1,0:T(4,128)S(1)} %copy-done.6, ...), custom_call_target="tpu_custom_call" | custom-call | flops 33554432 | bytes 2097152 | tf_op jit(solution)/shard_map/middle/pallas_call | solution.py:274
  29.0 10.2 %all_to_all.17.got_ref = bf16[32,2,1152]{2,1,0:T(2,128)(2,1)S(1)} all-to-all(bf16[32,2,1152]{2,1,0:T(2,128)(2,1)S(1)} %middle.1), channel_id=1, replica_groups=mesh['dp'=4,'expert'=8] {'expert','dp'}, dimensions={0} | all-to-all | bytes 294912 | tf_op jit(solution)/shard_map/all_to_all | solution.py:395
  39.2 3.1 %backward.1 = (bf16[1024,1024]{1,0:T(8,128)(2,1)}, bf16[1024,1024]{1,0:T(8,128)(2,1)}, f32[4,1,1024]{2,1,0:T(1,128)}) custom-call(bf16[32,2,1152]{2,1,0:T(2,128)(2,1)S(1)} %all_to_all.17.got_ref, bf16[64,1024]{1,0:T(8,128)(2,1)S(1)} %get-tuple-element.13.every_ref, bf16[64,1024]{1,0:T(8,128)(2,1)S(1)} %get-tuple-element.14.hidden_ref, ...), custom_call_target="tpu_custom_call" | custom-call | flops 402653184 | bytes 6291456 | tf_op jit(solution)/shard_map/backward/pallas_call | solution.py:354
  (2 shorter events, 0.0 us)
Async XLA Ops:
  0.6 0.7 %copy-start.4 = (bf16[2,1024]{1,0:T(2,128)(2,1)S(1)}, bf16[2,1024]{1,0:T(2,128)(2,1)}, u32[]{:S(2)}) copy-start(bf16[2,1024]{1,0:T(2,128)(2,1)} %events_ref.1) | copy-start | bytes 12292
  1.3 15.4 %copy-start = (bf16[1,1024,1024]{2,1,0:T(8,128)(2,1)S(1)}, bf16[1,1024,1024]{2,1,0:T(8,128)(2,1)}, u32[]{:S(2)}) copy-start(bf16[1,1024,1024]{2,1,0:T(8,128)(2,1)} %param.12) | copy-start | bytes 6291460
  1.3 15.4 %copy-start.1 = (bf16[1,1024,1024]{2,1,0:T(8,128)(2,1)S(1)}, bf16[1,1024,1024]{2,1,0:T(8,128)(2,1)}, u32[]{:S(2)}) copy-start(bf16[1,1024,1024]{2,1,0:T(8,128)(2,1)} %param.11) | copy-start | bytes 6291460
  1.4 15.4 %copy-start.3 = (bf16[4,1024,8]{1,2,0:T(8,128)(2,1)S(1)}, bf16[4,1024,8]{1,2,0:T(8,128)(2,1)}, u32[]{:S(2)}) copy-start(bf16[4,1024,8]{1,2,0:T(8,128)(2,1)} %param.13) | copy-start | bytes 196612
  16.7 11.0 %copy-start.2 = (bf16[4,1024,256]{2,1,0:T(8,128)(2,1)S(1)}, bf16[4,1024,256]{2,1,0:T(8,128)(2,1)}, u32[]{:S(2)}) copy-start(bf16[4,1024,256]{2,1,0:T(8,128)(2,1)} %tower_in_ref.1) | copy-start | bytes 6291460
  16.7 11.0 %copy-start.5 = (f32[4,256]{1,0:T(4,128)S(1)}, f32[4,256]{1,0:T(4,128)}, u32[]{:S(2)}) copy-start(f32[4,256]{1,0:T(4,128)} %bias_ref.1) | copy-start | bytes 12292
  16.7 11.0 %copy-start.6 = (f32[4,256]{1,0:T(4,128)S(1)}, f32[4,256]{1,0:T(4,128)}, u32[]{:S(2)}) copy-start(f32[4,256]{1,0:T(4,128)} %weight_ref.1) | copy-start | bytes 12292
  16.8 11.0 %copy-start.7 = (s32[2,4]{1,0:T(2,128)S(1)}, s32[2,4]{1,0:T(2,128)}, u32[]{:S(2)}) copy-start(s32[2,4]{1,0:T(2,128)} %labels_ref.1) | copy-start | bytes 100
  16.8 11.0 %copy-start.8 = (f32[4]{0:T(128)S(1)}, f32[4]{0:T(128)}, u32[]{:S(2)}) copy-start(f32[4]{0:T(128)} %param.17) | copy-start | bytes 52

commit v17 on v15

--- a/solution.py
+++ b/solution.py
@@ -93,10 +93,15 @@
     )(value)
 
 
-def unpack(message_ref, rows_ref):
+def unpack(message_ref, rows_ref, block):
     own = message_ref.shape[1]
     for at in range(message_ref.shape[0]):
-        rows_ref[at * own : (at + 1) * own, :] = message_ref[at].astype(jnp.float32)
+        here = slice(at * own, (at + 1) * own)
+        rows_ref[here, block] = message_ref[at, :, block].astype(jnp.float32)
+
+
+def blocks_of(count, size):
+    return [slice(at, at + size) for at in range(0, count, size)]
 
 
 def iota(shape, axis):
@@ -143,14 +148,21 @@
         probs = jnp.where(lane == task, prob / jnp.sum(gates, -1, keepdims=True), probs)
     prob_ref[...] = probs
 
-    unpack(got_ref, wide_ref)
+    halves = blocks_of(every_ref.shape[1], every_ref.shape[1] // 2)
+    if rows != chunk:
+        unpack(got_ref, wide_ref, slice(None))
 
     def body(step):
         here = span(step, chunk)
-        every = wide_ref[here, :].astype(jnp.bfloat16)
-        every_ref[here, :] = every
-        blocks = [slice(at, at + TILE) for at in range(0, first_ref.shape[1], TILE)]
-        pre = [dot(every, first_ref[:, block], (1, 0)) for block in blocks]
+        blocks = blocks_of(first_ref.shape[1], TILE)
+        pre = [0.0] * len(blocks)
+        for half in halves:
+            if rows == chunk:
+                unpack(got_ref, wide_ref, half)
+            every = wide_ref[here, half].astype(jnp.bfloat16)
+            every_ref[here, half] = every
+            for at, block in enumerate(blocks):
+                pre[at] = pre[at] + dot(every, first_ref[half, block], (1, 0))
         part = 0.0
         for block, value in zip(blocks, pre):
             hidden = gelu_pair(value)[0].astype(jnp.bfloat16)
@@ -202,7 +214,7 @@
     tasks = tower_in_ref.shape[0]
     float32, bfloat16 = jnp.float32, jnp.bfloat16
 
-    features = [slice(at, at + TILE) for at in range(0, width, TILE)]
+    features = blocks_of(width, TILE)
     singles = [0.0] * tasks
     for block in features:
         for expert in range(experts):
@@ -304,8 +316,7 @@
     blocks = units // TILE
     copies = []
 
-    def gradient(left, right, buf, target, cuts):
-        at = 0
+    def gradient(left, right, buf, target, cuts, at=0):
         for cut in cuts:
             here = pl.ds(at * LANES, cut * LANES)
             buf[here, :] = dot(left[:, here], right(), (0, 0)).astype(jnp.bfloat16)
@@ -321,15 +332,22 @@
         dhidden = dot(arrived_ref[:, :width], second_ref[here, :], (1, 1))
         dpre_ref[:, here] = (gelu_pair(pre_ref[:, here])[1] * dhidden).astype(jnp.bfloat16)
 
-    unpack(got_ref, wide_ref)
-    arrived_ref[...] = wide_ref[...].astype(jnp.bfloat16)
-    pairs = units // LANES // 2 - 1
+    top = slice(0, TILE)
+    for block in blocks_of(width, TILE) + [slice(width, width + LANES)]:
+        unpack(got_ref, wide_ref, block)
+        arrived_ref[:, block] = wide_ref[:, block].astype(jnp.bfloat16)
+        if block.stop <= width:
+            second_buf[top, block] = dot(
+                hidden_ref[:, top], arrived_ref[:, block], (0, 0)
+            ).astype(jnp.bfloat16)
+    send(second_buf.at[top, :], grad_second_ref.at[top, :])
     gradient(
         hidden_ref,
         lambda: arrived_ref[:, :width],
         second_buf,
         grad_second_ref,
-        [1] + [2] * pairs + [1],
+        [2] * (units // TILE - 1),
+        TILE // LANES,
     )
     gate = dot(arrived_ref[:, width:], every_ref[...], (0, 0))
     for task in range(tasks):

time: 41.9 us -> 41.9 us (level)
  no operation moved by 1% of the time
where the time goes in v17:
time: 41.9 us; the launch traced here: 41.7 us
  blocking collectives  34.9 us (83%)
  Pallas kernels  5.27 us (13%)
  between operations  0.75 us (2%)
  local copies, waits for them, and re-layouts  0.73 us (2%)
    all_to_all x1, blocking collectives, per_device(): got = lax.all_to_all(ahead(spread(events, devices)), BOTH, 0, 0, tiled=True)  14.8 us
    all_to_all x1, blocking collectives, per_device(): got = lax.all_to_all(message, BOTH, 0, 0, tiled=True)  10.1 us
    all_to_all x1, blocking collectives, per_device(): parts = lax.all_to_all(part, BOTH, 0, 0, tiled=True)  10 us
    pallas_call x1, Pallas kernels, backward(): pl.pallas_call(functools.partial(backward_kernel, tasks), out_shape=[jax....  3.08 us
    pallas_call x1, Pallas kernels, middle(): pl.pallas_call(functools.partial(middle_kernel, dp), out_shape=pltpu.VMEM...  1.23 us
    pallas_call x1, Pallas kernels, forward(): pl.pallas_call(forward_kernel, out_shape=[pltpu.VMEM(got.shape, jnp.bfloa...  0.95 us

profile of v17, /device:TPU:0, one launch (start us, length us, event | category | flops | bytes accessed | tf_op | source)
XLA Modules:
  0.0 41.7 jit_solution(3335158708754451256)
XLA Ops:
  0.6 0.0 copy-start.4
  0.6 0.7 %copy-done.4 = bf16[2,1024]{1,0:T(2,128)(2,1)S(1)} copy-done((bf16[2,1024]{1,0:T(2,128)(2,1)S(1)}, bf16[2,1024]{1,0:T(2,128)(2,1)}, u32[]{:S(2)}) %copy-start.4) | copy-done | bytes 4120
  1.3 0.0 copy-start
  1.3 0.0 copy-start.1
  1.4 0.0 copy-start.3
  1.4 14.8 %all_to_all.15.got_ref = bf16[32,2,1024]{2,1,0:T(2,128)(2,1)S(1)} all-to-all(bf16[32,2,1024]{2,1,0:T(2,128)(2,1)S(1)} %ahead.1), channel_id=1, replica_groups=mesh['dp'=4,'expert'=8] {'dp','expert'}, dimensions={0} | all-to-all | bytes 262144 | tf_op jit(solution)/shard_map/all_to_all | solution.py:404
  16.2 0.0 copy-done
  16.2 0.0 copy-done.1
  16.2 0.0 copy-done.3
  16.2 0.0 copy-start.2
  16.2 0.0 copy-start.5
  16.3 0.0 copy-start.6
  16.3 0.0 copy-start.7
  16.3 0.0 copy-start.8
  16.3 1.0 %forward.1 = (bf16[32,2,1024]{2,1,0:T(2,128)(2,1)S(1)}, bf16[64,1024]{1,0:T(8,128)(2,1)S(1)}, f32[64,1024]{1,0:T(8,128)S(1)}, bf16[64,1024]{1,0:T(8,128)(2,1)S(1)}, f32[16,128]{1,0:T(8,128)S(1)}) custom-call(bf16[32,2,1024]{2,1,0:T(2,128)(2,1)S(1)} %all_to_all.15.got_ref, bf16[2,1024]{1,0:T(2,128)(2,1)S(1)} %copy-done.4, bf16[32,1024]{1,0:T(8,128)(2,1)S(1)} %bitcast.12, ...), custom_call_target="tpu_custom_call" | custom-call | flops 268435456 | bytes 4194304 | tf_op jit(solution)/shard_map/forward/pallas_call | solution.py:183
  17.3 10.0 %all_to_all.16.parts_ref = bf16[32,2,1024]{2,1,0:T(2,128)(2,1)S(1)} all-to-all(bf16[32,2,1024]{2,1,0:T(2,128)(2,1)S(1)} %get-tuple-element.11), channel_id=1, replica_groups=mesh['dp'=4,'expert'=8] {'dp','expert'}, dimensions={0} | all-to-all | bytes 262144 | tf_op jit(solution)/shard_map/all_to_all | solution.py:407
  27.3 0.0 copy-done.2
  27.3 0.0 copy-done.5
  27.3 0.0 copy-done.6
  27.3 0.0 copy-done.7
  27.3 0.0 copy-done.8
  27.3 1.2 %middle.1 = bf16[32,2,1152]{2,1,0:T(2,128)(2,1)S(1)} custom-call(bf16[32,2,1024]{2,1,0:T(2,128)(2,1)S(1)} %all_to_all.16.parts_ref, f32[16,128]{1,0:T(8,128)S(1)} %get-tuple-element.12.prob_ref, s32[2,4]{1,0:T(2,128)S(1)} %copy-done.7, bf16[4,1024,256]{2,1,0:T(8,128)(2,1)S(1)} %copy-done.2, f32[4,256]{1,0:T(4,128)S(1)} %copy-done.5, f32[4,256]{1,0:T(4,128)S(1)} %copy-done.6, ...), custom_call_target="tpu_custom_call" | custom-call | flops 33554432 | bytes 2097152 | tf_op jit(solution)/shard_map/middle/pallas_call | solution.py:285
  28.5 10.1 %all_to_all.17.got_ref = bf16[32,2,1152]{2,1,0:T(2,128)(2,1)S(1)} all-to-all(bf16[32,2,1152]{2,1,0:T(2,128)(2,1)S(1)} %middle.1), channel_id=1, replica_groups=mesh['dp'=4,'expert'=8] {'dp','expert'}, dimensions={0} | all-to-all | bytes 294912 | tf_op jit(solution)/shard_map/all_to_all | solution.py:412
  38.6 3.1 %backward.1 = (bf16[1024,1024]{1,0:T(8,128)(2,1)}, bf16[1024,1024]{1,0:T(8,128)(2,1)}, f32[4,1,1024]{2,1,0:T(1,128)}) custom-call(bf16[32,2,1152]{2,1,0:T(2,128)(2,1)S(1)} %all_to_all.17.got_ref, bf16[64,1024]{1,0:T(8,128)(2,1)S(1)} %get-tuple-element.13.every_ref, bf16[64,1024]{1,0:T(8,128)(2,1)S(1)} %get-tuple-element.14.hidden_ref, ...), custom_call_target="tpu_custom_call" | custom-call | flops 402653184 | bytes 6291456 | tf_op jit(solution)/shard_map/backward/pallas_call | solution.py:371
  (2 shorter events, 0.0 us)
Async XLA Ops:
  0.6 0.7 %copy-start.4 = (bf16[2,1024]{1,0:T(2,128)(2,1)S(1)}, bf16[2,1024]{1,0:T(2,128)(2,1)}, u32[]{:S(2)}) copy-start(bf16[2,1024]{1,0:T(2,128)(2,1)} %events_ref.1) | copy-start | bytes 12292
  1.3 14.9 %copy-start = (bf16[1,1024,1024]{2,1,0:T(8,128)(2,1)S(1)}, bf16[1,1024,1024]{2,1,0:T(8,128)(2,1)}, u32[]{:S(2)}) copy-start(bf16[1,1024,1024]{2,1,0:T(8,128)(2,1)} %param.12) | copy-start | bytes 6291460
  1.3 14.9 %copy-start.1 = (bf16[1,1024,1024]{2,1,0:T(8,128)(2,1)S(1)}, bf16[1,1024,1024]{2,1,0:T(8,128)(2,1)}, u32[]{:S(2)}) copy-start(bf16[1,1024,1024]{2,1,0:T(8,128)(2,1)} %param.11) | copy-start | bytes 6291460
  1.4 14.9 %copy-start.3 = (bf16[4,1024,8]{1,2,0:T(8,128)(2,1)S(1)}, bf16[4,1024,8]{1,2,0:T(8,128)(2,1)}, u32[]{:S(2)}) copy-start(bf16[4,1024,8]{1,2,0:T(8,128)(2,1)} %param.13) | copy-start | bytes 196612
  16.2 11.0 %copy-start.2 = (bf16[4,1024,256]{2,1,0:T(8,128)(2,1)S(1)}, bf16[4,1024,256]{2,1,0:T(8,128)(2,1)}, u32[]{:S(2)}) copy-start(bf16[4,1024,256]{2,1,0:T(8,128)(2,1)} %tower_in_ref.1) | copy-start | bytes 6291460
  16.2 11.0 %copy-start.5 = (f32[4,256]{1,0:T(4,128)S(1)}, f32[4,256]{1,0:T(4,128)}, u32[]{:S(2)}) copy-start(f32[4,256]{1,0:T(4,128)} %bias_ref.1) | copy-start | bytes 12292
  16.3 11.0 %copy-start.6 = (f32[4,256]{1,0:T(4,128)S(1)}, f32[4,256]{1,0:T(4,128)}, u32[]{:S(2)}) copy-start(f32[4,256]{1,0:T(4,128)} %weight_ref.1) | copy-start | bytes 12292
  16.3 11.0 %copy-start.7 = (s32[2,4]{1,0:T(2,128)S(1)}, s32[2,4]{1,0:T(2,128)}, u32[]{:S(2)}) copy-start(s32[2,4]{1,0:T(2,128)} %labels_ref.1) | copy-start | bytes 100
  16.3 11.0 %copy-start.8 = (f32[4]{0:T(128)S(1)}, f32[4]{0:T(128)}, u32[]{:S(2)}) copy-start(f32[4]{0:T(128)} %param.17) | copy-start | bytes 52

commit v18 on v17

--- a/solution.py
+++ b/solution.py
@@ -349,15 +349,21 @@
         [2] * (units // TILE - 1),
         TILE // LANES,
     )
+    steps(blocks, flat, dpre_step)
+    pairs = width // LANES // 2 - 1
+    gradient(every_ref, lambda: dpre_ref[...], first_buf, grad_first_ref, [2])
     gate = dot(arrived_ref[:, width:], every_ref[...], (0, 0))
     for task in range(tasks):
         lanes = [at * tasks + task for at in range(3)]
         gate_buf[task] = sum(gate[lane : lane + 1] for lane in lanes)
     send(gate_buf, grad_gate_ref)
-    steps(blocks, flat, dpre_step)
-    pairs = width // LANES // 2 - 1
     gradient(
-        every_ref, lambda: dpre_ref[...], first_buf, grad_first_ref, [2] * pairs + [1, 1]
+        every_ref,
+        lambda: dpre_ref[...],
+        first_buf,
+        grad_first_ref,
+        [2] * (pairs - 1) + [1, 1],
+        TILE // LANES,
     )
     for copy in copies:
         copy.wait()

time: 41.9 us -> 41.9 us (level)
  no operation moved by 1% of the time
where the time goes in v18:
time: 41.9 us; the launch traced here: 41.6 us
  blocking collectives  34.9 us (83%)
  Pallas kernels  5.2 us (12%)
  between operations  0.75 us (2%)
  local copies, waits for them, and re-layouts  0.73 us (2%)
    all_to_all x1, blocking collectives, per_device(): got = lax.all_to_all(ahead(spread(events, devices)), BOTH, 0, 0, tiled=True)  14.8 us
    all_to_all x1, blocking collectives, per_device(): got = lax.all_to_all(message, BOTH, 0, 0, tiled=True)  10.1 us
    all_to_all x1, blocking collectives, per_device(): parts = lax.all_to_all(part, BOTH, 0, 0, tiled=True)  10 us
    pallas_call x1, Pallas kernels, backward(): pl.pallas_call(functools.partial(backward_kernel, tasks), out_shape=[jax....  3.01 us
    pallas_call x1, Pallas kernels, middle(): pl.pallas_call(functools.partial(middle_kernel, dp), out_shape=pltpu.VMEM...  1.23 us
    pallas_call x1, Pallas kernels, forward(): pl.pallas_call(forward_kernel, out_shape=[pltpu.VMEM(got.shape, jnp.bfloa...  0.95 us

profile of v18, /device:TPU:0, one launch (start us, length us, event | category | flops | bytes accessed | tf_op | source)
XLA Modules:
  0.0 41.6 jit_solution(10361770507337375288)
XLA Ops:
  0.6 0.0 copy-start.4
  0.6 0.7 %copy-done.4 = bf16[2,1024]{1,0:T(2,128)(2,1)S(1)} copy-done((bf16[2,1024]{1,0:T(2,128)(2,1)S(1)}, bf16[2,1024]{1,0:T(2,128)(2,1)}, u32[]{:S(2)}) %copy-start.4) | copy-done | bytes 4120
  1.3 0.0 copy-start
  1.3 0.0 copy-start.1
  1.4 0.0 copy-start.3
  1.4 14.8 %all_to_all.15.got_ref = bf16[32,2,1024]{2,1,0:T(2,128)(2,1)S(1)} all-to-all(bf16[32,2,1024]{2,1,0:T(2,128)(2,1)S(1)} %ahead.1), channel_id=1, replica_groups=mesh['dp'=4,'expert'=8] {'dp','expert'}, dimensions={0} | all-to-all | bytes 262144 | tf_op jit(solution)/shard_map/all_to_all | solution.py:410
  16.2 0.0 copy-done
  16.2 0.0 copy-done.1
  16.2 0.0 copy-done.3
  16.2 0.0 copy-start.2
  16.2 0.0 copy-start.5
  16.3 0.0 copy-start.6
  16.3 0.0 copy-start.7
  16.3 0.0 copy-start.8
  16.3 1.0 %forward.1 = (bf16[32,2,1024]{2,1,0:T(2,128)(2,1)S(1)}, bf16[64,1024]{1,0:T(8,128)(2,1)S(1)}, f32[64,1024]{1,0:T(8,128)S(1)}, bf16[64,1024]{1,0:T(8,128)(2,1)S(1)}, f32[16,128]{1,0:T(8,128)S(1)}) custom-call(bf16[32,2,1024]{2,1,0:T(2,128)(2,1)S(1)} %all_to_all.15.got_ref, bf16[2,1024]{1,0:T(2,128)(2,1)S(1)} %copy-done.4, bf16[32,1024]{1,0:T(8,128)(2,1)S(1)} %bitcast.12, ...), custom_call_target="tpu_custom_call" | custom-call | flops 268435456 | bytes 4194304 | tf_op jit(solution)/shard_map/forward/pallas_call | solution.py:183
  17.3 10.0 %all_to_all.16.parts_ref = bf16[32,2,1024]{2,1,0:T(2,128)(2,1)S(1)} all-to-all(bf16[32,2,1024]{2,1,0:T(2,128)(2,1)S(1)} %get-tuple-element.11), channel_id=1, replica_groups=mesh['dp'=4,'expert'=8] {'dp','expert'}, dimensions={0} | all-to-all | bytes 262144 | tf_op jit(solution)/shard_map/all_to_all | solution.py:413
  27.3 0.0 copy-done.2
  27.3 0.0 copy-done.5
  27.3 0.0 copy-done.6
  27.3 0.0 copy-done.7
  27.3 0.0 copy-done.8
  27.3 1.2 %middle.1 = bf16[32,2,1152]{2,1,0:T(2,128)(2,1)S(1)} custom-call(bf16[32,2,1024]{2,1,0:T(2,128)(2,1)S(1)} %all_to_all.16.parts_ref, f32[16,128]{1,0:T(8,128)S(1)} %get-tuple-element.12.prob_ref, s32[2,4]{1,0:T(2,128)S(1)} %copy-done.7, bf16[4,1024,256]{2,1,0:T(8,128)(2,1)S(1)} %copy-done.2, f32[4,256]{1,0:T(4,128)S(1)} %copy-done.5, f32[4,256]{1,0:T(4,128)S(1)} %copy-done.6, ...), custom_call_target="tpu_custom_call" | custom-call | flops 33554432 | bytes 2097152 | tf_op jit(solution)/shard_map/middle/pallas_call | solution.py:285
  28.5 10.1 %all_to_all.17.got_ref = bf16[32,2,1152]{2,1,0:T(2,128)(2,1)S(1)} all-to-all(bf16[32,2,1152]{2,1,0:T(2,128)(2,1)S(1)} %middle.1), channel_id=1, replica_groups=mesh['dp'=4,'expert'=8] {'dp','expert'}, dimensions={0} | all-to-all | bytes 294912 | tf_op jit(solution)/shard_map/all_to_all | solution.py:418
  38.6 3.0 %backward.1 = (bf16[1024,1024]{1,0:T(8,128)(2,1)}, bf16[1024,1024]{1,0:T(8,128)(2,1)}, f32[4,1,1024]{2,1,0:T(1,128)}) custom-call(bf16[32,2,1152]{2,1,0:T(2,128)(2,1)S(1)} %all_to_all.17.got_ref, bf16[64,1024]{1,0:T(8,128)(2,1)S(1)} %get-tuple-element.13.every_ref, bf16[64,1024]{1,0:T(8,128)(2,1)S(1)} %get-tuple-element.14.hidden_ref, ...), custom_call_target="tpu_custom_call" | custom-call | flops 402653184 | bytes 6291456 | tf_op jit(solution)/shard_map/backward/pallas_call | solution.py:377
  (2 shorter events, 0.0 us)
Async XLA Ops:
  0.6 0.7 %copy-start.4 = (bf16[2,1024]{1,0:T(2,128)(2,1)S(1)}, bf16[2,1024]{1,0:T(2,128)(2,1)}, u32[]{:S(2)}) copy-start(bf16[2,1024]{1,0:T(2,128)(2,1)} %events_ref.1) | copy-start | bytes 12292
  1.3 14.9 %copy-start = (bf16[1,1024,1024]{2,1,0:T(8,128)(2,1)S(1)}, bf16[1,1024,1024]{2,1,0:T(8,128)(2,1)}, u32[]{:S(2)}) copy-start(bf16[1,1024,1024]{2,1,0:T(8,128)(2,1)} %param.12) | copy-start | bytes 6291460
  1.3 14.9 %copy-start.1 = (bf16[1,1024,1024]{2,1,0:T(8,128)(2,1)S(1)}, bf16[1,1024,1024]{2,1,0:T(8,128)(2,1)}, u32[]{:S(2)}) copy-start(bf16[1,1024,1024]{2,1,0:T(8,128)(2,1)} %param.11) | copy-start | bytes 6291460
  1.4 14.9 %copy-start.3 = (bf16[4,1024,8]{1,2,0:T(8,128)(2,1)S(1)}, bf16[4,1024,8]{1,2,0:T(8,128)(2,1)}, u32[]{:S(2)}) copy-start(bf16[4,1024,8]{1,2,0:T(8,128)(2,1)} %param.13) | copy-start | bytes 196612
  16.2 11.0 %copy-start.2 = (bf16[4,1024,256]{2,1,0:T(8,128)(2,1)S(1)}, bf16[4,1024,256]{2,1,0:T(8,128)(2,1)}, u32[]{:S(2)}) copy-start(bf16[4,1024,256]{2,1,0:T(8,128)(2,1)} %tower_in_ref.1) | copy-start | bytes 6291460
  16.2 11.0 %copy-start.5 = (f32[4,256]{1,0:T(4,128)S(1)}, f32[4,256]{1,0:T(4,128)}, u32[]{:S(2)}) copy-start(f32[4,256]{1,0:T(4,128)} %bias_ref.1) | copy-start | bytes 12292
  16.3 11.0 %copy-start.6 = (f32[4,256]{1,0:T(4,128)S(1)}, f32[4,256]{1,0:T(4,128)}, u32[]{:S(2)}) copy-start(f32[4,256]{1,0:T(4,128)} %weight_ref.1) | copy-start | bytes 12292
  16.3 11.0 %copy-start.7 = (s32[2,4]{1,0:T(2,128)S(1)}, s32[2,4]{1,0:T(2,128)}, u32[]{:S(2)}) copy-start(s32[2,4]{1,0:T(2,128)} %labels_ref.1) | copy-start | bytes 100
  16.3 11.0 %copy-start.8 = (f32[4]{0:T(128)S(1)}, f32[4]{0:T(128)}, u32[]{:S(2)}) copy-start(f32[4]{0:T(128)} %param.17) | copy-start | bytes 52
